TPU v7x, 32 devices: a whole 2x2x4 slice. The times are simulated.
32 devices in a mesh: rows: 8 (over z, x), cols: 4 (over y, core).
Axes of the slice: x: 2, y: 2, z: 4, core: 2. Of those that a mesh axis runs over, the one named last changes fastest.
Arguments:
- features: float32 [2, 8192, 128], P(None, 'rows', 'cols'), may hold values from -6 to 6
- neigh_first: int32 [2, 4096, 5], P(None, 'rows'), may hold values from 0 to 8191, as said below
- count_first: int32 [2, 4096], P(None, 'rows'), may hold values from 1 to 5
- neigh_mid: int32 [2, 2048, 10], P(None, 'rows'), may hold values from 0 to 4095, as said below
- count_mid: int32 [2, 2048], P(None, 'rows'), may hold values from 1 to 10
- neigh_last: int32 [2, 1024, 15], P(None, 'rows'), may hold values from 0 to 2047, as said below
- count_last: int32 [2, 1024], P(None, 'rows'), may hold values from 1 to 15
- labels: int32 [2, 1024], P(None, 'rows'), may hold values from 0 to 46
- w_first: float32 [2, 128, 256], P(None, 'cols'), may hold values from -0.375 to 0.375
- w_mid: float32 [2, 256, 256], P(None, 'cols'), may hold values from -0.25 to 0.25
- w_last: float32 [2, 256, 47], P(None, 'cols'), may hold values from -0.25 to 0.25
- b_hidden: float32 [2, 256], P(None, 'cols'), may hold values from -3 to 3
- b_last: float32 [47], replicated, may hold values from -3 to 3
- m_first: float32 [2, 128, 256], P(None, 'cols'), may hold values from -3.0517578e-05 to 3.0517578e-05
- m_mid: float32 [2, 256, 256], P(None, 'cols'), may hold values from -3.0517578e-05 to 3.0517578e-05
- m_last: float32 [2, 256, 47], P(None, 'cols'), may hold values from -3.0517578e-05 to 3.0517578e-05
- m_hidden: float32 [2, 256], P(None, 'cols'), may hold values from -3.0517578e-05 to 3.0517578e-05
- m_bias: float32 [47], replicated, may hold values from -3.0517578e-05 to 3.0517578e-05
- v_first: float32 [2, 128, 256], P(None, 'cols'), may hold values from 4.5201622e-13 to 1.8080649e-12
- v_mid: float32 [2, 256, 256], P(None, 'cols'), may hold values from 4.5201622e-13 to 1.8080649e-12
- v_last: float32 [2, 256, 47], P(None, 'cols'), may hold values from 4.5201622e-13 to 1.8080649e-12
- v_hidden: float32 [2, 256], P(None, 'cols'), may hold values from 4.5201622e-13 to 1.8080649e-12
- v_bias: float32 [47], replicated, may hold values from 4.5201622e-13 to 1.8080649e-12
Outputs:
- new_first: float32 [2, 128, 256], P(None, 'cols')
- new_mid: float32 [2, 256, 256], P(None, 'cols')
- new_last: float32 [2, 256, 47], P(None, 'cols')
- new_hidden: float32 [2, 256], P(None, 'cols')
- new_bias: float32 [47], replicated
- moment_first: float32 [2, 128, 256], P(None, 'cols')
- moment_mid: float32 [2, 256, 256], P(None, 'cols')
- moment_last: float32 [2, 256, 47], P(None, 'cols')
- moment_hidden: float32 [2, 256], P(None, 'cols')
- moment_bias: float32 [47], replicated
- square_first: float32 [2, 128, 256], P(None, 'cols')
- square_mid: float32 [2, 256, 256], P(None, 'cols')
- square_last: float32 [2, 256, 47], P(None, 'cols')
- square_hidden: float32 [2, 256], P(None, 'cols')
- square_bias: float32 [47], replicated
- loss_sum: float32 [], replicated
- weight_sum: float32 [], replicated
- grad_norm: float32 [], replicated
Inputs may be any that keep to these rules, and one draw needn't show every extreme that they name: `neigh_first`: neighbor ids index the third-hop frontier of all devices, device by device in blocks of 1024; slots past a node's count are ignored; among the 2560 slots of one device's rows in a micro-batch, no device's block is named more than ceil(320) times, and some device's block exactly that often. `neigh_mid`: neighbor ids index the second-hop frontier of all devices, device by device in blocks of 512; slots past a node's count are ignored; among the 2560 slots of one device's rows in a micro-batch, no device's block is named more than ceil(320) times, and some device's block exactly that often. `neigh_last`: neighbor ids index the first-hop frontier of all devices, device by device in blocks of 256; slots past a seed's count are ignored; among the 1920 slots of one device's seeds in a micro-batch, no device's block is named more than ceil(240) times, and some device's block exactly that often.
All inputs are finite; a program needn't handle non-finite values.
Results may differ from a plain program's by a relative error of at most 0.0003.
Values sent between devices are 32-bit elements; how exact they have to be, the bound alone decides.
No kernel may reach another device: no remote copies, remote signals or barrier semaphores. Data moves between devices by JAX's collectives and lax.ppermute only.
A program may use at most 128 MiB of HBM per device.

v0:
```python
import jax
import jax.numpy as jnp
from jax import lax
from jax.sharding import PartitionSpec as P

STEP = 5


HIGH = lax.Precision.HIGHEST


def product(left, right):
    return jnp.dot(left, right, precision=HIGH, preferred_element_type=jnp.float32)


def inner_rows(left, right):
    return lax.dot_general(
        left, right, (((0,), (0,)), ((), ())), precision=HIGH, preferred_element_type=jnp.float32
    )


def outer_cols(left, right):
    return lax.dot_general(
        left, right, (((1,), (1,)), ((), ())), precision=HIGH, preferred_element_type=jnp.float32
    )


def slot_mask(neigh, count):
    slots = jnp.arange(neigh.shape[1], dtype=jnp.int32)
    return (slots[None, :] < count[:, None]).astype(jnp.float32)[:, :, None]


def neighbor_mean(hidden, neigh, count):
    mask = slot_mask(neigh, count)
    whole = lax.all_gather(hidden, "rows", axis=0, tiled=True)
    total = jnp.sum(jnp.take(whole, neigh, axis=0) * mask, axis=1)
    return total / count[:, None].astype(jnp.float32)


def neighbor_back(grad_mean, neigh, count, before):
    mask = slot_mask(neigh, count)
    spread = (grad_mean / count[:, None].astype(jnp.float32))[:, None, :] * mask
    whole = (
        jnp.zeros((before * lax.axis_size("rows"), grad_mean.shape[1]), jnp.float32)
        .at[neigh]
        .add(spread)
    )
    return lax.psum_scatter(whole, "rows", scatter_dimension=0, tiled=True)


def layer_forward(hidden, neigh, count, weight, bias, final):
    mean = neighbor_mean(hidden, neigh, count)
    own = hidden[: neigh.shape[0]]
    partial_out = product(own, weight[0]) + product(mean, weight[1])
    if final:
        pre = lax.psum(partial_out, "cols") + bias
    else:
        pre = lax.psum_scatter(partial_out, "cols", scatter_dimension=1, tiled=True) + bias
    return (pre, (own, mean))


def layer_backward(grad_pre, kept, weight, final, neigh, count, before, needed):
    own, mean = kept
    if final:
        grad_full = grad_pre
    else:
        grad_full = lax.all_gather(grad_pre, "cols", axis=1, tiled=True)
    grad_weight = jnp.stack([inner_rows(own, grad_full), inner_rows(mean, grad_full)])
    grad_bias = jnp.sum(grad_pre, axis=0)
    if not needed:
        return (grad_weight, grad_bias, None)
    grad_own = outer_cols(grad_full, weight[0])
    grad_mean = outer_cols(grad_full, weight[1])
    grad_hidden = neighbor_back(grad_mean, neigh, count, before)
    grad_hidden = grad_hidden + jnp.pad(grad_own, ((0, before - grad_own.shape[0]), (0, 0)))
    return (grad_weight, grad_bias, grad_hidden)


def silu_slope(pre):
    sigma = jax.nn.sigmoid(pre)
    return sigma * (1.0 + pre * (1.0 - sigma))


def adamw(weight, grad, first, second):
    moment = 0.9 * first + 0.1 * grad
    square = 0.999 * second + 0.001 * grad * grad
    corrected = moment / (1.0 - 0.9**STEP)
    root = jnp.sqrt(square / (1.0 - 0.999**STEP))
    return (weight - 0.05 * (corrected / (root + 1e-08) + 0.01 * weight), moment, square)


def on_device(
    features,
    neigh_first,
    count_first,
    neigh_mid,
    count_mid,
    neigh_last,
    count_last,
    labels,
    w_first,
    w_mid,
    w_last,
    b_hidden,
    b_last,
    m_first,
    m_mid,
    m_last,
    m_hidden,
    m_bias,
    v_first,
    v_mid,
    v_last,
    v_hidden,
    v_bias,
):
    classes = jnp.arange(w_last.shape[2], dtype=jnp.int32)
    onehot_all = (labels[:, :, None] == classes).astype(jnp.float32)
    counts = lax.psum(jnp.sum(onehot_all, axis=(0, 1)), "rows")
    cweight = 1.0 / jnp.maximum(counts, 1.0)
    weight_sum = jnp.sum(counts * cweight)
    totals = None
    for batch in range(features.shape[0]):
        inputs = features[batch]
        pre_one, kept_one = layer_forward(
            inputs, neigh_first[batch], count_first[batch], w_first, b_hidden[0], False
        )
        hidden_one = jax.nn.silu(pre_one)
        pre_two, kept_two = layer_forward(
            hidden_one, neigh_mid[batch], count_mid[batch], w_mid, b_hidden[1], False
        )
        hidden_two = jax.nn.silu(pre_two)
        logits, kept_three = layer_forward(
            hidden_two, neigh_last[batch], count_last[batch], w_last, b_last, True
        )
        onehot = onehot_all[batch]
        lse = jax.nn.logsumexp(logits, axis=1)
        target = jnp.sum(logits * onehot, axis=1)
        weight_seed = jnp.dot(onehot, cweight, precision=HIGH)
        loss_local = jnp.sum(weight_seed * (lse - target))
        grad_logits = weight_seed[:, None] * (jax.nn.softmax(logits, axis=1) - onehot) / weight_sum
        grad_last, grad_bl, grad_two = layer_backward(
            grad_logits,
            kept_three,
            w_last,
            True,
            neigh_last[batch],
            count_last[batch],
            hidden_two.shape[0],
            True,
        )
        grad_mid, grad_b2, grad_one = layer_backward(
            grad_two * silu_slope(pre_two),
            kept_two,
            w_mid,
            False,
            neigh_mid[batch],
            count_mid[batch],
            hidden_one.shape[0],
            True,
        )
        grad_first, grad_b1, unused = layer_backward(
            grad_one * silu_slope(pre_one),
            kept_one,
            w_first,
            False,
            neigh_first[batch],
            count_first[batch],
            inputs.shape[0],
            False,
        )
        local = (
            grad_first,
            grad_mid,
            grad_last,
            jnp.stack([grad_b1, grad_b2]),
            grad_bl,
            loss_local,
        )
        local = lax.psum((local[0], local[1], local[2], local[3], local[4], local[5]), "rows")
        totals = local if totals is None else jax.tree.map(jnp.add, totals, local)
    grads = totals[:5]
    loss_sum = totals[5]
    squares = sum((jnp.sum(g * g) for g in grads[:4])) + jnp.sum(
        grads[4] * grads[4]
    ) / lax.axis_size("cols")
    grad_norm = jnp.sqrt(lax.psum(squares, "cols"))
    scale = jnp.minimum(1.0, 0.01 / grad_norm)
    params = (w_first, w_mid, w_last, b_hidden, b_last)
    firsts = (m_first, m_mid, m_last, m_hidden, m_bias)
    seconds = (v_first, v_mid, v_last, v_hidden, v_bias)
    results = [adamw(w, g * scale, m, v) for w, g, m, v in zip(params, grads, firsts, seconds)]
    news = tuple((r[0] for r in results))
    moments = tuple((r[1] for r in results))
    squares_out = tuple((r[2] for r in results))
    return news + moments + squares_out + (loss_sum, weight_sum, grad_norm)


def solution(mesh):
    placed = (
        P(None, "rows", "cols"),
        P(None, "rows", None),
        P(None, "rows"),
        P(None, "rows", None),
        P(None, "rows"),
        P(None, "rows", None),
        P(None, "rows"),
        P(None, "rows"),
        P(None, "cols", None),
        P(None, "cols", None),
        P(None, "cols", None),
        P(None, "cols"),
        P(),
        P(None, "cols", None),
        P(None, "cols", None),
        P(None, "cols", None),
        P(None, "cols"),
        P(),
        P(None, "cols", None),
        P(None, "cols", None),
        P(None, "cols", None),
        P(None, "cols"),
        P(),
    )
    return jax.shard_map(
        on_device,
        mesh=mesh,
        in_specs=placed,
        out_specs=(
            P(None, "cols", None),
            P(None, "cols", None),
            P(None, "cols", None),
            P(None, "cols"),
            P(),
            P(None, "cols", None),
            P(None, "cols", None),
            P(None, "cols", None),
            P(None, "cols"),
            P(),
            P(None, "cols", None),
            P(None, "cols", None),
            P(None, "cols", None),
            P(None, "cols"),
            P(),
            P(),
            P(),
            P(),
        ),
        check_vma=False,
    )
```

profile of v0, /device:TPU:0, one launch (start us, length us, event | category | flops | bytes accessed | tf_op | source)
XLA Modules:
  0.0 881.3 jit_solution(9505681678657257467)
XLA Ops:
  16.0 70.3 %all-gather.11.cloned.1.call-done = f32[1,8192,32]{2,1,0:T(8,128)} async-done(((f32[1,1024,32]{2,1,0:T(8,128)}), f32[1,8192,32]{2,1,0:T(8,128)}) %all-gather.11.cloned.1.call-update) | async-done | bytes 1048592 | tf_op jit(solution)/shard_map/all_gather | solution.py:35
  86.3 6.3 gather_fusion
  92.9 3.9 fusion.3
  102.2 57.9 %all-gather.13.cloned.1.call-done = f32[1,8192,32]{2,1,0:T(8,128)} async-done(((f32[1,1024,32]{2,1,0:T(8,128)}), f32[1,8192,32]{2,1,0:T(8,128)}) %all-gather.13.cloned.1.call-update) | async-done | bytes 1048592 | tf_op jit(solution)/shard_map/all_gather | solution.py:35
  160.1 6.3 gather_fusion.3
  174.5 8.1 reduce-scatter.9.cloned.1.call-done
  182.6 24.2 %reduce-scatter.17.cloned.1.call-done = f32[512,64]{0,1:T(8,128)} async-done(((f32[512,256]{0,1:T(8,128)}), f32[512,64]{0,1:T(8,128)}) %reduce-scatter.17.cloned.1.call-update) | async-done | bytes 131088 | tf_op jit(solution)/shard_map/reduce_scatter | solution.py:58
  216.0 21.7 %psum.112 = f32[47]{0:T(128)S(1)} all-reduce(f32[47]{0:T(128)S(1)} %convert_reduce_fusion), channel_id=1, replica_groups=mesh['rows'=8,'cols'=4] {'rows'}, use_global_device_ids=true, to_apply=%region_1.0 | all-reduce | flops 47 | bytes 376 | tf_op jit(solution)/shard_map/psum | solution.py:119
  243.5 6.0 all-gather.7.cloned.1.call-done
  251.4 4.8 gather_fusion.1
  261.6 29.5 %all-gather.9.cloned.1.call-done = f32[4096,64]{0,1:T(8,128)} async-done(((f32[512,64]{0,1:T(8,128)}), f32[4096,64]{0,1:T(8,128)}) %all-gather.9.cloned.1.call-update) | async-done | bytes 1048592 | tf_op jit(solution)/shard_map/all_gather | solution.py:35
  293.0 4.1 gather_fusion.4
  302.5 9.9 %reduce-scatter.11.cloned.1.call-done = f32[256,64]{0,1:T(8,128)} async-done(((f32[256,256]{0,1:T(8,128)}), f32[256,64]{0,1:T(8,128)}) %reduce-scatter.11.cloned.1.call-update) | async-done | bytes 65552 | tf_op jit(solution)/shard_map/reduce_scatter | solution.py:58
  312.4 22.7 %reduce-scatter.19.cloned.1.call-done = f32[256,64]{0,1:T(8,128)} async-done(((f32[256,256]{0,1:T(8,128)}), f32[256,64]{0,1:T(8,128)}) %reduce-scatter.19.cloned.1.call-update) | async-done | bytes 65552 | tf_op jit(solution)/shard_map/reduce_scatter | solution.py:58
  336.1 31.4 %all_gather.37 = f32[2048,64]{0,1:T(8,128)S(1)} all-gather(f32[256,64]{0,1:T(8,128)S(1)} %get-tuple-element.148), channel_id=1, replica_groups=mesh['rows'=8,'cols'=4] {'rows'}, dimensions={0}, use_global_device_ids=true | all-gather | bytes 589824 | tf_op jit(solution)/shard_map/all_gather | solution.py:35
  368.2 31.3 %all_gather.32 = f32[2048,64]{0,1:T(8,128)S(1)} all-gather(f32[256,64]{0,1:T(8,128)S(1)} %get-tuple-element.149), channel_id=1, replica_groups=mesh['rows'=8,'cols'=4] {'rows'}, dimensions={0}, use_global_device_ids=true | all-gather | bytes 589824 | tf_op jit(solution)/shard_map/all_gather | solution.py:35
  411.1 10.8 %all-reduce.6 = (f32[128,47]{0,1:T(8,128)S(1)}, f32[128,47]{0,1:T(8,128)S(1)}) all-reduce(f32[128,47]{0,1:T(8,128)S(1)} %convolution_add_fusion.5, f32[128,47]{0,1:T(8,128)S(1)} %convolution_add_fusion.4), channel_id=1, replica_groups=mesh['rows'=8,'cols'=4] {'cols'}, use_global_device_ids=true, to_apply=%region_7.11 | all-reduce | flops 12032 | bytes 96256 | tf_op jit(solution)/shard_map/psum | solution.py:56
  425.7 12.1 %scatter_custom_fusion = f32[2048,64]{1,0:T(8,128)S(1)} fusion(s32[1920]{0:T(1024)} %reshape.427, f32[1920,64]{1,0:T(8,128)S(1)} %reshape.429, f32[]{:T(128)} %constant.41.clone.1), kind=kCustom, calls=%fused_computation.56 | custom fusion | flops 122880 | bytes 524800 | tf_op jit(solution)/shard_map/scatter-add | solution.py:46
  440.2 12.0 %scatter_custom_fusion.2 = f32[2048,64]{1,0:T(8,128)S(1)} fusion(s32[1920]{0:T(1024)S(1)} %reshape.443, f32[1920,64]{1,0:T(8,128)S(1)} %reshape.445, f32[]{:T(128)} %constant.41.clone.1), kind=kCustom, calls=%fused_computation.54 | custom fusion | flops 122880 | bytes 524292 | tf_op jit(solution)/shard_map/scatter-add | solution.py:46
  454.2 47.4 %reduce-scatter.13.cloned.1.call-done = f32[256,64]{0,1:T(8,128)} async-done(((f32[2048,64]{0,1:T(8,128)}), f32[256,64]{0,1:T(8,128)}) %reduce-scatter.13.cloned.1.call-update) | async-done | bytes 65552 | tf_op jit(solution)/shard_map/reduce_scatter | solution.py:48
  501.6 65.0 %reduce-scatter.21.cloned.1.call-done = f32[256,64]{0,1:T(8,128)} async-done(((f32[2048,64]{0,1:T(8,128)}), f32[256,64]{0,1:T(8,128)}) %reduce-scatter.21.cloned.1.call-update) | async-done | bytes 65552 | tf_op jit(solution)/shard_map/reduce_scatter | solution.py:48
  568.3 15.3 %all_gather.33 = f32[256,256]{0,1:T(8,128)S(1)} all-gather(f32[256,64]{0,1:T(8,128)S(1)} %get-tuple-element.147), channel_id=1, replica_groups=mesh['rows'=8,'cols'=4] {'cols'}, dimensions={1}, use_global_device_ids=true | all-gather | bytes 327680 | tf_op jit(solution)/shard_map/all_gather | solution.py:67
  585.8 15.0 %scatter_custom_fusion.1 = f32[4096,64]{1,0:T(8,128)S(1)} fusion(s32[2560]{0:T(1024)S(1)} %reshape.435, f32[2560,64]{1,0:T(8,128)} %reshape.437, f32[]{:T(128)} %constant.41.clone.1), kind=kCustom, calls=%fused_computation.50 | custom fusion | flops 163840 | bytes 1049088 | tf_op jit(solution)/shard_map/scatter-add | solution.py:46
  602.8 5.9 all_gather.38
  610.9 15.0 %scatter_custom_fusion.3 = f32[4096,64]{1,0:T(8,128)S(1)} fusion(s32[2560]{0:T(1024)S(1)} %reshape.451, f32[2560,64]{1,0:T(8,128)} %reshape.453, f32[]{:T(128)} %constant.41.clone.1), kind=kCustom, calls=%fused_computation.48 | custom fusion | flops 163840 | bytes 1049088 | tf_op jit(solution)/shard_map/scatter-add | solution.py:46
  634.2 31.4 %reduce-scatter.15.cloned.1.call-done = f32[512,64]{0,1:T(8,128)} async-done(((f32[4096,64]{0,1:T(8,128)}), f32[512,64]{0,1:T(8,128)}) %reduce-scatter.15.cloned.1.call-update) | async-done | bytes 131088 | tf_op jit(solution)/shard_map/reduce_scatter | solution.py:48
  665.6 66.5 %reduce-scatter.23.cloned.1.call-done = f32[512,64]{0,1:T(8,128)} async-done(((f32[4096,64]{0,1:T(8,128)}), f32[512,64]{0,1:T(8,128)}) %reduce-scatter.23.cloned.1.call-update) | async-done | bytes 131088 | tf_op jit(solution)/shard_map/reduce_scatter | solution.py:48
  733.3 7.2 all_gather.39
  742.0 7.4 all_gather.34
  750.8 35.6 %all-reduce.4 = (f32[2,64,47]{1,2,0:T(8,128)S(1)}, f32[2,64]{1,0:T(2,128)S(1)}, f32[47]{0:T(128)S(1)}, f32[]{:T(128)}) all-reduce(f32[2,64,47]{1,2,0:T(8,128)S(1)} %maximum_add_fusion.2, f32[2,64]{1,0:T(2,128)S(1)} %maximum_add_fusion.3, f32[47]{0:T(128)S(1)} %add.379, f32[]{:T(128)S(6)} %add.408), channel_id=1, replica_groups=mesh['rows'=8,'cols'=4] {'rows'}, use_global_device_ids=true, to_apply=%region_33.37 | all-reduce | flops 6192 | bytes 49536 | tf_op jit(solution)/shard_map/psum | solution.py:180
  789.5 65.1 %all-reduce.9.cloned.1.call-done = (f32[2,32,256]{2,1,0:T(8,128)}, f32[2,64,256]{2,1,0:T(8,128)}) async-done(((f32[2,32,256]{2,1,0:T(8,128)}, f32[2,64,256]{2,1,0:T(8,128)}), (f32[2,32,256]{2,1,0:T(8,128)}, f32[2,64,256]{2,1,0:T(8,128)})) %all-reduce.9.cloned.1.call-update) | async-done | bytes 196624 | tf_op jit(solution)/shard_map/psum | solution.py:180
  860.1 6.2 psum.125
  (372 shorter events, 102.7 us)
Async XLA Ops:
  7.2 79.1 %all-gather.11.cloned.1.call-start = ((), (), s32[]{:S(2)}) async-start(), calls=%async_computation.18 | async-start | bytes 4718592 | tf_op jit(solution)/shard_map/all_gather | solution.py:35
  9.3 150.8 %all-gather.13.cloned.1.call-start = ((), (), s32[]{:S(2)}) async-start(), calls=%async_computation.19 | async-start | bytes 4718592 | tf_op jit(solution)/shard_map/all_gather | solution.py:35
  10.4 172.1 %reduce-scatter.9.cloned.1.call-start = ((), (), s32[]{:S(2)}) async-start(), calls=%async_computation.8 | async-start | bytes 655360 | tf_op jit(solution)/shard_map/reduce_scatter | solution.py:58
  12.9 158.3 %copy-start.64 = (f32[512]{0:T(512)}, f32[512]{0:T(512)S(1)}, u32[]{:S(2)}) copy-start(f32[512]{0:T(512)S(1)} %convert_element_type.115) | copy-start | bytes 6148
  99.0 107.7 %reduce-scatter.17.cloned.1.call-start = ((), (), s32[]{:S(2)}) async-start(), calls=%async_computation.13 | async-start | bytes 655360 | tf_op jit(solution)/shard_map/reduce_scatter | solution.py:58
  173.6 76.0 %all-gather.7.cloned.1.call-start = ((), (), s32[]{:S(2)}) async-start(), calls=%async_computation.9 | async-start | bytes 1179648 | tf_op jit(solution)/shard_map/all_gather | solution.py:35
  208.6 82.5 %all-gather.9.cloned.1.call-start = ((), (), s32[]{:S(2)}) async-start(), calls=%async_computation.14 | async-start | bytes 1179648 | tf_op jit(solution)/shard_map/all_gather | solution.py:35
  237.7 74.7 %reduce-scatter.11.cloned.1.call-start = ((), (), s32[]{:S(2)}) async-start(), calls=%async_computation.10 | async-start | bytes 327680 | tf_op jit(solution)/shard_map/reduce_scatter | solution.py:58
  260.4 74.6 %reduce-scatter.19.cloned.1.call-start = ((), (), s32[]{:S(2)}) async-start(), calls=%async_computation.15 | async-start | bytes 327680 | tf_op jit(solution)/shard_map/reduce_scatter | solution.py:58
  301.4 200.2 %reduce-scatter.13.cloned.1.call-start = ((), (), s32[]{:S(2)}) async-start(), calls=%async_computation.11 | async-start | bytes 589824 | tf_op jit(solution)/shard_map/reduce_scatter | solution.py:48
  439.0 127.6 %reduce-scatter.21.cloned.1.call-start = ((), (), s32[]{:S(2)}) async-start(), calls=%async_computation.16 | async-start | bytes 589824 | tf_op jit(solution)/shard_map/reduce_scatter | solution.py:48
  440.2 126.4 %copy-start.26 = (f32[256,64]{0,1:T(8,128)S(1)}, f32[256,64]{0,1:T(8,128)}, u32[]{:S(2)}) copy-start(f32[256,64]{0,1:T(8,128)} %reduce-scatter.11.cloned.1.call-done) | copy-start | bytes 196612
  440.2 126.4 %copy-start.27 = (f32[256,64]{0,1:T(8,128)S(1)}, f32[256,64]{0,1:T(8,128)}, u32[]{:S(2)}) copy-start(f32[256,64]{0,1:T(8,128)} %reduce-scatter.19.cloned.1.call-done) | copy-start | bytes 196612
  440.2 143.4 %copy-start.55 = (f32[256]{0:T(256)S(1)}, f32[256]{0:T(256)}, u32[]{:S(2)}) copy-start(f32[256]{0:T(256)} %copy-done.54) | copy-start | bytes 3076
  452.2 131.8 %copy-start.4 = (f32[256,10]{1,0:T(8,128)S(1)}, f32[256,10]{1,0:T(8,128)}, u32[]{:S(2)}) copy-start(f32[256,10]{1,0:T(8,128)} %fusion.19) | copy-start | bytes 30724
  453.4 212.2 %reduce-scatter.15.cloned.1.call-start = ((), (), s32[]{:S(2)}) async-start(), calls=%async_computation.12 | async-start | bytes 1179648 | tf_op jit(solution)/shard_map/reduce_scatter | solution.py:48
  602.5 129.5 %reduce-scatter.23.cloned.1.call-start = ((), (), s32[]{:S(2)}) async-start(), calls=%async_computation.17 | async-start | bytes 1179648 | tf_op jit(solution)/shard_map/reduce_scatter | solution.py:48
  627.6 226.9 %all-reduce.9.cloned.1.call-start = ((), (), s32[]{:S(2)}) async-start(), calls=%async_computation.20 | async-start | bytes 393216 | tf_op jit(solution)/shard_map/psum | solution.py:180
  740.5 126.5 %copy-start.34 = (f32[2,64,47]{1,0,2:T(2,128)S(1)}, f32[2,64,47]{1,0,2:T(2,128)}, u32[]{:S(2)}) copy-start(f32[2,64,47]{1,0,2:T(2,128)} %param.39) | copy-start | bytes 72196
  740.5 126.5 %copy-start.44 = (f32[2,64,47]{1,0,2:T(2,128)S(1)}, f32[2,64,47]{1,0,2:T(2,128)}, u32[]{:S(2)}) copy-start(f32[2,64,47]{1,0,2:T(2,128)} %param.44) | copy-start | bytes 72196
  740.5 126.5 %copy-start.45 = (f32[2,64,47]{1,0,2:T(2,128)S(1)}, f32[2,64,47]{1,0,2:T(2,128)}, u32[]{:S(2)}) copy-start(f32[2,64,47]{1,0,2:T(2,128)} %param.49) | copy-start | bytes 72196
  741.3 127.8 %copy-start.61 = (f32[47]{0:T(128)S(1)}, f32[47]{0:T(128)}, u32[]{:S(2)}) copy-start(f32[47]{0:T(128)} %param.41) | copy-start | bytes 568
  741.3 127.8 %copy-start.87 = (f32[47]{0:T(128)S(1)}, f32[47]{0:T(128)}, u32[]{:S(2)}) copy-start(f32[47]{0:T(128)} %param.46) | copy-start | bytes 568
  741.3 127.8 %copy-start.88 = (f32[47]{0:T(128)S(1)}, f32[47]{0:T(128)}, u32[]{:S(2)}) copy-start(f32[47]{0:T(128)} %param.51) | copy-start | bytes 568
  741.3 128.3 %copy-start.71 = (f32[2,64]{1,0:T(2,128)S(1)}, f32[2,64]{1,0:T(2,128)}, u32[]{:S(2)}) copy-start(f32[2,64]{1,0:T(2,128)} %param.40) | copy-start | bytes 1540
  741.3 128.3 %copy-start.81 = (f32[2,64]{1,0:T(2,128)S(1)}, f32[2,64]{1,0:T(2,128)}, u32[]{:S(2)}) copy-start(f32[2,64]{1,0:T(2,128)} %param.45) | copy-start | bytes 1540
  741.3 128.3 %copy-start.82 = (f32[2,64]{1,0:T(2,128)S(1)}, f32[2,64]{1,0:T(2,128)}, u32[]{:S(2)}) copy-start(f32[2,64]{1,0:T(2,128)} %param.50) | copy-start | bytes 1540
  741.3 128.9 %copy-start.39 = (f32[2,64,256]{2,1,0:T(8,128)S(1)}, f32[2,64,256]{2,1,0:T(8,128)}, u32[]{:S(2)}) copy-start(f32[2,64,256]{2,1,0:T(8,128)} %param.43) | copy-start | bytes 393220
  741.4 128.9 %copy-start.40 = (f32[2,64,256]{2,1,0:T(8,128)S(1)}, f32[2,64,256]{2,1,0:T(8,128)}, u32[]{:S(2)}) copy-start(f32[2,64,256]{2,1,0:T(8,128)} %param.48) | copy-start | bytes 393220
  741.9 130.0 %copy-start.20 = (f32[2,32,256]{2,1,0:T(8,128)S(1)}, f32[2,32,256]{2,1,0:T(8,128)}, u32[]{:S(2)}) copy-start(f32[2,32,256]{2,1,0:T(8,128)} %param.37) | copy-start | bytes 196612
  741.9 130.0 %copy-start.42 = (f32[2,32,256]{2,1,0:T(8,128)S(1)}, f32[2,32,256]{2,1,0:T(8,128)}, u32[]{:S(2)}) copy-start(f32[2,32,256]{2,1,0:T(8,128)} %param.42) | copy-start | bytes 196612
  742.0 130.0 %copy-start.43 = (f32[2,32,256]{2,1,0:T(8,128)S(1)}, f32[2,32,256]{2,1,0:T(8,128)}, u32[]{:S(2)}) copy-start(f32[2,32,256]{2,1,0:T(8,128)} %param.47) | copy-start | bytes 196612
  (72 other events, 2170.2 us)
Sparse Core Ops, SparseCore 0:
  10.2 76.0 all-gather.10
  88.4 71.6 all-gather.12
  162.6 19.9 reduce-scatter.8
  185.1 21.6 reduce-scatter.16
  209.4 40.1 all-gather.6
  252.2 38.9 all-gather.8
  293.6 18.7 reduce-scatter.10
  315.0 20.0 reduce-scatter.18
  439.1 62.4 reduce-scatter.12
  505.2 61.4 reduce-scatter.20
  602.6 62.9 reduce-scatter.14
  669.2 62.7 reduce-scatter.22
  787.7 66.7 all-reduce.8
where the time goes:
time: 887 us; the launch traced here: 881 us
  waiting for transfers between devices  504 us (57%)
  blocking collectives  173 us (20%)
  other arithmetic  97.3 us (11%)
  local copies, waits for them, and re-layouts  59.7 us (7%)
  matrix products  24.5 us (3%)
  between operations  22.3 us (3%)
    reduce_scatter x4, waiting for transfers between devices, neighbor_back(): return lax.psum_scatter(whole, 'rows', scatter_dimension=0, tiled=True)  210 us
    all_gather x4, waiting for transfers between devices, neighbor_mean(): whole = lax.all_gather(hidden, 'rows', axis=0, tiled=True)  164 us
    psum x1, waiting for transfers between devices, on_device(): lax.psum((local[0], local[1], local[2], local[3], local[4], local[5]), 'r...  65.1 us
    reduce_scatter x4, waiting for transfers between devices, layer_forward(): lax.psum_scatter(partial_out, 'cols', scatter_dimension=1, tiled=True)  64.9 us
    all_gather x2, blocking collectives, neighbor_mean(): whole = lax.all_gather(hidden, 'rows', axis=0, tiled=True)  62.6 us
    scatter-add x4, other arithmetic, neighbor_back(): whole = jnp.zeros((before * lax.axis_size('rows'), grad_mean.shape[1]), j...  54.2 us
    all_gather x4, blocking collectives, layer_backward(): grad_full = lax.all_gather(grad_pre, 'cols', axis=1, tiled=True)  35.8 us
    psum x1, blocking collectives, on_device(): lax.psum((local[0], local[1], local[2], local[3], local[4], local[5]), 'r...  35.6 us
  transfers between devices with their start and end apart: 13, of which 13 were waited for; matrix products, arithmetic and copies ran while one was open for 13% of the time, Pallas kernels for 0%

commit v1 on v0

v1 whole, which is shorter than its diff:
```python
import functools

import jax
import jax.numpy as jnp
from jax import lax
from jax.experimental import pallas as pl
from jax.experimental.pallas import tpu as pltpu
from jax.sharding import Mesh
from jax.sharding import PartitionSpec as P

STEP = 5
F32 = jnp.float32
BF16 = jnp.bfloat16
I32 = jnp.int32
LANES = 128
CLASS_ROWS = 48
LAST_ROWS = 64
ROW_HIDDEN = 48
ROW_LAST = 49
LANE_LOSS = 47
MIB = 1 << 20


def dims(left, right):
    return (((left,), (right,)), ((), ()))


NN, NT = dims(1, 0), dims(1, 1)


def dot(left, right, form):
    return lax.dot_general(left, right, form, preferred_element_type=F32)


def halves(value):
    high = value.astype(BF16)
    return high, (value - high.astype(F32)).astype(BF16)


def dot_split(left, right, form):
    (lh, ll), (rh, rl) = left, right
    return dot(lh, rh, form) + dot(lh, rl, form) + dot(ll, rh, form)


def dot_full(left, right, form):
    return dot_split(halves(left), halves(right), form)


def sigmoid(value):
    return 1.0 / (1.0 + jnp.exp(-value))


def call(body, outs, name, vmem, smem_first=True, scratch=()):
    def run(*args):
        specs = [pl.BlockSpec(memory_space=pltpu.SMEM)]
        specs += [pl.BlockSpec(memory_space=pltpu.VMEM)] * (len(args) - 1)
        return pl.pallas_call(
            body,
            out_shape=[jax.ShapeDtypeStruct(s, d) for s, d in outs],
            in_specs=specs,
            out_specs=[pl.BlockSpec(memory_space=pltpu.VMEM)] * len(outs),
            scratch_shapes=list(scratch),
            name=name,
            compiler_params=pltpu.CompilerParams(vmem_limit_bytes=vmem * MIB),
        )(*args)

    return run


class Sizes:
    def __init__(self, mesh, features, neigh_first, neigh_mid, neigh_last):
        self.ranks = mesh.shape["zh"] * mesh.shape["rl"]
        self.rl = mesh.shape["rl"]
        self.s1, self.t1 = features.shape[1], neigh_first.shape[1]
        self.t2, self.t3 = neigh_mid.shape[1], neigh_last.shape[1]
        self.f1, self.f2, self.f3 = neigh_first.shape[2], neigh_mid.shape[2], neigh_last.shape[2]
        l1, l2, l3 = self.t1 // LANES, self.t2 // LANES, self.t3 // LANES
        self.l1, self.l2, self.l3 = l1, l2, l3
        self.at_first = 0
        self.at_mid = self.at_first + self.f1 * l1
        self.at_last = self.at_mid + self.f2 * l2
        self.at_label = self.at_last + self.f3 * l3
        self.at_c1 = self.at_label + 2 * l3
        self.at_c2 = self.at_c1 + l1
        self.at_c3 = self.at_c2 + l2
        self.id_rows = -(-(self.at_c3 + l3) // 8) * 8
        self.rf, self.rm, self.rlast = 64 // self.ranks, 128 // self.ranks, LAST_ROWS // self.ranks
        self.rs_rows = self.rf + self.rm + self.rlast
        self.ag_rows = 2 * (self.rf + self.rm) + self.rlast


def prep_body(z, pos, feats, nf, cf, nm, cm, nl, cl, labels, wf, wm, wl, bh, f0, f1, ids, wmsg, rows):
    y = pos[2]
    f0[...] = feats[y]
    f1[...] = feats[1 - y]
    rows[...] = jnp.zeros_like(rows)

    def put(mb, at, value):
        for j in range(value.shape[1] // LANES):
            rows[mb, at + j : at + j + 1, :] = value[:, j * LANES : (j + 1) * LANES]

    for mb in range(2):
        for fan, nb, cnt, at, at_c in (
            (z.f1, nf, cf, z.at_first, z.at_c1),
            (z.f2, nm, cm, z.at_mid, z.at_c2),
            (z.f3, nl, cl, z.at_last, z.at_c3),
        ):
            count = cnt[mb : mb + 1, :]
            lanes = count.shape[1] // LANES
            for k in range(fan):
                put(mb, at + k * lanes, jnp.where(count > k, nb[k, mb : mb + 1, :], -1))
            put(mb, at_c, count)
        for other in range(2):
            put(mb, z.at_label + other * z.l3, labels[other : other + 1, :])
        for d in range(z.rl):
            ids[mb * z.rl + d] = rows[mb]
    for j in range(2):
        wmsg[32 * j : 32 * j + 32, :] = wf[j]
        wmsg[64 + 64 * j : 128 + 64 * j, :] = wm[j]
    wmsg[192:248, :] = jnp.zeros((56, 256), F32)
    for j in range(2):
        wmsg[192 : 192 + 47, 64 * j : 64 * j + 64] = wl[:, j, :]
        wmsg[240:241, 64 * j : 64 * j + 64] = bh[j : j + 1, :]


def weights_body(pos, wall, blast, w1h, w1l, w2h, w2l, wmh, wml, wlt, wlc, bias, f32a, f32b):
    for s in range(4):
        for j in range(2):
            f32a[128 * j + 32 * s : 128 * j + 32 * s + 32, :] = wall[s, 32 * j : 32 * j + 32, :]
            f32b[256 * j + 64 * s : 256 * j + 64 * s + 64, :] = wall[s, 64 + 64 * j : 128 + 64 * j, :]
            wlt[j, :, 64 * s : 64 * s + 64] = wall[s, 192 : 192 + CLASS_ROWS, 64 * j : 64 * j + 64]
    w1h[...], w1l[...] = halves(f32a[...].T)
    w2h[...], w2l[...] = halves(f32b[...].T)
    for j in range(2):
        wmh[j], wml[j] = halves(f32b[256 * j : 256 * j + 256, :])
        wlc[j] = jnp.concatenate([wlt[j], jnp.zeros((128 - CLASS_ROWS, 256), F32)], axis=0).T
    rows = [jnp.concatenate([wall[s, 240:241, 64 * j : 64 * j + 64] for s in range(4)], axis=1) for j in range(2)]
    last = jnp.concatenate([blast[...], jnp.zeros((1, 256 - 47), F32)], axis=1)
    packed = jnp.concatenate(rows + [last, jnp.zeros((125, 256), F32)], axis=0)
    bias[...] = packed.T


def one_hot_sum(rows, size, base):
    at = lax.broadcasted_iota(I32, (size, LANES), 0)
    total = jnp.zeros((size, LANES), F32)
    for row in rows:
        total = total + jnp.where(at == row - base, 1.0, 0.0)
    return total.astype(BF16)


def adjacency_body(z, pos, ids, a2, a3, mine, cw):
    zh, rl, y = pos[0], pos[1], pos[2]
    me = y * z.rl + rl
    mine[...] = ids[me]
    s2, s3 = a2.shape[0], a3.shape[0]
    piece = 128

    def block(r, carry):
        for at, fan, lanes, size, out in (
            (z.at_mid, z.f2, z.l2, s2, a2),
            (z.at_last, z.f3, z.l3, s3, a3),
        ):
            for j in range(lanes):
                rows = [ids[r, pl.ds(at + k * lanes + j, 1), :] - me * size for k in range(fan)]
                where = pl.ds(pl.multiple_of((r * lanes + j) * LANES, LANES), LANES)
                for g in range(size // piece):
                    out[g * piece : (g + 1) * piece, where] = one_hot_sum(rows, piece, g * piece)
        return carry

    lax.fori_loop(0, 2 * z.rl, block, 0)
    classes = lax.broadcasted_iota(I32, (CLASS_ROWS, LANES), 0)

    def tally(r, total):
        for other in range(2 * z.l3):
            row = ids[r, pl.ds(z.at_label + other, 1), :]
            total = total + jnp.where(classes == row, 1.0, 0.0)
        return total

    total = lax.fori_loop(0, 2 * z.rl, tally, jnp.zeros((CLASS_ROWS, LANES), F32))
    counts = jnp.sum(total, axis=1, keepdims=True)
    weight = 1.0 / jnp.maximum(counts, 1.0)
    cw[0] = jnp.broadcast_to(weight, (CLASS_ROWS, LANES))
    both = jnp.sum(counts * weight, axis=0, keepdims=True)
    cw[1] = jnp.broadcast_to(both, (CLASS_ROWS, LANES))


def first_body(z, pos, ids, fa, fb, out, table, adj):
    me = pos[2] * z.rl + pos[1]
    width = fa.shape[0] * 2
    rows = jnp.concatenate([fa[...], fb[...]], axis=0)
    table[:width], table[width:] = halves(rows)
    piece = 128

    def block(r, carry):
        for j in range(z.l1):
            rows = [ids[r, pl.ds(z.at_first + k * z.l1 + j, 1), :] - me * z.s1 for k in range(z.f1)]
            for g in range(z.s1 // piece):
                adj[g * piece : (g + 1) * piece, j * LANES : (j + 1) * LANES] = one_hot_sum(rows, piece, g * piece)
        both = dot(table[...], adj[...], NN)
        out[r] = both[:width] + both[width:]
        return carry

    lax.fori_loop(0, 2 * z.rl, block, 0)


def inverse(z, mine, at, lanes):
    row = jnp.concatenate([mine[at + j : at + j + 1, :] for j in range(lanes)], axis=1)
    return 1.0 / row.astype(F32)


def sum_first_body(z, pos, mine, part, fa, fb, out):
    half = fa.shape[0]
    out[:half] = fa[:, : z.t1]
    out[half : 2 * half] = fb[:, : z.t1]
    total = part[0]
    for r in range(1, 2 * z.rl):
        total = total + part[r]
    out[2 * half :] = total * inverse(z, mine, z.at_c1, z.l1)


def put_columns(pos, own, other, out):
    c = pos[3]
    for j in range(2):
        for y in range(2):
            at = 128 * j + 64 * y
            out[pl.ds(pl.multiple_of(at + 32 * c, 32), 32)] = own[64 * j + 32 * y : 64 * j + 32 * y + 32]
            out[pl.ds(pl.multiple_of(at + 32 * (1 - c), 32), 32)] = other[64 * j + 32 * y : 64 * j + 32 * y + 32]


def hidden_one_body(z, pos, own, other, w1h, w1l, bias, a2, out, x1, h1, slope):
    c = pos[3]
    put_columns(pos, own, other, x1)
    pre = dot_split((w1h[...], w1l[...]), halves(x1[...]), NN) + bias[:, 0:1]
    sigma = sigmoid(pre)
    h1[...] = pre * sigma
    slope[...] = sigma * (1.0 + pre * (1.0 - sigma))
    table = jnp.concatenate(halves(h1[pl.ds(pl.multiple_of(c * 128, 128), 128)]), axis=0)
    for r in range(2 * z.rl):
        both = dot(table, a2[:, r * z.t2 : (r + 1) * z.t2], NN)
        out[r] = both[:128] + both[128:]


def sum_mid_body(z, pos, mine, part, out):
    total = part[0]
    for r in range(1, 2 * z.rl):
        total = total + part[r]
    out[...] = total * inverse(z, mine, z.at_c2, z.l2)


def hidden_two_body(z, pos, own, other, h1, w2h, w2l, bias, wlt, a3, out, y2, h2, slope, local):
    c = pos[3]
    y2[:256] = h1[:, : z.t2]
    y2[pl.ds(pl.multiple_of(256 + c * 128, 128), 128)] = own[...]
    y2[pl.ds(pl.multiple_of(256 + (1 - c) * 128, 128), 128)] = other[...]
    pre = dot_split((w2h[...], w2l[...]), halves(y2[...]), NN) + bias[:, 1:2]
    sigma = sigmoid(pre)
    hidden = pre * sigma
    h2[...] = hidden
    slope[...] = sigma * (1.0 + pre * (1.0 - sigma))
    split = halves(hidden)
    local[...] = dot_split(halves(wlt[0]), (split[0][:, : z.t3], split[1][:, : z.t3]), NN)
    table = jnp.concatenate(halves(dot_split(halves(wlt[1]), split, NN)), axis=0)
    for r in range(2 * z.rl):
        both = dot(table, a3[:, r * z.t3 : (r + 1) * z.t3], NN)
        out[r] = both[:CLASS_ROWS] + both[CLASS_ROWS:]


def logits_body(z, pos, mine, part, local, bias, cw, out, grad, loss):
    total = part[0]
    for r in range(1, 2 * z.rl):
        total = total + part[r]
    recip = inverse(z, mine, z.at_c3, z.l3)
    logits = total * recip + local[...] + bias[:CLASS_ROWS, 2:3]
    classes = lax.broadcasted_iota(I32, logits.shape, 0)
    logits = jnp.where(classes < 47, logits, -jnp.inf)
    label = jnp.where(
        pos[0] == 0,
        mine[z.at_label : z.at_label + 1, :],
        mine[z.at_label + z.l3 : z.at_label + z.l3 + 1, :],
    )
    onehot = jnp.where(classes == label, 1.0, 0.0)
    top = jnp.max(logits, axis=0, keepdims=True)
    powers = jnp.exp(logits - top)
    norm = jnp.sum(powers, axis=0, keepdims=True)
    weight = jnp.sum(onehot * cw[0], axis=0, keepdims=True)
    target = jnp.sum(jnp.where(classes == label, logits, 0.0), axis=0, keepdims=True)
    each = weight * (jnp.log(norm) + top - target)
    loss[...] = jnp.broadcast_to(jnp.sum(each, axis=1, keepdims=True), loss.shape)
    dlogits = weight * (powers / norm - onehot) / cw[1, 0:1, :]
    grad[...] = dlogits
    scaled = dlogits * recip
    for r in range(2 * z.rl):
        out[r] = scaled


def back_last_body(z, pos, mine, gall, grad, a3, wlc, h2, slope, out, dpre2, dwl):
    c = pos[3]
    both = None
    for r in range(2 * z.rl):
        table = jnp.concatenate(halves(gall[r]), axis=0)
        term = dot(table, a3[:, r * z.t3 : (r + 1) * z.t3], NT)
        both = term if both is None else both + term
    spread = both[:CLASS_ROWS] + both[CLASS_ROWS:]
    dh = dot_full(wlc[1][:, :CLASS_ROWS], spread, NN)
    own = dot_full(wlc[0][:, :CLASS_ROWS], grad[...], NN)
    dh = dh + jnp.concatenate([own, jnp.zeros((256, z.t2 - z.t3), F32)], axis=1)
    dpre2[...] = dh * slope[...]
    scaled = dpre2[pl.ds(pl.multiple_of(c * 128, 128), 128)] * inverse(z, mine, z.at_c2, z.l2)
    for r in range(2 * z.rl):
        out[r] = scaled
    dwl[0] = dot_full(grad[...], h2[:, : z.t3], NT)
    dwl[1] = dot_full(spread, h2[...], NT)


def back_mid_body(z, pos, gall, a2, out):
    both = None
    for r in range(2 * z.rl):
        table = jnp.concatenate(halves(gall[r]), axis=0)
        term = dot(table, a2[:, r * z.t2 : (r + 1) * z.t2], NT)
        both = term if both is None else both + term
    out[...] = both[:128] + both[128:]


def row_sums(value):
    ones = jnp.ones((8, value.shape[1]), BF16)
    high, low = halves(value)
    return dot(ones, high, NT) + dot(ones, low, NT)


def grads_body(z, pos, own, other, dpre2, wmh, wml, slope, x1, y2, dwl, grad, loss, out, spread, first, mid, last):
    c = pos[3]
    mine = pl.ds(pl.multiple_of(c * 128, 128), 128)
    spread[mine] = own[...]
    spread[pl.ds(pl.multiple_of((1 - c) * 128, 128), 128)] = other[...]
    dh = dot_split((wmh[1, mine, :], wml[1, mine, :]), halves(spread[...]), NN)
    at_own = dot_split((wmh[0, mine, :], wml[0, mine, :]), halves(dpre2[...]), NN)
    dh = dh + jnp.concatenate([at_own, jnp.zeros((128, z.t1 - z.t2), F32)], axis=1)
    dpre1 = dh * slope[mine]
    half2 = dpre2[mine]
    first[...] = dot_full(x1[...], dpre1, NT)
    mid[...] = dot_full(y2[...], half2, NT)
    b1, b2, b3 = row_sums(dpre1), row_sums(half2), row_sums(grad[...])
    last[...] = jnp.zeros_like(last)
    core0 = jnp.where(c == 0, 1.0, 0.0)
    for s in range(4):
        last[s, :CLASS_ROWS, :64] = dwl[0][:, 64 * s : 64 * s + 64] * core0
        last[s, :CLASS_ROWS, 64:] = dwl[1][:, 64 * s : 64 * s + 64] * (1.0 - core0)
        here = jnp.where(c == s // 2, 1.0, 0.0)
        at = 64 * (s % 2)
        last[s, ROW_HIDDEN : ROW_HIDDEN + 1, :64] = b1[0:1, at : at + 64] * here
        last[s, ROW_HIDDEN : ROW_HIDDEN + 1, 64:] = b2[0:1, at : at + 64] * here
        last[s, ROW_LAST : ROW_LAST + 1, :LANE_LOSS] = b3[0:1, :LANE_LOSS] * core0
        last[s, ROW_LAST : ROW_LAST + 1, LANE_LOSS : LANE_LOSS + 1] = loss[0:1, 0:1] * core0
    for q in range(z.ranks):
        for s in range(4):
            d = q * 4 + s
            e = z.rf * q
            at = 128 * (e // 32) + 32 * s + e % 32
            out[d, : z.rf] = first[at : at + z.rf]
            e = z.rm * q
            at = 256 * (e // 64) + 64 * s + e % 64
            out[d, z.rf : z.rf + z.rm] = mid[at : at + z.rm]
            out[d, z.rf + z.rm :] = last[s, z.rlast * q : z.rlast * (q + 1)]


def sum_grads_body(z, pos, part, out):
    n = z.rf + z.rm
    even, odd = part[0], part[1]
    for d in range(2, z.ranks * 4, 2):
        even = even + part[d]
        odd = odd + part[d + 1]
    for q in range(z.ranks):
        out[q, :n] = even[:n]
        out[q, n : 2 * n] = odd[:n]
        out[q, 2 * n :] = even[n:] + odd[n:]


def squares_body(z, pos, whole, out):
    n = 2 * (z.rf + z.rm)
    first_cols = jnp.where(jnp.logical_and(pos[2] == 0, pos[3] == 0), 1.0, 0.0)
    total = jnp.zeros((1, LANES), F32)
    lane = lax.broadcasted_iota(I32, (1, LANES), 1)
    for q in range(z.ranks):
        value = whole[q, :n]
        total = total + jnp.sum(value * value, axis=0, keepdims=True)
        for i in range(z.rlast):
            at = q * z.rlast + i
            row = whole[q, n + i : n + i + 1]
            if at <= ROW_HIDDEN:
                total = total + row * row
            elif at == ROW_LAST:
                total = total + jnp.where(lane < 47, row * row, 0.0) * first_cols
    out[...] = jnp.broadcast_to(jnp.sum(total, axis=1, keepdims=True), out.shape)


def update_body(z, pos, whole, s0, s1, s2, s3, cw, *refs):
    w, m, v = refs[0:5], refs[5:10], refs[10:15]
    new, moment, square = refs[15:20], refs[20:25], refs[25:30]
    loss, weight_sum, norm = refs[30:33]
    total = s0[0:1, 0:1] + s1[0:1, 0:1] + s2[0:1, 0:1] + s3[0:1, 0:1]
    root = jnp.sqrt(total)
    scale = jnp.minimum(1.0, 0.01 / root)
    norm[...] = root
    weight_sum[...] = cw[1, 0:1, 0:1]

    def adamw(weight, grad, first, second):
        grad = grad * scale
        mo = 0.9 * first + 0.1 * grad
        sq = 0.999 * second + 0.001 * grad * grad
        corrected = mo / (1.0 - 0.9**STEP)
        rt = jnp.sqrt(sq / (1.0 - 0.999**STEP))
        return (weight - 0.05 * (corrected / (rt + 1e-08) + 0.01 * weight), mo, sq)

    def put(i, at, grad):
        outs = adamw(w[i][at], grad, m[i][at], v[i][at])
        new[i][at], moment[i][at], square[i][at] = outs

    n = z.rf + z.rm
    for q in range(z.ranks):
        e = z.rf * q
        g = jnp.concatenate([whole[q, : z.rf], whole[q, n : n + z.rf]], axis=1)
        put(0, (e // 32, slice(e % 32, e % 32 + z.rf), slice(None)), g)
        e = z.rm * q
        g = jnp.concatenate([whole[q, z.rf : n], whole[q, n + z.rf : 2 * n]], axis=1)
        put(1, (e // 64, slice(e % 64, e % 64 + z.rm), slice(None)), g)
        a = z.rlast * q
        b = min(a + z.rlast, 47)
        if a < b:
            for j in range(2):
                put(2, (slice(a, b), j, slice(None)), whole[q, 2 * n : 2 * n + b - a, 64 * j : 64 * j + 64])
        for i in range(z.rlast):
            row = whole[q, 2 * n + i : 2 * n + i + 1]
            if a + i == ROW_HIDDEN:
                for j in range(2):
                    put(3, (slice(j, j + 1), slice(None)), row[:, 64 * j : 64 * j + 64])
            elif a + i == ROW_LAST:
                put(4, (slice(None), slice(None)), row[:, :47])
                loss[...] = row[:, LANE_LOSS : LANE_LOSS + 1]


def on_device(
    mesh, features, neigh_first, count_first, neigh_mid, count_mid, neigh_last, count_last, labels,
    w_first, w_mid, w_last, b_hidden, b_last,
    m_first, m_mid, m_last, m_hidden, m_bias,
    v_first, v_mid, v_last, v_hidden, v_bias,
):
    z = Sizes(mesh, features, neigh_first, neigh_mid, neigh_last)
    bind = functools.partial
    blocks = 2 * z.rl
    pos = jnp.stack([lax.axis_index(a) for a in ("zh", "rl", "y", "c")]).astype(I32)

    def flip(value):
        return lax.ppermute(value, "c", [(0, 1), (1, 0)])

    def exchange(value):
        return lax.all_to_all(value, ("y", "rl"), 0, 0)

    def swapped(value):
        return jnp.transpose(value, (2, 0, 1))

    f0, f1, ids, wmsg = call(
        bind(prep_body, z),
        [((32, z.s1), F32), ((32, z.s1), F32), ((z.ranks, z.id_rows, LANES), I32), ((248, 256), F32)],
        "prep", 8, scratch=[pltpu.VMEM((2, z.id_rows, LANES), I32)],
    )(
        pos, jnp.transpose(features, (0, 2, 1)), swapped(neigh_first), count_first, swapped(neigh_mid), count_mid,
        swapped(neigh_last), count_last, labels, w_first, w_mid, swapped(w_last), b_hidden,
    )
    got = [
        lax.ppermute(f, ("zh", "y"), [(2 * zh + y, 2 * (y ^ j) + zh) for zh in range(2) for y in range(2)])
        for j, f in enumerate((f0, f1))
    ]
    wall = lax.all_gather(wmsg, ("y", "c"), axis=0)
    ids = lax.all_to_all(ids, ("zh", "rl"), 0, 0)
    swap = pos[0] == 1
    fa = jnp.where(swap, got[1], got[0])
    fb = jnp.where(swap, got[0], got[1])

    a2, a3, mine, cw = call(
        bind(adjacency_body, z),
        [
            ((z.t1, blocks * z.t2), BF16), ((z.t2, blocks * z.t3), BF16),
            ((z.id_rows, LANES), I32), ((2, CLASS_ROWS, LANES), F32),
        ],
        "adjacency", 24,
    )(pos, ids)
    part = call(
        bind(first_body, z), [((blocks, 64, z.t1), F32)], "first", 24,
        scratch=[pltpu.VMEM((128, z.s1), BF16), pltpu.VMEM((z.s1, z.t1), BF16)],
    )(pos, ids, fa, fb)[0]
    w1h, w1l, w2h, w2l, wmh, wml, wlt, wlc, bias = call(
        weights_body,
        [
            ((256, 256), BF16), ((256, 256), BF16), ((256, 512), BF16), ((256, 512), BF16),
            ((2, 256, 256), BF16), ((2, 256, 256), BF16),
            ((2, CLASS_ROWS, 256), F32), ((2, 256, 128), F32), ((256, 128), F32),
        ],
        "weights", 16, scratch=[pltpu.VMEM((256, 256), F32), pltpu.VMEM((512, 256), F32)],
    )(pos, wall, b_last[None])
    part = exchange(part)
    half = call(bind(sum_first_body, z), [((128, z.t1), F32)], "sum_first", 16)(pos, mine, part, fa, fb)[0]
    other = flip(half)
    part, x1, h1, slope1 = call(
        bind(hidden_one_body, z),
        [((blocks, 128, z.t2), F32), ((256, z.t1), F32), ((256, z.t1), F32), ((256, z.t1), F32)],
        "hidden_one", 32,
    )(pos, half, other, w1h, w1l, bias, a2)
    part = exchange(part)
    half = call(bind(sum_mid_body, z), [((128, z.t2), F32)], "sum_mid", 16)(pos, mine, part)[0]
    other = flip(half)
    part, y2, h2, slope2, local = call(
        bind(hidden_two_body, z),
        [
            ((blocks, CLASS_ROWS, z.t3), F32), ((512, z.t2), F32), ((256, z.t2), F32), ((256, z.t2), F32),
            ((CLASS_ROWS, z.t3), F32),
        ],
        "hidden_two", 24,
    )(pos, half, other, h1, w2h, w2l, bias, wlt, a3)
    part = exchange(part)
    part, grad, loss = call(
        bind(logits_body, z),
        [((blocks, CLASS_ROWS, z.t3), F32), ((CLASS_ROWS, z.t3), F32), ((8, LANES), F32)],
        "logits", 8,
    )(pos, mine, part, local, bias, cw)
    part = exchange(part)
    part, dpre2, dwl = call(
        bind(back_last_body, z),
        [((blocks, 128, z.t2), F32), ((256, z.t2), F32), ((2, CLASS_ROWS, 256), F32)],
        "back_last", 24,
    )(pos, mine, part, grad, a3, wlc, h2, slope2)
    part = exchange(part)
    half = call(bind(back_mid_body, z), [((128, z.t1), F32)], "back_mid", 24)(pos, part, a2)[0]
    other = flip(half)
    part = call(
        bind(grads_body, z), [((z.ranks * 4, z.rs_rows, LANES), F32)], "grads", 24,
        scratch=[
            pltpu.VMEM((256, z.t1), F32), pltpu.VMEM((256, 128), F32), pltpu.VMEM((512, 128), F32),
            pltpu.VMEM((4, LAST_ROWS, LANES), F32),
        ],
    )(pos, half, other, dpre2, wmh, wml, slope1, x1, y2, dwl, grad, loss)[0]
    part = lax.all_to_all(part, ("zh", "rl", "y", "c"), 0, 0)
    part = call(bind(sum_grads_body, z), [((z.ranks, z.ag_rows, LANES), F32)], "sum_grads", 8)(pos, part)[0]
    whole = lax.all_to_all(part, ("zh", "rl"), 0, 0)
    mine_sq = call(bind(squares_body, z), [((8, LANES), F32)], "squares", 8)(pos, whole)[0]
    pair = [(i, i ^ 1) for i in range(4)]
    across = [(i, i ^ 2) for i in range(4)]
    both = [(i, i ^ 3) for i in range(4)]
    others = [lax.ppermute(mine_sq, ("y", "c"), p) for p in (across, both, pair)]

    params = (w_first, w_mid, swapped(w_last), b_hidden, b_last[None])
    firsts = (m_first, m_mid, swapped(m_last), m_hidden, m_bias[None])
    seconds = (v_first, v_mid, swapped(v_last), v_hidden, v_bias[None])
    shapes = [(p.shape, F32) for p in params]
    outs = call(bind(update_body, z), shapes * 3 + [((1, 1), F32)] * 3, "update", 8)(
        pos, whole, mine_sq, *others, cw, *params, *firsts, *seconds
    )
    results = []
    for g in range(3):
        a, b, c, d, e = outs[5 * g : 5 * g + 5]
        results += [a, b, jnp.transpose(c, (1, 2, 0)), d, e[0]]
    return tuple(results) + tuple(o[0, 0] for o in outs[15:])


def solution(mesh):
    rows, cols = mesh.shape["rows"], mesh.shape["cols"]
    fine = Mesh(mesh.devices.reshape(2, rows // 2, 2, cols // 2), ("zh", "rl", "y", "c"))
    r, c = ("zh", "rl"), ("y", "c")
    weights = (P(None, c, None),) * 3 + (P(None, c), P())
    nodes = (P(None, r, None), P(None, r))
    placed = (P(None, r, c),) + nodes * 3 + (P(None, r),) + weights * 3
    return jax.shard_map(
        functools.partial(on_device, fine),
        mesh=fine,
        in_specs=placed,
        out_specs=weights * 3 + (P(), P(), P()),
        check_vma=False,
    )
```

time: 887 us -> 186 us (0.21)
  waiting for transfers between devices: 504 us -> 19.1 us
  other arithmetic: 97.3 us -> 0.1 us
  blocking collectives: 173 us -> 93.1 us
  local copies, waits for them, and re-layouts: 59.7 us -> 13.6 us
  Pallas kernels: 0 us -> 39.1 us
  matrix products: 24.5 us -> 0 us
  between operations: 22.3 us -> 1.01 us
  starting transfers between devices: 0.8 us -> 18.8 us
    reduce_scatter x8 -> x0, waiting for transfers between devices: 275 us -> none  [the longest x4 210 us: neighbor_back(): return lax.psum_scatter(whole, 'rows', scatter_dimension=0, tiled=True)]
    all_gather x4 -> x0, waiting for transfers between devices: 164 us -> none  [neighbor_mean(): whole = lax.all_gather(hidden, 'rows', axis=0, tiled=True)]
    all_gather x6 -> x1, blocking collectives: 98.4 us -> 10.3 us  [on_device(): wall = lax.all_gather(wmsg, ('y', 'c'), axis=0)]
    all_to_all x0 -> x6, blocking collectives: none -> 82.8 us  [the longest x4 53.3 us: exchange(): return lax.all_to_all(value, ('y', 'rl'), 0, 0)]
    psum x4 -> x0, blocking collectives: 74.2 us -> none  [the longest x1 35.6 us: on_device(): lax.psum((local[0], local[1], local[2], local[3], local[4], local[5]), 'r...]
    psum x1 -> x0, waiting for transfers between devices: 65.1 us -> none  [on_device(): lax.psum((local[0], local[1], local[2], local[3], local[4], local[5]), 'r...]
    scatter-add x4 -> x0, other arithmetic: 54.2 us -> none  [neighbor_back(): whole = jnp.zeros((before * lax.axis_size('rows'), grad_mean.shape[1]), j...]
    pallas_call x0 -> x15, Pallas kernels: none -> 39.1 us  [run(): pl.pallas_call(body, out_shape=[jax.ShapeDtypeStruct(s, d) for s, d in ou...]
  transfers between devices with their start and end apart: 13 -> 10, of which waited for: 13 -> 7; matrix products, arithmetic and copies ran while one was open for 13% -> 0% of each run, Pallas kernels for 0% -> 5%
where the time goes in v1:
time: 186 us; the launch traced here: 185 us
  blocking collectives  93.1 us (50%)
  Pallas kernels  39.1 us (21%)
  waiting for transfers between devices  19.1 us (10%)
  starting transfers between devices  18.8 us (10%)
  local copies, waits for them, and re-layouts  13.6 us (7%)
    all_to_all x4, blocking collectives, exchange(): return lax.all_to_all(value, ('y', 'rl'), 0, 0)  53.3 us
    pallas_call x15, Pallas kernels, run(): pl.pallas_call(body, out_shape=[jax.ShapeDtypeStruct(s, d) for s, d in ou...  39.1 us
    all_to_all x1, blocking collectives, on_device(): part = lax.all_to_all(part, ('zh', 'rl', 'y', 'c'), 0, 0)  18.1 us
    unnamed x72, local copies, waits for them, and re-layouts  13.6 us
    all_to_all x1, blocking collectives, on_device(): whole = lax.all_to_all(part, ('zh', 'rl'), 0, 0)  11.4 us
    all_gather x1, blocking collectives, on_device(): wall = lax.all_gather(wmsg, ('y', 'c'), axis=0)  10.3 us
    all_to_all x1, starting transfers between devices, on_device(): ids = lax.all_to_all(ids, ('zh', 'rl'), 0, 0)  7.25 us
    all_to_all x1, starting transfers between devices, exchange(): return lax.all_to_all(value, ('y', 'rl'), 0, 0)  5.62 us
  transfers between devices with their start and end apart: 10, of which 7 were waited for; matrix products, arithmetic and copies ran while one was open for 0% of the time, Pallas kernels for 5%

profile of v1, /device:TPU:0, one launch (start us, length us, event | category | flops | bytes accessed | tf_op | source)
XLA Modules:
  0.0 184.7 jit_solution(9754083836749961022)
XLA Ops:
  0.7 0.9 copy-done.6
  1.6 0.9 copy-done.8
  2.6 0.8 copy-done.9
  9.8 1.4 prep.1
  11.9 7.3 %all-to-all-start = ((s32[8,64,128]{2,1,0:T(8,128)}), s32[8,64,128]{2,1,0:T(8,128)S(1)}, u32[]{:S(2)}, u32[]{:S(2)}) async-start(s32[8,64,128]{2,1,0:T(8,128)} %get-tuple-element.68), calls=%async_computation | async-start | bytes 524288 | tf_op jit(solution)/shard_map/all_to_all | solution.py:474
  19.1 2.9 %collective-permute-start = (f32[32,1024]{1,0:T(8,128)S(1)}, f32[32,1024]{1,0:T(8,128)S(1)}, u32[]{:S(2)}, u32[]{:S(2)}) collective-permute-start(f32[32,1024]{1,0:T(8,128)S(1)} %get-tuple-element.70), channel_id=1, source_target_pairs={{0,16},{2,0},{16,18},{18,2},{1,17},{3,1},{17,19},{19,3},{4,20},{6,... | collective-permute-start | bytes 393224 | tf_op jit(solution)/shard_map/ppermute | solution.py:470
  22.7 3.6 %collective-permute-done = f32[32,1024]{1,0:T(8,128)S(1)} collective-permute-done((f32[32,1024]{1,0:T(8,128)S(1)}, f32[32,1024]{1,0:T(8,128)S(1)}, u32[]{:S(2)}, u32[]{:S(2)}) %collective-permute-start) | collective-permute-done | bytes 131104 | tf_op jit(solution)/shard_map/ppermute | solution.py:470
  26.3 5.4 %all-to-all-done.ids = s32[8,64,128]{2,1,0:T(8,128)S(1)} async-done(((s32[8,64,128]{2,1,0:T(8,128)}), s32[8,64,128]{2,1,0:T(8,128)S(1)}, u32[]{:S(2)}, u32[]{:S(2)}) %all-to-all-start) | async-done | bytes 262176 | tf_op jit(solution)/shard_map/all_to_all | solution.py:474
  31.8 15.1 %first.1 = f32[8,64,512]{2,1,0:T(8,128)} custom-call(s32[4]{0:T(128)S(1)} %pad_add_fusion.pos, s32[8,64,128]{2,1,0:T(8,128)S(1)} %all-to-all-done.ids, f32[32,1024]{1,0:T(8,128)S(1)} %get-tuple-element.119.fa, f32[32,1024]{1,0:T(8,128)S(1)} %get-tuple-element.118.fb), custom_call_target="tpu_custom_call" | custom-call | tf_op jit(solution)/shard_map/first/pallas_call | solution.py:57
  46.9 5.6 %all-to-all-start.1 = ((f32[8,64,512]{2,1,0:T(8,128)}), f32[8,64,512]{2,1,0:T(8,128)S(1)}, u32[]{:S(2)}, u32[]{:S(2)}) async-start(f32[8,64,512]{2,1,0:T(8,128)} %first.1), calls=%async_computation.1 | async-start | bytes 2097152 | tf_op jit(solution)/shard_map/all_to_all | solution.py:456
  52.5 8.6 %adjacency.1 = (bf16[512,2048]{1,0:T(8,128)(2,1)S(1)}, bf16[256,1024]{1,0:T(8,128)(2,1)S(1)}, s32[64,128]{1,0:T(8,128)S(1)}, f32[2,48,128]{2,1,0:T(8,128)S(1)}) custom-call(s32[4]{0:T(128)S(1)} %pad_add_fusion.pos, s32[8,64,128]{2,1,0:T(8,128)S(1)} %all-to-all-done.ids), custom_call_target="tpu_custom_call" | custom-call | tf_op jit(solution)/shard_map/adjacency/pallas_call | solution.py:57
  63.1 4.4 %all-to-all-done.1.part = f32[8,64,512]{2,1,0:T(8,128)S(1)} async-done(((f32[8,64,512]{2,1,0:T(8,128)}), f32[8,64,512]{2,1,0:T(8,128)S(1)}, u32[]{:S(2)}, u32[]{:S(2)}) %all-to-all-start.1) | async-done | bytes 1048608 | tf_op jit(solution)/shard_map/all_to_all | solution.py:456
  67.6 0.9 copy-done.3
  69.9 10.3 %all-gather = f32[992,256]{1,0:T(8,128)S(1)} all-gather(f32[248,256]{1,0:T(8,128)} %copy-done.11), channel_id=2, replica_groups=mesh['zh'=2,'rl'=4,'y'=2,'c'=2] {'y','c'}, dimensions={0}, use_global_device_ids=true | all-gather | bytes 1269760 | tf_op jit(solution)/shard_map/all_gather | solution.py:473
  80.2 1.0 weights.1
  81.2 1.8 hidden_one.1
  83.0 18.7 %all_to_all.40.part = f32[8,128,256]{2,1,0:T(8,128)S(1)} all-to-all(f32[8,128,256]{2,1,0:T(8,128)S(1)} %get-tuple-element.77), channel_id=1, replica_groups=mesh['zh'=2,'rl'=4,'y'=2,'c'=2] {'y','rl'}, dimensions={0} | all-to-all | bytes 2097152 | tf_op jit(solution)/shard_map/all_to_all | solution.py:456
  102.5 1.3 collective-permute-done.3.other
  103.8 1.7 hidden_two.1
  105.5 9.3 %all_to_all.41.part = f32[8,48,128]{2,1,0:T(8,128)S(1)} all-to-all(f32[8,48,128]{2,1,0:T(8,128)S(1)} %get-tuple-element.83), channel_id=1, replica_groups=mesh['zh'=2,'rl'=4,'y'=2,'c'=2] {'y','rl'}, dimensions={0} | all-to-all | bytes 393216 | tf_op jit(solution)/shard_map/all_to_all | solution.py:456
  115.5 9.0 %all_to_all.42.gall = f32[8,48,128]{2,1,0:T(8,128)S(1)} all-to-all(f32[8,48,128]{2,1,0:T(8,128)S(1)} %get-tuple-element.86), channel_id=1, replica_groups=mesh['zh'=2,'rl'=4,'y'=2,'c'=2] {'y','rl'}, dimensions={0} | all-to-all | bytes 393216 | tf_op jit(solution)/shard_map/all_to_all | solution.py:456
  124.5 1.5 back_last.1
  126.1 16.3 %all_to_all.43.gall = f32[8,128,256]{2,1,0:T(8,128)S(1)} all-to-all(f32[8,128,256]{2,1,0:T(8,128)S(1)} %get-tuple-element.91), channel_id=1, replica_groups=mesh['zh'=2,'rl'=4,'y'=2,'c'=2] {'y','rl'}, dimensions={0} | all-to-all | bytes 2097152 | tf_op jit(solution)/shard_map/all_to_all | solution.py:456
  142.3 1.3 back_mid.1.own
  143.7 1.5 collective-permute-done.4.other
  145.2 1.7 grads.1
  147.0 18.1 %all_to_all.44.part = f32[32,32,128]{2,1,0:T(8,128)S(1)} all-to-all(f32[32,32,128]{2,1,0:T(8,128)S(1)} %grads.1), channel_id=1, replica_groups=mesh['zh'=2,'rl'=4,'y'=2,'c'=2] {'zh','rl','y','c'}, dimensions={0} | all-to-all | bytes 1048576 | tf_op jit(solution)/shard_map/all_to_all | solution.py:541
  165.8 11.4 %all_to_all.45.whole = f32[8,56,128]{2,1,0:T(8,128)S(1)} all-to-all(f32[8,56,128]{2,1,0:T(8,128)S(1)} %sum_grads.1), channel_id=1, replica_groups=mesh['zh'=2,'rl'=4,'y'=2,'c'=2] {'zh','rl'}, dimensions={0} | all-to-all | bytes 458752 | tf_op jit(solution)/shard_map/all_to_all | solution.py:543
  177.8 1.3 collective-permute-start.6
  180.0 1.0 collective-permute-done.6.s2
  180.9 1.9 %collective-permute-done.5.s1 = f32[8,128]{1,0:T(8,128)S(1)} collective-permute-done((f32[8,128]{1,0:T(8,128)S(1)}, f32[8,128]{1,0:T(8,128)S(1)}, u32[]{:S(2)}, u32[]{:S(2)}) %collective-permute-start.5) | collective-permute-done | bytes 4128 | tf_op jit(solution)/shard_map/ppermute | solution.py:548
  182.9 1.8 update.1
  (84 shorter events, 14.9 us)
Async XLA Ops:
  0.7 0.9 copy-start.6
  1.6 0.9 copy-start.8
  2.6 0.8 copy-start.9
  11.9 19.9 %all-to-all-start = ((s32[8,64,128]{2,1,0:T(8,128)}), s32[8,64,128]{2,1,0:T(8,128)S(1)}, u32[]{:S(2)}, u32[]{:S(2)}) async-start(s32[8,64,128]{2,1,0:T(8,128)} %get-tuple-element.68), calls=%async_computation | async-start | bytes 524288 | tf_op jit(solution)/shard_map/all_to_all | solution.py:474
  19.1 7.2 %collective-permute-start = (f32[32,1024]{1,0:T(8,128)S(1)}, f32[32,1024]{1,0:T(8,128)S(1)}, u32[]{:S(2)}, u32[]{:S(2)}) collective-permute-start(f32[32,1024]{1,0:T(8,128)S(1)} %get-tuple-element.70), channel_id=1, source_target_pairs={{0,16},{2,0},{16,18},{18,2},{1,17},{3,1},{17,19},{19,3},{4,20},{6,... | collective-permute-start | bytes 393224 | tf_op jit(solution)/shard_map/ppermute | solution.py:470
  22.0 4.3 %collective-permute-start.1 = (f32[32,1024]{1,0:T(8,128)S(1)}, f32[32,1024]{1,0:T(8,128)S(1)}, u32[]{:S(2)}, u32[]{:S(2)}) collective-permute-start(f32[32,1024]{1,0:T(8,128)S(1)} %get-tuple-element.71), channel_id=1, source_target_pairs={{0,0},{2,16},{16,2},{18,18},{1,1},{3,17},{17,3},{19,19},{4,4},{6,2... | collective-permute-start | bytes 393224 | tf_op jit(solution)/shard_map/ppermute | solution.py:470
  26.3 20.5 %copy-start.2 = (f32[32,1024]{1,0:T(8,128)}, f32[32,1024]{1,0:T(8,128)S(1)}, u32[]{:S(2)}) copy-start(f32[32,1024]{1,0:T(8,128)S(1)} %get-tuple-element.119.fa) | copy-start | bytes 393220
  46.9 20.7 %all-to-all-start.1 = ((f32[8,64,512]{2,1,0:T(8,128)}), f32[8,64,512]{2,1,0:T(8,128)S(1)}, u32[]{:S(2)}, u32[]{:S(2)}) async-start(f32[8,64,512]{2,1,0:T(8,128)} %first.1), calls=%async_computation.1 | async-start | bytes 2097152 | tf_op jit(solution)/shard_map/all_to_all | solution.py:456
  52.5 27.8 %copy-start.29 = (f32[47]{0:T(128)S(1)}, f32[47]{0:T(128)}, u32[]{:S(2)}) copy-start(f32[47]{0:T(128)} %param.35) | copy-start | bytes 568
  67.6 0.9 copy-start.3
  69.8 11.4 %collective-permute-start.2 = (f32[128,512]{1,0:T(8,128)S(1)}, f32[128,512]{1,0:T(8,128)S(1)}, u32[]{:S(2)}, u32[]{:S(2)}) collective-permute-start(f32[128,512]{1,0:T(8,128)S(1)} %sum_first.1.own), channel_id=1, source_target_pairs={{0,1},{1,0},{2,3},{3,2},{4,5},{5,4},{6,7},{7,6},{8,9},{9,8},{10,11... | collective-permute-start | bytes 786440 | tf_op jit(solution)/shard_map/ppermute | solution.py:453
  83.0 20.8 %copy-start.1 = (bf16[256,1024]{1,0:T(8,128)(2,1)S(1)}, bf16[256,1024]{1,0:T(8,128)(2,1)}, u32[]{:S(2)}) copy-start(bf16[256,1024]{1,0:T(8,128)(2,1)} %copy-done) | copy-start | bytes 1572868
  101.8 13.0 %copy-start.13 = (f32[2,48,128]{2,1,0:T(8,128)S(1)}, f32[2,48,128]{2,1,0:T(8,128)}, u32[]{:S(2)}) copy-start(f32[2,48,128]{2,1,0:T(8,128)} %copy-done.12) | copy-start | bytes 147460
  102.4 1.4 collective-permute-start.3
  143.6 1.6 collective-permute-start.4
  146.9 35.9 %copy-start.7 = (f32[2,64,256]{2,1,0:T(8,128)S(1)}, f32[2,64,256]{2,1,0:T(8,128)}, u32[]{:S(2)}) copy-start(f32[2,64,256]{2,1,0:T(8,128)} %refs_1_.1) | copy-start | bytes 393220
  146.9 35.9 %copy-start.10 = (f32[2,32,256]{2,1,0:T(8,128)S(1)}, f32[2,32,256]{2,1,0:T(8,128)}, u32[]{:S(2)}) copy-start(f32[2,32,256]{2,1,0:T(8,128)} %refs_0_.1) | copy-start | bytes 196612
  146.9 35.9 %copy-start.15 = (f32[2,64,47]{1,0,2:T(2,128)S(1)}, f32[2,64,47]{1,0,2:T(2,128)}, u32[]{:S(2)}) copy-start(f32[2,64,47]{1,0,2:T(2,128)} %param.33) | copy-start | bytes 72196
  146.9 35.9 %copy-start.16 = (f32[2,64,256]{2,1,0:T(8,128)S(1)}, f32[2,64,256]{2,1,0:T(8,128)}, u32[]{:S(2)}) copy-start(f32[2,64,256]{2,1,0:T(8,128)} %refs_6_.1) | copy-start | bytes 393220
  146.9 35.9 %copy-start.17 = (f32[2,64,256]{2,1,0:T(8,128)S(1)}, f32[2,64,256]{2,1,0:T(8,128)}, u32[]{:S(2)}) copy-start(f32[2,64,256]{2,1,0:T(8,128)} %refs_11_.1) | copy-start | bytes 393220
  146.9 35.9 %copy-start.18 = (f32[2,32,256]{2,1,0:T(8,128)S(1)}, f32[2,32,256]{2,1,0:T(8,128)}, u32[]{:S(2)}) copy-start(f32[2,32,256]{2,1,0:T(8,128)} %refs_5_.1) | copy-start | bytes 196612
  146.9 35.9 %copy-start.19 = (f32[2,32,256]{2,1,0:T(8,128)S(1)}, f32[2,32,256]{2,1,0:T(8,128)}, u32[]{:S(2)}) copy-start(f32[2,32,256]{2,1,0:T(8,128)} %refs_10_.1) | copy-start | bytes 196612
  147.0 35.9 %copy-start.20 = (f32[2,64,47]{1,0,2:T(2,128)S(1)}, f32[2,64,47]{1,0,2:T(2,128)}, u32[]{:S(2)}) copy-start(f32[2,64,47]{1,0,2:T(2,128)} %param.38) | copy-start | bytes 72196
  147.0 35.9 %copy-start.21 = (f32[2,64,47]{1,0,2:T(2,128)S(1)}, f32[2,64,47]{1,0,2:T(2,128)}, u32[]{:S(2)}) copy-start(f32[2,64,47]{1,0,2:T(2,128)} %param.43) | copy-start | bytes 72196
  147.0 35.9 %copy-start.27 = (f32[2,64]{1,0:T(2,128)S(1)}, f32[2,64]{1,0:T(2,128)}, u32[]{:S(2)}) copy-start(f32[2,64]{1,0:T(2,128)} %refs_3_.1) | copy-start | bytes 1540
  147.0 35.9 %copy-start.32 = (f32[2,64]{1,0:T(2,128)S(1)}, f32[2,64]{1,0:T(2,128)}, u32[]{:S(2)}) copy-start(f32[2,64]{1,0:T(2,128)} %refs_8_.1) | copy-start | bytes 1540
  147.0 35.9 %copy-start.33 = (f32[2,64]{1,0:T(2,128)S(1)}, f32[2,64]{1,0:T(2,128)}, u32[]{:S(2)}) copy-start(f32[2,64]{1,0:T(2,128)} %refs_13_.1) | copy-start | bytes 1540
  147.0 35.9 %copy-start.34 = (f32[47]{0:T(128)S(1)}, f32[47]{0:T(128)}, u32[]{:S(2)}) copy-start(f32[47]{0:T(128)} %param.40) | copy-start | bytes 568
  147.0 35.9 %copy-start.35 = (f32[47]{0:T(128)S(1)}, f32[47]{0:T(128)}, u32[]{:S(2)}) copy-start(f32[47]{0:T(128)} %param.45) | copy-start | bytes 568
  177.8 2.1 %collective-permute-start.7 = (f32[8,128]{1,0:T(8,128)S(1)}, f32[8,128]{1,0:T(8,128)S(1)}, u32[]{:S(2)}, u32[]{:S(2)}) collective-permute-start(f32[8,128]{1,0:T(8,128)S(1)} %squares.1.s0), channel_id=1, source_target_pairs={{0,1},{1,0},{2,3},{3,2},{4,5},{5,4},{6,7},{7,6},{8,9},{9,8},{10,11... | collective-permute-start | bytes 12296 | tf_op jit(solution)/shard_map/ppermute | solution.py:548
  177.8 3.1 %collective-permute-start.6 = (f32[8,128]{1,0:T(8,128)S(1)}, f32[8,128]{1,0:T(8,128)S(1)}, u32[]{:S(2)}, u32[]{:S(2)}) collective-permute-start(f32[8,128]{1,0:T(8,128)S(1)} %squares.1.s0), channel_id=1, source_target_pairs={{0,3},{1,2},{2,1},{3,0},{4,7},{5,6},{6,5},{7,4},{8,11},{9,10},{10,... | collective-permute-start | bytes 12296 | tf_op jit(solution)/shard_map/ppermute | solution.py:548
  179.2 3.6 %collective-permute-start.5 = (f32[8,128]{1,0:T(8,128)S(1)}, f32[8,128]{1,0:T(8,128)S(1)}, u32[]{:S(2)}, u32[]{:S(2)}) collective-permute-start(f32[8,128]{1,0:T(8,128)S(1)} %squares.1.s0), channel_id=1, source_target_pairs={{0,2},{1,3},{2,0},{3,1},{4,6},{5,7},{6,4},{7,5},{8,10},{9,11},{10,... | collective-permute-start | bytes 12296 | tf_op jit(solution)/shard_map/ppermute | solution.py:548
  (14 other events, 9.9 us)

commit v2 on v1

v2 whole, which is shorter than its diff:
```python
import functools

import jax
import jax.numpy as jnp
from jax import lax
from jax.experimental import pallas as pl
from jax.experimental.pallas import tpu as pltpu
from jax.sharding import Mesh
from jax.sharding import PartitionSpec as P

STEP = 5
F32 = jnp.float32
BF16 = jnp.bfloat16
I32 = jnp.int32
LANES = 128
CLASS_ROWS = 48
LAST_ROWS = 64
ROW_HIDDEN = 48
ROW_LAST = 49
LANE_LOSS = 47
MIB = 1 << 20


def dims(left, right):
    return (((left,), (right,)), ((), ()))


NN, NT = dims(1, 0), dims(1, 1)


def dot(left, right, form):
    return lax.dot_general(left, right, form, preferred_element_type=F32)


def halves(value):
    high = value.astype(BF16)
    return high, (value - high.astype(F32)).astype(BF16)


def dot_split(left, right, form):
    (lh, ll), (rh, rl) = left, right
    return dot(lh, rh, form) + dot(lh, rl, form) + dot(ll, rh, form)


def dot_full(left, right, form):
    return dot_split(halves(left), halves(right), form)


def sigmoid(value):
    return 1.0 / (1.0 + jnp.exp(-value))


VMEM = pl.BlockSpec(memory_space=pltpu.VMEM)
HBM = pl.BlockSpec(memory_space=pltpu.HBM)


AXES = ("zh", "rl", "y", "c")


def call(body, outs, name, vmem, scratch=(), where=VMEM, us=1.0):
    def placed(*refs):
        body([lax.axis_index(a) for a in AXES], *refs)

    def run(*args):
        return pl.pallas_call(
            placed,
            out_shape=[jax.ShapeDtypeStruct(s, d) for s, d in outs],
            in_specs=[where] * len(args),
            out_specs=[VMEM] * len(outs),
            scratch_shapes=list(scratch),
            name=name,
            compiler_params=pltpu.CompilerParams(vmem_limit_bytes=vmem * MIB),
            cost_estimate=pl.CostEstimate(flops=0, bytes_accessed=int(us * 3.6e6), transcendentals=0),
        )(*args)

    return run


def fetch(sources, targets, sems):
    copies = [pltpu.make_async_copy(s, t, sems.at[i]) for i, (s, t) in enumerate(zip(sources, targets))]
    for copy in copies:
        copy.start()
    for copy in copies:
        copy.wait()


def like(*arrays):
    return [pltpu.VMEM(a.shape, a.dtype) for a in arrays] + [pltpu.SemaphoreType.DMA((len(arrays),))]


class Sizes:
    def __init__(self, mesh, features, neigh_first, neigh_mid, neigh_last):
        self.ranks = mesh.shape["zh"] * mesh.shape["rl"]
        self.rl = mesh.shape["rl"]
        self.s1, self.t1 = features.shape[1], neigh_first.shape[1]
        self.t2, self.t3 = neigh_mid.shape[1], neigh_last.shape[1]
        self.f1, self.f2, self.f3 = neigh_first.shape[2], neigh_mid.shape[2], neigh_last.shape[2]
        l1, l2, l3 = self.t1 // LANES, self.t2 // LANES, self.t3 // LANES
        self.l1, self.l2, self.l3 = l1, l2, l3
        self.at_first = 0
        self.at_mid = self.at_first + self.f1 * l1
        self.at_last = self.at_mid + self.f2 * l2
        self.at_label = self.at_last + self.f3 * l3
        self.at_c1 = self.at_label + 2 * l3
        self.at_c2 = self.at_c1 + l1
        self.at_c3 = self.at_c2 + l2
        self.id_rows = -(-(self.at_c3 + l3) // 32) * 32
        self.id_part = self.id_rows // 4
        self.blocks = 2 * self.rl
        self.pieces = 4 * self.rl
        self.nf, self.nm, self.nl = 64 // self.pieces, 128 // self.pieces, LAST_ROWS // self.pieces
        self.half_rows = 4 * (self.nf + self.nm)
        self.sum_rows = 2 * self.half_rows + 4 * self.nl
        self.ag_rows = -(-(2 * (self.nf + self.nm) + self.nl + 1) // 8) * 8
        self.keep_first = self.blocks * self.t1 * self.s1 * 2 <= 8 * MIB


def prep_body(z, pos, *refs):
    ids, f0, f1, wmsg, rows = refs[12:17]
    nf, cf, nm, cm, nl, cl, labels, feats, wf, wm, wl, bh = refs[17:29]
    fetch(refs[:12], refs[17:29], refs[29])

    def put(mb, at, value):
        for j in range(value.shape[1] // LANES):
            rows[mb, at + j : at + j + 1, :] = value[:, j * LANES : (j + 1) * LANES]

    for mb in range(2):
        for fan, nb, cnt, at, at_c in (
            (z.f1, nf, cf, z.at_first, z.at_c1),
            (z.f2, nm, cm, z.at_mid, z.at_c2),
            (z.f3, nl, cl, z.at_last, z.at_c3),
        ):
            count = cnt[mb : mb + 1, :]
            lanes = count.shape[1] // LANES
            for k in range(fan):
                put(mb, at + k * lanes, jnp.where(count > k, nb[k, mb : mb + 1, :], -1))
            put(mb, at_c, count)
        for other in range(2):
            put(mb, z.at_label + other * z.l3, labels[other : other + 1, :])
        end = z.at_c3 + z.l3
        if end < z.id_rows:
            rows[mb, end:, :] = jnp.zeros((z.id_rows - end, LANES), I32)
    part = pl.ds(pl.multiple_of((2 * pos[2] + pos[3]) * z.id_part, 8), z.id_part)
    for mb in range(2):
        mine = rows[mb, part]
        for s in range(4):
            for lead in range(z.rl):
                ids[(2 * s + mb) * z.rl + lead] = mine
    y = pos[2]
    f0[...] = feats[y]
    f1[...] = feats[1 - y]
    for j in range(2):
        wmsg[32 * j : 32 * j + 32, :] = wf[j]
        wmsg[64 + 64 * j : 128 + 64 * j, :] = wm[j]
    wmsg[192:248, :] = jnp.zeros((56, 256), F32)
    for j in range(2):
        wmsg[192 : 192 + 47, 64 * j : 64 * j + 64] = wl[:, j, :]
        wmsg[240:241, 64 * j : 64 * j + 64] = bh[j : j + 1, :]


def weights_body(pos, own, acr, dia, cor, blast, after, w1h, w1l, w2h, w2l, wmh, wml, wlt, wlc, bias, wall, f32a, f32b):
    s = 2 * pos[2] + pos[3]
    for at, part in ((s, own), (s ^ 2, acr), (s ^ 3, dia), (s ^ 1, cor)):
        wall[at] = part[...]
    for s in range(4):
        for j in range(2):
            f32a[128 * j + 32 * s : 128 * j + 32 * s + 32, :] = wall[s, 32 * j : 32 * j + 32, :]
            f32b[256 * j + 64 * s : 256 * j + 64 * s + 64, :] = wall[s, 64 + 64 * j : 128 + 64 * j, :]
            wlt[j, :, 64 * s : 64 * s + 64] = wall[s, 192 : 192 + CLASS_ROWS, 64 * j : 64 * j + 64]
    w1h[...], w1l[...] = halves(f32a[...].T)
    w2h[...], w2l[...] = halves(f32b[...].T)
    for j in range(2):
        wmh[j], wml[j] = halves(f32b[256 * j : 256 * j + 256, :])
        wlc[j] = jnp.concatenate([wlt[j], jnp.zeros((128 - CLASS_ROWS, 256), F32)], axis=0).T
    rows = [jnp.concatenate([wall[s, 240:241, 64 * j : 64 * j + 64] for s in range(4)], axis=1) for j in range(2)]
    last = jnp.concatenate([blast[...], jnp.zeros((1, 256 - 47), F32)], axis=1)
    packed = jnp.concatenate(rows + [last, jnp.zeros((125, 256), F32)], axis=0)
    bias[...] = packed.T


PIECE = 256


def all_rows(z, ids, row, zs):
    first = (row // z.id_part * 2 + zs) * z.rl
    return ids[first : first + z.rl, row % z.id_part, :]


def distinct(z, ids, at, fan, lanes, size, base, local, times):
    for zs in range(2):
        for j in range(lanes):
            rows = [all_rows(z, ids, at + k * lanes + j, zs) for k in range(fan)]
            count = [jnp.ones(rows[0].shape, F32) for _ in range(fan)]
            seen = [None] * fan
            for a in range(fan):
                for b in range(a + 1, fan):
                    same = rows[a] == rows[b]
                    count[a] = count[a] + jnp.where(same, 1.0, 0.0)
                    seen[b] = same if seen[b] is None else jnp.logical_or(seen[b], same)
            for k in range(fan):
                times[zs * lanes + j, k] = count[k]
                rel = rows[k] - base
                for g in range(size // PIECE):
                    inside = jnp.logical_and(rel >= g * PIECE, rel < (g + 1) * PIECE)
                    if seen[k] is not None:
                        inside = jnp.logical_and(inside, jnp.logical_not(seen[k]))
                    local[zs * lanes + j, g * fan + k] = jnp.where(inside, rel - g * PIECE, -1).astype(F32)


def adjacency_block(z, zs, lead, fan, lanes, size, local, times, at, out, column):
    for j in range(lanes):
        row = pl.ds(lead, 1)
        many = [jnp.broadcast_to(times[zs * lanes + j, k, row], (PIECE, LANES)).astype(BF16) for k in range(fan)]
        for g in range(size // PIECE):
            total = jnp.zeros((PIECE, LANES), BF16)
            for k in range(fan):
                name = jnp.broadcast_to(local[zs * lanes + j, g * fan + k, row], (PIECE, LANES)).astype(BF16)
                total = jnp.where(at == name, many[k], total)
            out[g * PIECE : (g + 1) * PIECE, column(j)] = total


def numbers():
    return lax.broadcasted_iota(I32, (PIECE, LANES), 0).astype(F32).astype(BF16)


def tables(z, fan, lanes, size):
    return [
        pltpu.VMEM((2 * lanes, size // PIECE * fan, z.rl, LANES), F32),
        pltpu.VMEM((2 * lanes, fan, z.rl, LANES), F32),
    ]


def adjacency_all(z, ids, first, fan, lanes, size, base, local, times, out):
    distinct(z, ids, first, fan, lanes, size, base, local, times)
    at = numbers()
    for zs in range(2):

        def block(lead, carry):
            def column(j):
                return pl.ds(pl.multiple_of(((zs * z.rl + lead) * lanes + j) * LANES, LANES), LANES)

            adjacency_block(z, zs, lead, fan, lanes, size, local, times, at, out, column)
            return carry

        lax.fori_loop(0, z.rl, block, 0)


def adjacency_first_body(z, pos, ids, a1, local, times):
    me = pos[2] * z.rl + pos[1]
    adjacency_all(z, ids, z.at_first, z.f1, z.l1, z.s1, me * z.s1, local, times, a1)


def class_weights(z, ids):
    classes = lax.broadcasted_iota(I32, (CLASS_ROWS, LANES), 0)
    total = jnp.zeros((CLASS_ROWS, LANES), F32)
    for zs in range(2):
        for other in range(2 * z.l3):
            rows = all_rows(z, ids, z.at_label + other, zs)
            for lead in range(z.rl):
                total = total + jnp.where(classes == rows[lead : lead + 1], 1.0, 0.0)
    counts = jnp.sum(total, axis=1, keepdims=True)
    weight = 1.0 / jnp.maximum(counts, 1.0)
    return weight, jnp.sum(counts * weight, axis=0, keepdims=True)


def adjacency_body(z, pos, ids, a2, a3, small, local2, times2, local3, times3):
    me = pos[2] * z.rl + pos[1]
    for q in range(4):
        small[q * z.id_part : (q + 1) * z.id_part] = ids[2 * q * z.rl + me].astype(F32)
    adjacency_all(z, ids, z.at_mid, z.f2, z.l2, z.t1, me * z.t1, local2, times2, a2)
    adjacency_all(z, ids, z.at_last, z.f3, z.l3, z.t2, me * z.t2, local3, times3, a3)
    weight, total = class_weights(z, ids)
    n = z.id_rows
    small[n : n + CLASS_ROWS] = jnp.broadcast_to(weight, (CLASS_ROWS, LANES))
    small[n + CLASS_ROWS :] = jnp.broadcast_to(total, (8, LANES))


def columns(pos, got0, got1, lanes):
    swap = pos[0] == 1
    a, b = got0[:, :lanes], got1[:, :lanes]
    return jnp.where(swap, b, a), jnp.where(swap, a, b)


def first_table(z, pos, got0, got1, table):
    width = 2 * got0.shape[0]
    rows = jnp.concatenate(columns(pos, got0, got1, z.s1), axis=0)
    table[:width], table[width:] = halves(rows)


def first_kept_body(z, pos, a1, got0, got1, after, out, table):
    first_table(z, pos, got0, got1, table)
    for r in range(z.blocks):
        both = dot(table[...], a1[:, r * z.t1 : (r + 1) * z.t1], NN)
        out[r] = both[: both.shape[0] // 2] + both[both.shape[0] // 2 :]


def first_body(z, pos, ids, got0, got1, after, out, table, adj, local, times):
    me = pos[2] * z.rl + pos[1]
    first_table(z, pos, got0, got1, table)
    width = 2 * got0.shape[0]
    at = numbers()
    distinct(z, ids, z.at_first, z.f1, z.l1, z.s1, me * z.s1, local, times)
    for zs in range(2):

        def block(lead, carry):
            def column(j):
                return slice(j * LANES, (j + 1) * LANES)

            adjacency_block(z, zs, lead, z.f1, z.l1, z.s1, local, times, at, adj, column)
            both = dot(table[...], adj[...], NN)
            out[zs * z.rl + lead] = both[:width] + both[width:]
            return carry

        lax.fori_loop(0, z.rl, block, 0)


def inverse(z, mine, at, lanes):
    row = jnp.concatenate([mine[at + j : at + j + 1, :] for j in range(lanes)], axis=1)
    return 1.0 / row


def sum_first_body(z, pos, mine, part, got0, got1, out):
    half = got0.shape[0]
    out[:half], out[half : 2 * half] = columns(pos, got0, got1, z.t1)
    total = part[0]
    for r in range(1, 2 * z.rl):
        total = total + part[r]
    out[2 * half :] = total * inverse(z, mine, z.at_c1, z.l1)


def put_columns(pos, own, other, out):
    c = pos[3]
    for j in range(2):
        for y in range(2):
            at = 128 * j + 64 * y
            out[pl.ds(pl.multiple_of(at + 32 * c, 32), 32)] = own[64 * j + 32 * y : 64 * j + 32 * y + 32]
            out[pl.ds(pl.multiple_of(at + 32 * (1 - c), 32), 32)] = other[64 * j + 32 * y : 64 * j + 32 * y + 32]


def hidden_one_body(z, pos, own, other, w1h, w1l, bias, a2, out, x1, h1, slope):
    c = pos[3]
    put_columns(pos, own, other, x1)
    pre = dot_split((w1h[...], w1l[...]), halves(x1[...]), NN) + bias[:, 0:1]
    sigma = sigmoid(pre)
    h1[...] = pre * sigma
    slope[...] = sigma * (1.0 + pre * (1.0 - sigma))
    table = jnp.concatenate(halves(h1[pl.ds(pl.multiple_of(c * 128, 128), 128)]), axis=0)
    for r in range(2 * z.rl):
        both = dot(table, a2[:, r * z.t2 : (r + 1) * z.t2], NN)
        out[r] = both[:128] + both[128:]


def sum_mid_body(z, pos, mine, part, out):
    total = part[0]
    for r in range(1, 2 * z.rl):
        total = total + part[r]
    out[...] = total * inverse(z, mine, z.at_c2, z.l2)


def hidden_two_body(z, pos, own, other, h1, w2h, w2l, bias, wlt, a3, out, y2, h2, slope, local):
    c = pos[3]
    y2[:256] = h1[:, : z.t2]
    y2[pl.ds(pl.multiple_of(256 + c * 128, 128), 128)] = own[...]
    y2[pl.ds(pl.multiple_of(256 + (1 - c) * 128, 128), 128)] = other[...]
    pre = dot_split((w2h[...], w2l[...]), halves(y2[...]), NN) + bias[:, 1:2]
    sigma = sigmoid(pre)
    hidden = pre * sigma
    h2[...] = hidden
    slope[...] = sigma * (1.0 + pre * (1.0 - sigma))
    split = halves(hidden)
    local[...] = dot_split(halves(wlt[0]), (split[0][:, : z.t3], split[1][:, : z.t3]), NN)
    for_mean = dot_split(halves(wlt[1]), split, NN)
    table = jnp.concatenate(halves(for_mean), axis=0)
    for r in range(z.blocks):
        both = dot(table, a3[:, r * z.t3 : (r + 1) * z.t3], NN)
        out[r] = both[:CLASS_ROWS] + both[CLASS_ROWS:]


def logits_body(z, pos, mine, part, local, bias, out, grad, loss):
    total = part[0]
    for r in range(1, 2 * z.rl):
        total = total + part[r]
    recip = inverse(z, mine, z.at_c3, z.l3)
    logits = total * recip + local[...] + bias[:CLASS_ROWS, 2:3]
    classes = lax.broadcasted_iota(I32, logits.shape, 0)
    logits = jnp.where(classes < 47, logits, -jnp.inf)
    label = jnp.where(
        pos[0] == 0,
        mine[z.at_label : z.at_label + 1, :],
        mine[z.at_label + z.l3 : z.at_label + z.l3 + 1, :],
    ).astype(I32)
    onehot = jnp.where(classes == label, 1.0, 0.0)
    top = jnp.max(logits, axis=0, keepdims=True)
    powers = jnp.exp(logits - top)
    norm = jnp.sum(powers, axis=0, keepdims=True)
    weight = jnp.sum(onehot * mine[z.id_rows : z.id_rows + CLASS_ROWS], axis=0, keepdims=True)
    target = jnp.sum(jnp.where(classes == label, logits, 0.0), axis=0, keepdims=True)
    each = weight * (jnp.log(norm) + top - target)
    loss[...] = jnp.broadcast_to(jnp.sum(each, axis=1, keepdims=True), loss.shape)
    dlogits = weight * (powers / norm - onehot) / mine[z.id_rows + CLASS_ROWS : z.id_rows + CLASS_ROWS + 1, :]
    grad[...] = dlogits
    scaled = dlogits * recip
    for r in range(2 * z.rl):
        out[r] = scaled


def back_last_body(z, pos, mine, gall, grad, a3, wlc, h2, slope, out, dpre2, dwl):
    both = None
    for r in range(2 * z.rl):
        table = jnp.concatenate(halves(gall[r]), axis=0)
        term = dot(table, a3[:, r * z.t3 : (r + 1) * z.t3], NT)
        both = term if both is None else both + term
    back_last(z, pos, mine, both[:CLASS_ROWS] + both[CLASS_ROWS:], grad, wlc, h2, slope, out, dpre2, dwl)


def back_last(z, pos, mine, spread, grad, wlc, h2, slope, out, dpre2, dwl):
    c = pos[3]
    dh = dot_full(wlc[1][:, :CLASS_ROWS], spread, NN)
    own = dot_full(wlc[0][:, :CLASS_ROWS], grad[...], NN)
    dh = dh + jnp.concatenate([own, jnp.zeros((256, z.t2 - z.t3), F32)], axis=1)
    dpre2[...] = dh * slope[...]
    scaled = dpre2[pl.ds(pl.multiple_of(c * 128, 128), 128)] * inverse(z, mine, z.at_c2, z.l2)
    for r in range(2 * z.rl):
        out[r] = scaled
    dwl[0] = dot_full(grad[...], h2[:, : z.t3], NT)
    dwl[1] = dot_full(spread, h2[...], NT)


def back_mid_body(z, pos, gall, a2, out):
    both = None
    for r in range(2 * z.rl):
        table = jnp.concatenate(halves(gall[r]), axis=0)
        term = dot(table, a2[:, r * z.t2 : (r + 1) * z.t2], NT)
        both = term if both is None else both + term
    out[...] = both[:128] + both[128:]


def row_sums(value):
    ones = jnp.ones((8, value.shape[1]), BF16)
    high, low = halves(value)
    return dot(ones, high, NT) + dot(ones, low, NT)


def grads_body(z, pos, own, other, dpre2, wmh, wml, slope, x1, y2, dwl, grad, loss, out, spread, first, mid, last):
    c = pos[3]
    mine = pl.ds(pl.multiple_of(c * 128, 128), 128)
    spread[mine] = own[...]
    spread[pl.ds(pl.multiple_of((1 - c) * 128, 128), 128)] = other[...]
    dh = dot_split((wmh[1, mine, :], wml[1, mine, :]), halves(spread[...]), NN)
    at_own = dot_split((wmh[0, mine, :], wml[0, mine, :]), halves(dpre2[...]), NN)
    dh = dh + jnp.concatenate([at_own, jnp.zeros((128, z.t1 - z.t2), F32)], axis=1)
    dpre1 = dh * slope[mine]
    half2 = dpre2[mine]
    first[...] = dot_full(x1[...], dpre1, NT)
    mid[...] = dot_full(y2[...], half2, NT)
    b1, b2, b3 = row_sums(dpre1), row_sums(half2), row_sums(grad[...])
    last[...] = jnp.zeros_like(last)
    core0 = jnp.where(c == 0, 1.0, 0.0)
    for s in range(4):
        last[s, :CLASS_ROWS, :64] = dwl[0][:, 64 * s : 64 * s + 64] * core0
        last[s, :CLASS_ROWS, 64:] = dwl[1][:, 64 * s : 64 * s + 64] * (1.0 - core0)
        here = jnp.where(c == s // 2, 1.0, 0.0)
        at = 64 * (s % 2)
        last[s, ROW_HIDDEN : ROW_HIDDEN + 1, :64] = b1[0:1, at : at + 64] * here
        last[s, ROW_HIDDEN : ROW_HIDDEN + 1, 64:] = b2[0:1, at : at + 64] * here
        last[s, ROW_LAST : ROW_LAST + 1, :LANE_LOSS] = b3[0:1, :LANE_LOSS] * core0
        last[s, ROW_LAST : ROW_LAST + 1, LANE_LOSS : LANE_LOSS + 1] = loss[0:1, 0:1] * core0
    n = 4 * (z.nf + z.nm)
    for p in range(z.pieces):
        for s in range(4):
            e = z.nf * p
            at = 128 * (e // 32) + 32 * s + e % 32
            out[p, s * z.nf : (s + 1) * z.nf] = first[at : at + z.nf]
            e = z.nm * p
            at = 256 * (e // 64) + 64 * s + e % 64
            out[p, 4 * z.nf + s * z.nm : 4 * z.nf + (s + 1) * z.nm] = mid[at : at + z.nm]
            out[p, n + s * z.nl : n + (s + 1) * z.nl] = last[s, z.nl * p : z.nl * (p + 1)]


def sum_grads_body(z, pos, part, out):
    n = z.half_rows
    even, odd = part[0], part[1]
    for d in range(2, z.pieces, 2):
        even = even + part[d]
        odd = odd + part[d + 1]
    out[:n] = even[:n]
    out[n : 2 * n] = odd[:n]
    out[2 * n :] = even[n:] + odd[n:]


def share_body(z, pos, own, other, out):
    n, nf, nm, nl = z.half_rows, z.nf, z.nm, z.nl
    total = own[...] + other[...]
    piece = 4 * pos[1] + 2 * pos[2] + pos[3]
    lane = lax.broadcasted_iota(I32, (1, LANES), 1)
    squares = jnp.sum(total[: 2 * n] * total[: 2 * n], axis=0, keepdims=True)
    for s in range(4):
        for i in range(nl):
            row = total[2 * n + s * nl + i : 2 * n + s * nl + i + 1]
            at = piece * nl + i
            squares = squares + jnp.where(at <= ROW_HIDDEN, 1.0, 0.0) * row * row
            if s == 0:
                squares = squares + jnp.where(at == ROW_LAST, 1.0, 0.0) * jnp.where(lane < 47, row * row, 0.0)
    squares = jnp.broadcast_to(jnp.sum(squares, axis=1, keepdims=True), (1, LANES))
    pad = z.ag_rows - 2 * (nf + nm) - nl - 1
    for s in range(4):
        rows = []
        for h in range(2):
            rows.append(total[h * n + s * nf : h * n + (s + 1) * nf])
            rows.append(total[h * n + 4 * nf + s * nm : h * n + 4 * nf + (s + 1) * nm])
        rows += [total[2 * n + s * nl : 2 * n + (s + 1) * nl], squares]
        if pad:
            rows.append(jnp.zeros((pad, LANES), F32))
        rows = jnp.concatenate(rows, axis=0)
        for lead in range(z.rl):
            out[4 * lead + s] = rows


def update_body(z, pos, whole, mine, *refs):
    w, m, v = refs[0:5], refs[5:10], refs[10:15]
    new, moment, square = refs[15:20], refs[20:25], refs[25:30]
    loss, weight_sum, norm = refs[30:33]
    nf, nm, nl = z.nf, z.nm, z.nl
    at = 2 * (nf + nm) + nl
    total = whole[0, at : at + 1, 0:1]
    for p in range(1, z.pieces):
        total = total + whole[p, at : at + 1, 0:1]
    root = jnp.sqrt(total)
    scale = jnp.minimum(1.0, 0.01 / root)
    norm[...] = root
    weight_sum[...] = mine[z.id_rows + CLASS_ROWS : z.id_rows + CLASS_ROWS + 1, 0:1]

    def adamw(weight, grad, first, second):
        grad = grad * scale
        mo = 0.9 * first + 0.1 * grad
        sq = 0.999 * second + 0.001 * grad * grad
        corrected = mo / (1.0 - 0.9**STEP)
        rt = jnp.sqrt(sq / (1.0 - 0.999**STEP))
        return (weight - 0.05 * (corrected / (rt + 1e-08) + 0.01 * weight), mo, sq)

    def put(i, at, grad):
        outs = adamw(w[i][at], grad, m[i][at], v[i][at])
        new[i][at], moment[i][at], square[i][at] = outs

    h = nf + nm
    for p in range(z.pieces):
        e = nf * p
        g = jnp.concatenate([whole[p, :nf], whole[p, h : h + nf]], axis=1)
        put(0, (e // 32, slice(e % 32, e % 32 + nf), slice(None)), g)
        e = nm * p
        g = jnp.concatenate([whole[p, nf:h], whole[p, h + nf : 2 * h]], axis=1)
        put(1, (e // 64, slice(e % 64, e % 64 + nm), slice(None)), g)
        a = nl * p
        b = min(a + nl, 47)
        if a < b:
            for j in range(2):
                put(2, (slice(a, b), j, slice(None)), whole[p, 2 * h : 2 * h + b - a, 64 * j : 64 * j + 64])
        for i in range(nl):
            row = whole[p, 2 * h + i : 2 * h + i + 1]
            if a + i == ROW_HIDDEN:
                for j in range(2):
                    put(3, (slice(j, j + 1), slice(None)), row[:, 64 * j : 64 * j + 64])
            elif a + i == ROW_LAST:
                put(4, (slice(None), slice(None)), row[:, :47])
                loss[...] = row[:, LANE_LOSS : LANE_LOSS + 1]


def on_device(
    mesh, features, neigh_first, count_first, neigh_mid, count_mid, neigh_last, count_last, labels,
    w_first, w_mid, w_last, b_hidden, b_last,
    m_first, m_mid, m_last, m_hidden, m_bias,
    v_first, v_mid, v_last, v_hidden, v_bias,
):
    z = Sizes(mesh, features, neigh_first, neigh_mid, neigh_last)
    bind = functools.partial
    blocks = z.blocks

    def flip(value):
        return lax.ppermute(value, "c", [(0, 1), (1, 0)])

    def exchange(value):
        return lax.all_to_all(value, ("y", "rl"), 0, 0)

    def swapped(value):
        return jnp.transpose(value, (2, 0, 1))

    raw = (
        swapped(neigh_first), count_first, swapped(neigh_mid), count_mid, swapped(neigh_last), count_last, labels,
        jnp.transpose(features, (0, 2, 1)), w_first, w_mid, swapped(w_last), b_hidden,
    )
    ids, f0, f1, wmsg = call(
        bind(prep_body, z),
        [((4 * z.ranks, z.id_part, LANES), I32), ((32, z.s1), F32), ((32, z.s1), F32), ((248, 256), F32)],
        "prep", 58, scratch=[pltpu.VMEM((2, z.id_rows, LANES), I32), *like(*raw)], where=HBM, us=2.0,
    )(*raw)
    got0, got1 = (
        lax.ppermute(f, ("zh", "y"), [(2 * zh + y, 2 * (y ^ j) + zh) for zh in range(2) for y in range(2)])
        for j, f in enumerate((f0, f1))
    )
    across = lax.ppermute(wmsg, "y", [(0, 1), (1, 0)])
    walls = (wmsg, across, flip(across), flip(wmsg))
    ids = lax.all_to_all(ids, ("y", "c", "zh", "rl"), 0, 0)
    a2, a3, mine = call(
        bind(adjacency_body, z),
        [
            ((z.t1, blocks * z.t2), BF16), ((z.t2, blocks * z.t3), BF16),
            ((z.id_rows + CLASS_ROWS + 8, LANES), F32),
        ],
        "adjacency", 8, us=4.0, scratch=tables(z, z.f2, z.l2, z.t1) + tables(z, z.f3, z.l3, z.t2),
    )(ids)
    w1h, w1l, w2h, w2l, wmh, wml, wlt, wlc, bias = call(
        weights_body,
        [
            ((256, 256), BF16), ((256, 256), BF16), ((256, 512), BF16), ((256, 512), BF16),
            ((2, 256, 256), BF16), ((2, 256, 256), BF16),
            ((2, CLASS_ROWS, 256), F32), ((2, 256, 128), F32), ((256, 128), F32),
        ],
        "weights", 8,
        scratch=[pltpu.VMEM((4, 248, 256), F32), pltpu.VMEM((256, 256), F32), pltpu.VMEM((512, 256), F32)],
    )(*walls, b_last[None], mine)
    table = pltpu.VMEM((128, z.s1), BF16)
    sums = [((blocks, 64, z.t1), F32)]
    if z.keep_first:
        a1 = call(
            bind(adjacency_first_body, z), [((z.s1, blocks * z.t1), BF16)], "adjacency_first", 4, us=6.0,
            scratch=tables(z, z.f1, z.l1, z.s1),
        )(ids)[0]
        part = call(bind(first_kept_body, z), sums, "first", 4, us=3.0, scratch=[table])(a1, got0, got1, bias)[0]
    else:
        part = call(
            bind(first_body, z), sums, "first", 16, us=8.0,
            scratch=[table, pltpu.VMEM((z.s1, z.t1), BF16), *tables(z, z.f1, z.l1, z.s1)],
        )(ids, got0, got1, bias)[0]
    part = exchange(part)
    half = call(bind(sum_first_body, z), [((128, z.t1), F32)], "sum_first", 8)(mine, part, got0, got1)[0]
    other = flip(half)
    part, x1, h1, slope1 = call(
        bind(hidden_one_body, z),
        [((blocks, 128, z.t2), F32), ((256, z.t1), F32), ((256, z.t1), F32), ((256, z.t1), F32)],
        "hidden_one", 16,
    )(half, other, w1h, w1l, bias, a2)
    part = exchange(part)
    half = call(bind(sum_mid_body, z), [((128, z.t2), F32)], "sum_mid", 8)(mine, part)[0]
    other = flip(half)
    part, y2, h2, slope2, local = call(
        bind(hidden_two_body, z),
        [
            ((blocks, CLASS_ROWS, z.t3), F32),
            ((512, z.t2), F32), ((256, z.t2), F32), ((256, z.t2), F32), ((CLASS_ROWS, z.t3), F32),
        ],
        "hidden_two", 12,
    )(half, other, h1, w2h, w2l, bias, wlt, a3)
    part = exchange(part)
    backs = [((blocks, 128, z.t2), F32), ((256, z.t2), F32), ((2, CLASS_ROWS, 256), F32)]
    ends = [((CLASS_ROWS, z.t3), F32), ((8, LANES), F32)]
    part, grad, loss = call(bind(logits_body, z), [((blocks, CLASS_ROWS, z.t3), F32), *ends], "logits", 8)(
        mine, part, local, bias
    )
    part = exchange(part)
    part, dpre2, dwl = call(bind(back_last_body, z), backs, "back_last", 12, us=1.5)(
        mine, part, grad, a3, wlc, h2, slope2
    )
    part = exchange(part)
    half = call(bind(back_mid_body, z), [((128, z.t1), F32)], "back_mid", 12)(part, a2)[0]
    other = flip(half)
    part = call(
        bind(grads_body, z), [((z.pieces, 4 * (z.nf + z.nm + z.nl), LANES), F32)], "grads", 12,
        scratch=[
            pltpu.VMEM((256, z.t1), F32), pltpu.VMEM((256, 128), F32), pltpu.VMEM((512, 128), F32),
            pltpu.VMEM((4, LAST_ROWS, LANES), F32),
        ],
    )(half, other, dpre2, wmh, wml, slope1, x1, y2, dwl, grad, loss)[0]
    part = lax.all_to_all(part, ("rl", "y", "c"), 0, 0)
    own = call(bind(sum_grads_body, z), [((z.sum_rows, LANES), F32)], "sum_grads", 8)(part)[0]
    other = lax.ppermute(own, "zh", [(0, 1), (1, 0)])
    part = call(bind(share_body, z), [((z.pieces, z.ag_rows, LANES), F32)], "share", 8)(own, other)[0]
    whole = lax.all_to_all(part, ("rl", "y", "c"), 0, 0)

    params = (w_first, w_mid, swapped(w_last), b_hidden, b_last[None])
    firsts = (m_first, m_mid, swapped(m_last), m_hidden, m_bias[None])
    seconds = (v_first, v_mid, swapped(v_last), v_hidden, v_bias[None])
    shapes = [(p.shape, F32) for p in params]
    state = (*params, *firsts, *seconds)
    outs = call(
        bind(update_body, z), shapes * 3 + [((1, 1), F32)] * 3, "update", 8
    )(whole, mine, *state)
    results = []
    for g in range(3):
        a, b, c, d, e = outs[5 * g : 5 * g + 5]
        results += [a, b, jnp.transpose(c, (1, 2, 0)), d, e[0]]
    return tuple(results) + tuple(o[0, 0] for o in outs[15:])


def solution(mesh):
    rows, cols = mesh.shape["rows"], mesh.shape["cols"]
    fine = Mesh(mesh.devices.reshape(2, rows // 2, 2, cols // 2), ("zh", "rl", "y", "c"))
    r, c = ("zh", "rl"), ("y", "c")
    weights = (P(None, c, None),) * 3 + (P(None, c), P())
    nodes = (P(None, r, None), P(None, r))
    placed = (P(None, r, c),) + nodes * 3 + (P(None, r),) + weights * 3
    return jax.shard_map(
        functools.partial(on_device, fine),
        mesh=fine,
        in_specs=placed,
        out_specs=weights * 3 + (P(), P(), P()),
        check_vma=False,
    )
```

time: 186 us -> 151 us (0.81)
  Pallas kernels: 39.1 us -> 19.8 us
  local copies, waits for them, and re-layouts: 13.6 us -> 0.1 us
  waiting for transfers between devices: 19.1 us -> 16.7 us
  blocking collectives: 93.1 us -> 95.4 us
    pallas_call x15 -> x16, Pallas kernels: 39.1 us -> 19.8 us  [run(): pl.pallas_call(placed, out_shape=[jax.ShapeDtypeStruct(s, d) for s, d in...]
    all_to_all x4 -> x5, blocking collectives: 53.3 us -> 71.9 us  [exchange(): return lax.all_to_all(value, ('y', 'rl'), 0, 0)]
    unnamed x72 -> x32, local copies, waits for them, and re-layouts: 13.6 us -> 0.1 us
    all_gather x1 -> x0, blocking collectives: 10.3 us -> none  [on_device(): wall = lax.all_gather(wmsg, ('y', 'c'), axis=0)]
    all_to_all x2 -> x1, waiting for transfers between devices: 9.84 us -> 0.01 us  [on_device(): ids = lax.all_to_all(ids, ('y', 'c', 'zh', 'rl'), 0, 0)]
    ppermute x3 -> x2, waiting for transfers between devices: 2.81 us -> 12.3 us  [the longest x1 9.36 us: on_device(): across = lax.ppermute(wmsg, 'y', [(0, 1), (1, 0)])]
    all_to_all x2, blocking collectives: 29.5 us -> 23.5 us  [the longest x1 13.2 us: on_device(): part = lax.all_to_all(part, ('rl', 'y', 'c'), 0, 0)]
    all_to_all x2 -> x1, starting transfers between devices: 12.9 us -> 7.3 us  [on_device(): ids = lax.all_to_all(ids, ('y', 'c', 'zh', 'rl'), 0, 0)]
  transfers between devices with their start and end apart: 10 -> 10, of which waited for: 7 -> 5; matrix products, arithmetic and copies ran while one was open for 0% -> 0% of each run, Pallas kernels for 5% -> 6%
where the time goes in v2:
time: 151 us
  blocking collectives  95.4 us (63%)
  Pallas kernels  19.8 us (13%)
  starting transfers between devices  17.6 us (12%)
  waiting for transfers between devices  16.7 us (11%)
    all_to_all x5, blocking collectives, exchange(): return lax.all_to_all(value, ('y', 'rl'), 0, 0)  71.9 us
    pallas_call x16, Pallas kernels, run(): pl.pallas_call(placed, out_shape=[jax.ShapeDtypeStruct(s, d) for s, d in...  19.8 us
    all_to_all x1, blocking collectives, on_device(): part = lax.all_to_all(part, ('rl', 'y', 'c'), 0, 0)  13.2 us
    all_to_all x1, blocking collectives, on_device(): whole = lax.all_to_all(part, ('rl', 'y', 'c'), 0, 0)  10.3 us
    ppermute x1, waiting for transfers between devices, on_device(): across = lax.ppermute(wmsg, 'y', [(0, 1), (1, 0)])  9.36 us
    all_to_all x1, starting transfers between devices, on_device(): ids = lax.all_to_all(ids, ('y', 'c', 'zh', 'rl'), 0, 0)  7.3 us
    ppermute x2, starting transfers between devices, on_device(): lax.ppermute(f, ('zh', 'y'), [(2 * zh + y, 2 * (y ^ j) + zh) for zh in ra...  5.46 us
    ppermute x5, waiting for transfers between devices, flip(): return lax.ppermute(value, 'c', [(0, 1), (1, 0)])  4.38 us
  transfers between devices with their start and end apart: 10, of which 5 were waited for; matrix products, arithmetic and copies ran while one was open for 0% of the time, Pallas kernels for 6%

profile of v2, /device:TPU:0, one launch (start us, length us, event | category | flops | bytes accessed | tf_op | source)
XLA Modules:
  0.0 150.6 jit_solution(8282579498936767969)
XLA Ops:
  0.7 2.2 %prep.1 = (s32[32,16,128]{2,1,0:T(8,128)}, f32[32,1024]{1,0:T(8,128)}, f32[32,1024]{1,0:T(8,128)}, f32[248,256]{1,0:T(8,128)}) custom-call(s32[5,2,512]{2,1,0:T(2,128)} %bitcast.28, s32[2,512]{1,0:T(2,128)} %refs_1_.1, s32[10,2,256]{2,1,0:T(2,128)} %bitcast.29, s32[2,256]{1,0:T(2,128)} %refs_3_.2, s32[15,2,128]{2,1,0:T(2,128)} %bitcast.30, ...), custom_call_target="tpu_custom_call" | custom-call | bytes 7200000 | tf_op jit(solution)/shard_map/prep/pallas_call | solution.py:65
  2.9 7.3 %all-to-all-start = ((s32[32,16,128]{2,1,0:T(8,128)}), s32[32,16,128]{2,1,0:T(8,128)S(1)}, u32[]{:S(2)}, u32[]{:S(2)}) async-start(s32[32,16,128]{2,1,0:T(8,128)} %get-tuple-element.67), calls=%async_computation | async-start | bytes 524288 | tf_op jit(solution)/shard_map/all_to_all | solution.py:602
  10.2 1.8 %collective-permute-start.2 = (f32[248,256]{1,0:T(8,128)}, f32[248,256]{1,0:T(8,128)S(1)}, u32[]{:S(2)}, u32[]{:S(2)}) collective-permute-start(f32[248,256]{1,0:T(8,128)} %get-tuple-element.71.refs_0_), channel_id=1, source_target_pairs={{0,2},{2,0},{1,3},{3,1},{4,6},{6,4},{5,7},{7,5},{8,10},{10,8},{9,1... | collective-permute-start | bytes 761864 | tf_op jit(solution)/shard_map/ppermute | solution.py:600
  12.0 9.4 %collective-permute-done.2.refs_1_ = f32[248,256]{1,0:T(8,128)S(1)} collective-permute-done((f32[248,256]{1,0:T(8,128)}, f32[248,256]{1,0:T(8,128)S(1)}, u32[]{:S(2)}, u32[]{:S(2)}) %collective-permute-start.2) | collective-permute-done | bytes 253984 | tf_op jit(solution)/shard_map/ppermute | solution.py:600
  21.4 1.6 %collective-permute-start = (f32[32,1024]{1,0:T(8,128)}, f32[32,1024]{1,0:T(8,128)S(1)}, u32[]{:S(2)}, u32[]{:S(2)}) collective-permute-start(f32[32,1024]{1,0:T(8,128)} %get-tuple-element.69), channel_id=1, source_target_pairs={{0,0},{2,16},{16,2},{18,18},{1,1},{3,17},{17,3},{19,19},{4,4},{6,2... | collective-permute-start | bytes 393224 | tf_op jit(solution)/shard_map/ppermute | solution.py:597
  22.9 3.9 %collective-permute-start.1 = (f32[32,1024]{1,0:T(8,128)}, f32[32,1024]{1,0:T(8,128)S(1)}, u32[]{:S(2)}, u32[]{:S(2)}) collective-permute-start(f32[32,1024]{1,0:T(8,128)} %get-tuple-element.70), channel_id=1, source_target_pairs={{0,16},{2,0},{16,18},{18,2},{1,17},{3,1},{17,19},{19,3},{4,20},{6,... | collective-permute-start | bytes 393224 | tf_op jit(solution)/shard_map/ppermute | solution.py:597
  26.8 4.0 %adjacency.1 = (bf16[512,2048]{1,0:T(8,128)(2,1)S(1)}, bf16[256,1024]{1,0:T(8,128)(2,1)S(1)}, f32[120,128]{1,0:T(8,128)S(1)}) custom-call(s32[32,16,128]{2,1,0:T(8,128)S(1)} %all-to-all-done.refs_0_), custom_call_target="tpu_custom_call" | custom-call | bytes 14400000 | tf_op jit(solution)/shard_map/adjacency/pallas_call | solution.py:65
  30.9 4.5 %adjacency_first.1.refs_0_ = bf16[1024,4096]{1,0:T(8,128)(2,1)S(1)} custom-call(s32[32,16,128]{2,1,0:T(8,128)S(1)} %all-to-all-done.refs_0_), custom_call_target="tpu_custom_call" | custom-call | bytes 21600000 | tf_op jit(solution)/shard_map/adjacency_first/pallas_call | solution.py:65
  35.5 0.5 weights.1
  36.0 1.3 first.1
  37.3 19.0 %all_to_all.40.refs_1_ = f32[8,64,512]{2,1,0:T(8,128)S(1)} all-to-all(f32[8,64,512]{2,1,0:T(8,128)S(1)} %first.1), channel_id=1, replica_groups=mesh['zh'=2,'rl'=4,'y'=2,'c'=2] {'y','rl'}, dimensions={0} | all-to-all | bytes 2097152 | tf_op jit(solution)/shard_map/all_to_all | solution.py:582
  56.3 0.1 collective-permute-start.5
  56.4 1.5 %collective-permute-done.5.refs_1_ = f32[128,512]{1,0:T(8,128)S(1)} collective-permute-done((f32[128,512]{1,0:T(8,128)S(1)}, f32[128,512]{1,0:T(8,128)S(1)}, u32[]{:S(2)}, u32[]{:S(2)}) %collective-permute-start.5) | collective-permute-done | bytes 262176 | tf_op jit(solution)/shard_map/ppermute | solution.py:579
  57.9 1.3 hidden_one.1
  59.2 18.4 %all_to_all.41.refs_1_ = f32[8,128,256]{2,1,0:T(8,128)S(1)} all-to-all(f32[8,128,256]{2,1,0:T(8,128)S(1)} %get-tuple-element.76), channel_id=1, replica_groups=mesh['zh'=2,'rl'=4,'y'=2,'c'=2] {'y','rl'}, dimensions={0} | all-to-all | bytes 2097152 | tf_op jit(solution)/shard_map/all_to_all | solution.py:582
  77.9 1.3 collective-permute-done.6.refs_1_
  79.2 1.2 hidden_two.1
  80.4 9.3 %all_to_all.42.refs_1_ = f32[8,48,128]{2,1,0:T(8,128)S(1)} all-to-all(f32[8,48,128]{2,1,0:T(8,128)S(1)} %get-tuple-element.82), channel_id=1, replica_groups=mesh['zh'=2,'rl'=4,'y'=2,'c'=2] {'y','rl'}, dimensions={0} | all-to-all | bytes 393216 | tf_op jit(solution)/shard_map/all_to_all | solution.py:582
  89.7 0.2 logits.1
  89.9 9.0 %all_to_all.43.refs_1_ = f32[8,48,128]{2,1,0:T(8,128)S(1)} all-to-all(f32[8,48,128]{2,1,0:T(8,128)S(1)} %get-tuple-element.84), channel_id=1, replica_groups=mesh['zh'=2,'rl'=4,'y'=2,'c'=2] {'y','rl'}, dimensions={0} | all-to-all | bytes 393216 | tf_op jit(solution)/shard_map/all_to_all | solution.py:582
  98.9 1.0 back_last.1
  99.9 16.3 %all_to_all.44.refs_0_ = f32[8,128,256]{2,1,0:T(8,128)S(1)} all-to-all(f32[8,128,256]{2,1,0:T(8,128)S(1)} %get-tuple-element.89), channel_id=1, replica_groups=mesh['zh'=2,'rl'=4,'y'=2,'c'=2] {'y','rl'}, dimensions={0} | all-to-all | bytes 2097152 | tf_op jit(solution)/shard_map/all_to_all | solution.py:582
  116.2 0.7 back_mid.1.refs_0_
  116.9 0.1 collective-permute-start.7
  117.0 1.5 %collective-permute-done.7.refs_1_ = f32[128,512]{1,0:T(8,128)S(1)} collective-permute-done((f32[128,512]{1,0:T(8,128)S(1)}, f32[128,512]{1,0:T(8,128)S(1)}, u32[]{:S(2)}, u32[]{:S(2)}) %collective-permute-start.7) | collective-permute-done | bytes 262176 | tf_op jit(solution)/shard_map/ppermute | solution.py:579
  118.5 1.2 grads.1
  119.7 13.2 %all_to_all.45.refs_0_ = f32[16,64,128]{2,1,0:T(8,128)S(1)} all-to-all(f32[16,64,128]{2,1,0:T(8,128)S(1)} %grads.1), channel_id=1, replica_groups=mesh['zh'=2,'rl'=4,'y'=2,'c'=2] {'rl','y','c'}, dimensions={0} | all-to-all | bytes 1048576 | tf_op jit(solution)/shard_map/all_to_all | solution.py:673
  132.9 2.8 %collective-permute-start.8 = (f32[112,128]{1,0:T(8,128)S(1)}, f32[112,128]{1,0:T(8,128)S(1)}, u32[]{:S(2)}, u32[]{:S(2)}) collective-permute-start(f32[112,128]{1,0:T(8,128)S(1)} %sum_grads.1.refs_0_), channel_id=1, source_target_pairs={{0,16},{16,0},{1,17},{17,1},{2,18},{18,2},{3,19},{19,3},{4,20},{20... | collective-permute-start | bytes 172040 | tf_op jit(solution)/shard_map/ppermute | solution.py:675
  135.7 2.9 %collective-permute-done.8.refs_1_ = f32[112,128]{1,0:T(8,128)S(1)} collective-permute-done((f32[112,128]{1,0:T(8,128)S(1)}, f32[112,128]{1,0:T(8,128)S(1)}, u32[]{:S(2)}, u32[]{:S(2)}) %collective-permute-start.8) | collective-permute-done | bytes 57376 | tf_op jit(solution)/shard_map/ppermute | solution.py:675
  138.6 0.1 share.1
  138.7 10.3 %all_to_all.46.refs_0_ = f32[16,32,128]{2,1,0:T(8,128)S(1)} all-to-all(f32[16,32,128]{2,1,0:T(8,128)S(1)} %share.1), channel_id=1, replica_groups=mesh['zh'=2,'rl'=4,'y'=2,'c'=2] {'rl','y','c'}, dimensions={0} | all-to-all | bytes 524288 | tf_op jit(solution)/shard_map/all_to_all | solution.py:677
  149.2 1.4 update.1
  (43 shorter events, 0.3 us)
Async XLA Ops:
  0.7 34.8 %copy-start.11 = (f32[47]{0:T(128)S(1)}, f32[47]{0:T(128)}, u32[]{:S(2)}) copy-start(f32[47]{0:T(128)} %param.35) | copy-start | bytes 568
  2.9 32.6 %copy-start.2 = (f32[248,256]{1,0:T(8,128)S(1)}, f32[248,256]{1,0:T(8,128)}, u32[]{:S(2)}) copy-start(f32[248,256]{1,0:T(8,128)} %get-tuple-element.71.refs_0_) | copy-start | bytes 761860
  2.9 24.0 %all-to-all-start = ((s32[32,16,128]{2,1,0:T(8,128)}), s32[32,16,128]{2,1,0:T(8,128)S(1)}, u32[]{:S(2)}, u32[]{:S(2)}) async-start(s32[32,16,128]{2,1,0:T(8,128)} %get-tuple-element.67), calls=%async_computation | async-start | bytes 524288 | tf_op jit(solution)/shard_map/all_to_all | solution.py:602
  10.2 11.2 %collective-permute-start.2 = (f32[248,256]{1,0:T(8,128)}, f32[248,256]{1,0:T(8,128)S(1)}, u32[]{:S(2)}, u32[]{:S(2)}) collective-permute-start(f32[248,256]{1,0:T(8,128)} %get-tuple-element.71.refs_0_), channel_id=1, source_target_pairs={{0,2},{2,0},{1,3},{3,1},{4,6},{6,4},{5,7},{7,5},{8,10},{10,8},{9,1... | collective-permute-start | bytes 761864 | tf_op jit(solution)/shard_map/ppermute | solution.py:600
  12.0 23.4 %collective-permute-start.4 = (f32[248,256]{1,0:T(8,128)}, f32[248,256]{1,0:T(8,128)S(1)}, u32[]{:S(2)}, u32[]{:S(2)}) collective-permute-start(f32[248,256]{1,0:T(8,128)} %get-tuple-element.71.refs_0_), channel_id=1, source_target_pairs={{0,1},{1,0},{2,3},{3,2},{4,5},{5,4},{6,7},{7,6},{8,9},{9,8},{10,11... | collective-permute-start | bytes 761864 | tf_op jit(solution)/shard_map/ppermute | solution.py:579
  21.4 14.1 %collective-permute-start.3 = (f32[248,256]{1,0:T(8,128)S(1)}, f32[248,256]{1,0:T(8,128)S(1)}, u32[]{:S(2)}, u32[]{:S(2)}) collective-permute-start(f32[248,256]{1,0:T(8,128)S(1)} %collective-permute-done.2.refs_1_), channel_id=1, source_target_pairs={{0,1},{1,0},{2,3},{3,2},{4,5},{5,4},{6,7},{7,6},{8,9},{9,8},{10,11... | collective-permute-start | bytes 761864 | tf_op jit(solution)/shard_map/ppermute | solution.py:579
  21.4 14.6 %collective-permute-start = (f32[32,1024]{1,0:T(8,128)}, f32[32,1024]{1,0:T(8,128)S(1)}, u32[]{:S(2)}, u32[]{:S(2)}) collective-permute-start(f32[32,1024]{1,0:T(8,128)} %get-tuple-element.69), channel_id=1, source_target_pairs={{0,0},{2,16},{16,2},{18,18},{1,1},{3,17},{17,3},{19,19},{4,4},{6,2... | collective-permute-start | bytes 393224 | tf_op jit(solution)/shard_map/ppermute | solution.py:597
  22.9 13.1 %collective-permute-start.1 = (f32[32,1024]{1,0:T(8,128)}, f32[32,1024]{1,0:T(8,128)S(1)}, u32[]{:S(2)}, u32[]{:S(2)}) collective-permute-start(f32[32,1024]{1,0:T(8,128)} %get-tuple-element.70), channel_id=1, source_target_pairs={{0,16},{2,0},{16,18},{18,2},{1,17},{3,1},{17,19},{19,3},{4,20},{6,... | collective-permute-start | bytes 393224 | tf_op jit(solution)/shard_map/ppermute | solution.py:597
  56.3 1.6 %collective-permute-start.5 = (f32[128,512]{1,0:T(8,128)S(1)}, f32[128,512]{1,0:T(8,128)S(1)}, u32[]{:S(2)}, u32[]{:S(2)}) collective-permute-start(f32[128,512]{1,0:T(8,128)S(1)} %sum_first.1.refs_0_), channel_id=1, source_target_pairs={{0,1},{1,0},{2,3},{3,2},{4,5},{5,4},{6,7},{7,6},{8,9},{9,8},{10,11... | collective-permute-start | bytes 786440 | tf_op jit(solution)/shard_map/ppermute | solution.py:579
  77.6 71.4 %copy-start = (f32[2,64,256]{2,1,0:T(8,128)S(1)}, f32[2,64,256]{2,1,0:T(8,128)}, u32[]{:S(2)}) copy-start(f32[2,64,256]{2,1,0:T(8,128)} %refs_3_.3) | copy-start | bytes 393220
  77.7 71.4 %copy-start.1 = (f32[2,32,256]{2,1,0:T(8,128)S(1)}, f32[2,32,256]{2,1,0:T(8,128)}, u32[]{:S(2)}) copy-start(f32[2,32,256]{2,1,0:T(8,128)} %refs_2_.1) | copy-start | bytes 196612
  77.7 71.4 %copy-start.3 = (f32[2,64,47]{1,0,2:T(2,128)S(1)}, f32[2,64,47]{1,0,2:T(2,128)}, u32[]{:S(2)}) copy-start(f32[2,64,47]{1,0,2:T(2,128)} %param.33) | copy-start | bytes 72196
  77.7 71.4 %copy-start.4 = (f32[2,64,256]{2,1,0:T(8,128)S(1)}, f32[2,64,256]{2,1,0:T(8,128)}, u32[]{:S(2)}) copy-start(f32[2,64,256]{2,1,0:T(8,128)} %refs_8_.3) | copy-start | bytes 393220
  77.7 71.4 %copy-start.5 = (f32[2,64,256]{2,1,0:T(8,128)S(1)}, f32[2,64,256]{2,1,0:T(8,128)}, u32[]{:S(2)}) copy-start(f32[2,64,256]{2,1,0:T(8,128)} %refs_13_.1) | copy-start | bytes 393220
  77.7 71.4 %copy-start.6 = (f32[2,32,256]{2,1,0:T(8,128)S(1)}, f32[2,32,256]{2,1,0:T(8,128)}, u32[]{:S(2)}) copy-start(f32[2,32,256]{2,1,0:T(8,128)} %refs_7_.1) | copy-start | bytes 196612
  77.7 71.4 %copy-start.7 = (f32[2,32,256]{2,1,0:T(8,128)S(1)}, f32[2,32,256]{2,1,0:T(8,128)}, u32[]{:S(2)}) copy-start(f32[2,32,256]{2,1,0:T(8,128)} %refs_12_.1) | copy-start | bytes 196612
  77.7 71.4 %copy-start.8 = (f32[2,64,47]{1,0,2:T(2,128)S(1)}, f32[2,64,47]{1,0,2:T(2,128)}, u32[]{:S(2)}) copy-start(f32[2,64,47]{1,0,2:T(2,128)} %param.38) | copy-start | bytes 72196
  77.7 71.4 %copy-start.9 = (f32[2,64,47]{1,0,2:T(2,128)S(1)}, f32[2,64,47]{1,0,2:T(2,128)}, u32[]{:S(2)}) copy-start(f32[2,64,47]{1,0,2:T(2,128)} %param.43) | copy-start | bytes 72196
  77.8 71.4 %copy-start.10 = (f32[2,64]{1,0:T(2,128)S(1)}, f32[2,64]{1,0:T(2,128)}, u32[]{:S(2)}) copy-start(f32[2,64]{1,0:T(2,128)} %refs_5_.3) | copy-start | bytes 1540
  77.8 71.4 %copy-start.12 = (f32[2,64]{1,0:T(2,128)S(1)}, f32[2,64]{1,0:T(2,128)}, u32[]{:S(2)}) copy-start(f32[2,64]{1,0:T(2,128)} %refs_10_.1) | copy-start | bytes 1540
  77.8 71.4 %copy-start.13 = (f32[2,64]{1,0:T(2,128)S(1)}, f32[2,64]{1,0:T(2,128)}, u32[]{:S(2)}) copy-start(f32[2,64]{1,0:T(2,128)} %refs_15_.1) | copy-start | bytes 1540
  77.8 71.4 %copy-start.14 = (f32[47]{0:T(128)S(1)}, f32[47]{0:T(128)}, u32[]{:S(2)}) copy-start(f32[47]{0:T(128)} %param.40) | copy-start | bytes 568
  77.8 71.4 %copy-start.15 = (f32[47]{0:T(128)S(1)}, f32[47]{0:T(128)}, u32[]{:S(2)}) copy-start(f32[47]{0:T(128)} %param.45) | copy-start | bytes 568
  77.8 1.4 collective-permute-start.6
  116.9 1.6 %collective-permute-start.7 = (f32[128,512]{1,0:T(8,128)S(1)}, f32[128,512]{1,0:T(8,128)S(1)}, u32[]{:S(2)}, u32[]{:S(2)}) collective-permute-start(f32[128,512]{1,0:T(8,128)S(1)} %back_mid.1.refs_0_), channel_id=1, source_target_pairs={{0,1},{1,0},{2,3},{3,2},{4,5},{5,4},{6,7},{7,6},{8,9},{9,8},{10,11... | collective-permute-start | bytes 786440 | tf_op jit(solution)/shard_map/ppermute | solution.py:579
  132.9 5.7 %collective-permute-start.8 = (f32[112,128]{1,0:T(8,128)S(1)}, f32[112,128]{1,0:T(8,128)S(1)}, u32[]{:S(2)}, u32[]{:S(2)}) collective-permute-start(f32[112,128]{1,0:T(8,128)S(1)} %sum_grads.1.refs_0_), channel_id=1, source_target_pairs={{0,16},{16,0},{1,17},{17,1},{2,18},{18,2},{3,19},{19,3},{4,20},{20... | collective-permute-start | bytes 172040 | tf_op jit(solution)/shard_map/ppermute | solution.py:675

commit v3 on v2

--- a/solution.py
+++ b/solution.py
@@ -158,6 +158,10 @@
         wmsg[240:241, 64 * j : 64 * j + 64] = bh[j : j + 1, :]
 
 
+def held_body(pos, value, after, out):
+    out[...] = value[...]
+
+
 def weights_body(pos, own, acr, dia, cor, blast, after, w1h, w1l, w2h, w2l, wmh, wml, wlt, wlc, bias, wall, f32a, f32b):
     s = 2 * pos[2] + pos[3]
     for at, part in ((s, own), (s ^ 2, acr), (s ^ 3, dia), (s ^ 1, cor)):
@@ -245,9 +249,26 @@
         lax.fori_loop(0, z.rl, block, 0)
 
 
-def adjacency_first_body(z, pos, ids, a1, local, times):
+def adjacency_first_body(z, pos, ids, after0, after1, a1, small, local, times):
     me = pos[2] * z.rl + pos[1]
-    adjacency_all(z, ids, z.at_first, z.f1, z.l1, z.s1, me * z.s1, local, times, a1)
+    for q in range(4):
+        small[q * z.id_part : (q + 1) * z.id_part] = ids[2 * q * z.rl + me].astype(F32)
+    weight, total = class_weights(z, ids)
+    n = z.id_rows
+    small[n : n + CLASS_ROWS] = jnp.broadcast_to(weight, (CLASS_ROWS, LANES))
+    small[n + CLASS_ROWS :] = jnp.broadcast_to(total, (8, LANES))
+    if z.keep_first:
+        adjacency_all(z, ids, z.at_first, z.f1, z.l1, z.s1, me * z.s1, local, times, a1)
+
+
+def adjacency_mid_body(z, pos, ids, after, a2, local, times):
+    me = pos[2] * z.rl + pos[1]
+    adjacency_all(z, ids, z.at_mid, z.f2, z.l2, z.t1, me * z.t1, local, times, a2)
+
+
+def adjacency_last_body(z, pos, ids, after, a3, local, times):
+    me = pos[2] * z.rl + pos[1]
+    adjacency_all(z, ids, z.at_last, z.f3, z.l3, z.t2, me * z.t2, local, times, a3)
 
 
 def class_weights(z, ids):
@@ -261,18 +282,6 @@
     counts = jnp.sum(total, axis=1, keepdims=True)
     weight = 1.0 / jnp.maximum(counts, 1.0)
     return weight, jnp.sum(counts * weight, axis=0, keepdims=True)
-
-
-def adjacency_body(z, pos, ids, a2, a3, small, local2, times2, local3, times3):
-    me = pos[2] * z.rl + pos[1]
-    for q in range(4):
-        small[q * z.id_part : (q + 1) * z.id_part] = ids[2 * q * z.rl + me].astype(F32)
-    adjacency_all(z, ids, z.at_mid, z.f2, z.l2, z.t1, me * z.t1, local2, times2, a2)
-    adjacency_all(z, ids, z.at_last, z.f3, z.l3, z.t2, me * z.t2, local3, times3, a3)
-    weight, total = class_weights(z, ids)
-    n = z.id_rows
-    small[n : n + CLASS_ROWS] = jnp.broadcast_to(weight, (CLASS_ROWS, LANES))
-    small[n + CLASS_ROWS :] = jnp.broadcast_to(total, (8, LANES))
 
 
 def columns(pos, got0, got1, lanes):
@@ -404,49 +413,40 @@
         out[r] = scaled
 
 
-def back_last_body(z, pos, mine, gall, grad, a3, wlc, h2, slope, out, dpre2, dwl):
+def back_last_body(z, pos, mine, gall, grad, a3, wlc, h2, slope, wmh, wml, out, dpre2, dwl):
     both = None
     for r in range(2 * z.rl):
         table = jnp.concatenate(halves(gall[r]), axis=0)
         term = dot(table, a3[:, r * z.t3 : (r + 1) * z.t3], NT)
         both = term if both is None else both + term
-    back_last(z, pos, mine, both[:CLASS_ROWS] + both[CLASS_ROWS:], grad, wlc, h2, slope, out, dpre2, dwl)
-
-
-def back_last(z, pos, mine, spread, grad, wlc, h2, slope, out, dpre2, dwl):
-    c = pos[3]
+    spread = both[:CLASS_ROWS] + both[CLASS_ROWS:]
     dh = dot_full(wlc[1][:, :CLASS_ROWS], spread, NN)
     own = dot_full(wlc[0][:, :CLASS_ROWS], grad[...], NN)
     dh = dh + jnp.concatenate([own, jnp.zeros((256, z.t2 - z.t3), F32)], axis=1)
     dpre2[...] = dh * slope[...]
-    scaled = dpre2[pl.ds(pl.multiple_of(c * 128, 128), 128)] * inverse(z, mine, z.at_c2, z.l2)
+    rows = pl.ds(pl.multiple_of(pos[3] * 128, 128), 128)
+    scaled = dot_split((wmh[1, rows, :], wml[1, rows, :]), halves(dpre2[...]), NN) * inverse(z, mine, z.at_c2, z.l2)
     for r in range(2 * z.rl):
         out[r] = scaled
     dwl[0] = dot_full(grad[...], h2[:, : z.t3], NT)
     dwl[1] = dot_full(spread, h2[...], NT)
 
 
-def back_mid_body(z, pos, gall, a2, out):
-    both = None
-    for r in range(2 * z.rl):
-        table = jnp.concatenate(halves(gall[r]), axis=0)
-        term = dot(table, a2[:, r * z.t2 : (r + 1) * z.t2], NT)
-        both = term if both is None else both + term
-    out[...] = both[:128] + both[128:]
-
-
 def row_sums(value):
     ones = jnp.ones((8, value.shape[1]), BF16)
     high, low = halves(value)
     return dot(ones, high, NT) + dot(ones, low, NT)
 
 
-def grads_body(z, pos, own, other, dpre2, wmh, wml, slope, x1, y2, dwl, grad, loss, out, spread, first, mid, last):
+def grads_body(z, pos, gall, a2, dpre2, wmh, wml, slope, x1, y2, dwl, grad, loss, out, first, mid, last):
     c = pos[3]
     mine = pl.ds(pl.multiple_of(c * 128, 128), 128)
-    spread[mine] = own[...]
-    spread[pl.ds(pl.multiple_of((1 - c) * 128, 128), 128)] = other[...]
-    dh = dot_split((wmh[1, mine, :], wml[1, mine, :]), halves(spread[...]), NN)
+    both = None
+    for r in range(z.blocks):
+        table = jnp.concatenate(halves(gall[r]), axis=0)
+        term = dot(table, a2[:, r * z.t2 : (r + 1) * z.t2], NT)
+        both = term if both is None else both + term
+    dh = both[:128] + both[128:]
     at_own = dot_split((wmh[0, mine, :], wml[0, mine, :]), halves(dpre2[...]), NN)
     dh = dh + jnp.concatenate([at_own, jnp.zeros((128, z.t1 - z.t2), F32)], axis=1)
     dpre1 = dh * slope[mine]
@@ -597,17 +597,27 @@
         lax.ppermute(f, ("zh", "y"), [(2 * zh + y, 2 * (y ^ j) + zh) for zh in range(2) for y in range(2)])
         for j, f in enumerate((f0, f1))
     )
-    across = lax.ppermute(wmsg, "y", [(0, 1), (1, 0)])
-    walls = (wmsg, across, flip(across), flip(wmsg))
     ids = lax.all_to_all(ids, ("y", "c", "zh", "rl"), 0, 0)
-    a2, a3, mine = call(
-        bind(adjacency_body, z),
-        [
-            ((z.t1, blocks * z.t2), BF16), ((z.t2, blocks * z.t3), BF16),
-            ((z.id_rows + CLASS_ROWS + 8, LANES), F32),
-        ],
-        "adjacency", 8, us=4.0, scratch=tables(z, z.f2, z.l2, z.t1) + tables(z, z.f3, z.l3, z.t2),
-    )(ids)
+    table = pltpu.VMEM((128, z.s1), BF16)
+    sums = [((blocks, 64, z.t1), F32)]
+    small = ((z.id_rows + CLASS_ROWS + 8, LANES), F32)
+    a1, mine = call(
+        bind(adjacency_first_body, z), [((z.s1, blocks * z.t1) if z.keep_first else (8, LANES), BF16), small],
+        "adjacency_first", 4, us=6.0, scratch=tables(z, z.f1, z.l1, z.s1),
+    )(ids, got0, got1)
+    w_across = lax.ppermute(wmsg, "y", [(0, 1), (1, 0)])
+    w_across = call(held_body, [((248, 256), F32)], "held", 4)(w_across, mine)[0]
+    if z.keep_first:
+        part = call(bind(first_kept_body, z), sums, "first", 4, us=3.0, scratch=[table])(a1, got0, got1, w_across)[0]
+    else:
+        part = call(
+            bind(first_body, z), sums, "first", 16, us=8.0,
+            scratch=[table, pltpu.VMEM((z.s1, z.t1), BF16), *tables(z, z.f1, z.l1, z.s1)],
+        )(ids, got0, got1, w_across)[0]
+    part = exchange(part)
+    half = call(bind(sum_first_body, z), [((128, z.t1), F32)], "sum_first", 8)(mine, part, got0, got1)[0]
+    other = flip(half)
+    walls = (wmsg, w_across, flip(w_across), flip(wmsg))
     w1h, w1l, w2h, w2l, wmh, wml, wlt, wlc, bias = call(
         weights_body,
         [
@@ -617,23 +627,11 @@
         ],
         "weights", 8,
         scratch=[pltpu.VMEM((4, 248, 256), F32), pltpu.VMEM((256, 256), F32), pltpu.VMEM((512, 256), F32)],
-    )(*walls, b_last[None], mine)
-    table = pltpu.VMEM((128, z.s1), BF16)
-    sums = [((blocks, 64, z.t1), F32)]
-    if z.keep_first:
-        a1 = call(
-            bind(adjacency_first_body, z), [((z.s1, blocks * z.t1), BF16)], "adjacency_first", 4, us=6.0,
-            scratch=tables(z, z.f1, z.l1, z.s1),
-        )(ids)[0]
-        part = call(bind(first_kept_body, z), sums, "first", 4, us=3.0, scratch=[table])(a1, got0, got1, bias)[0]
-    else:
-        part = call(
-            bind(first_body, z), sums, "first", 16, us=8.0,
-            scratch=[table, pltpu.VMEM((z.s1, z.t1), BF16), *tables(z, z.f1, z.l1, z.s1)],
-        )(ids, got0, got1, bias)[0]
-    part = exchange(part)
-    half = call(bind(sum_first_body, z), [((128, z.t1), F32)], "sum_first", 8)(mine, part, got0, got1)[0]
-    other = flip(half)
+    )(*walls, b_last[None], half)
+    a2 = call(
+        bind(adjacency_mid_body, z), [((z.t1, blocks * z.t2), BF16)], "adjacency_mid", 4, us=3.0,
+        scratch=tables(z, z.f2, z.l2, z.t1),
+    )(ids, half)[0]
     part, x1, h1, slope1 = call(
         bind(hidden_one_body, z),
         [((blocks, 128, z.t2), F32), ((256, z.t1), F32), ((256, z.t1), F32), ((256, z.t1), F32)],
@@ -642,6 +640,10 @@
     part = exchange(part)
     half = call(bind(sum_mid_body, z), [((128, z.t2), F32)], "sum_mid", 8)(mine, part)[0]
     other = flip(half)
+    a3 = call(
+        bind(adjacency_last_body, z), [((z.t2, blocks * z.t3), BF16)], "adjacency_last", 4, us=1.0,
+        scratch=tables(z, z.f3, z.l3, z.t2),
+    )(ids, half)[0]
     part, y2, h2, slope2, local = call(
         bind(hidden_two_body, z),
         [
@@ -658,18 +660,16 @@
     )
     part = exchange(part)
     part, dpre2, dwl = call(bind(back_last_body, z), backs, "back_last", 12, us=1.5)(
-        mine, part, grad, a3, wlc, h2, slope2
+        mine, part, grad, a3, wlc, h2, slope2, wmh, wml
     )
     part = exchange(part)
-    half = call(bind(back_mid_body, z), [((128, z.t1), F32)], "back_mid", 12)(part, a2)[0]
-    other = flip(half)
     part = call(
         bind(grads_body, z), [((z.pieces, 4 * (z.nf + z.nm + z.nl), LANES), F32)], "grads", 12,
         scratch=[
-            pltpu.VMEM((256, z.t1), F32), pltpu.VMEM((256, 128), F32), pltpu.VMEM((512, 128), F32),
+            pltpu.VMEM((256, 128), F32), pltpu.VMEM((512, 128), F32),
             pltpu.VMEM((4, LAST_ROWS, LANES), F32),
         ],
-    )(half, other, dpre2, wmh, wml, slope1, x1, y2, dwl, grad, loss)[0]
+    )(part, a2, dpre2, wmh, wml, slope1, x1, y2, dwl, grad, loss)[0]
     part = lax.all_to_all(part, ("rl", "y", "c"), 0, 0)
     own = call(bind(sum_grads_body, z), [((z.sum_rows, LANES), F32)], "sum_grads", 8)(part)[0]
     other = lax.ppermute(own, "zh", [(0, 1), (1, 0)])

time: 151 us -> 146 us (0.967)
  waiting for transfers between devices: 16.7 us -> 11.3 us
  blocking collectives: 95.4 us -> 97.1 us
    ppermute x1, waiting for transfers between devices: 9.36 us -> 0.01 us  [on_device(): w_across = lax.ppermute(wmsg, 'y', [(0, 1), (1, 0)])]
    ppermute x2, waiting for transfers between devices: 0.01 us -> 7.59 us  [on_device(): lax.ppermute(f, ('zh', 'y'), [(2 * zh + y, 2 * (y ^ j) + zh) for zh in ra...]
    ppermute x5 -> x4, waiting for transfers between devices: 4.38 us -> 0.01 us  [flip(): return lax.ppermute(value, 'c', [(0, 1), (1, 0)])]
    all_to_all x5, blocking collectives: 71.9 us -> 73.6 us  [exchange(): return lax.all_to_all(value, ('y', 'rl'), 0, 0)]
    pallas_call x16 -> x17, Pallas kernels: 19.8 us -> 19.5 us  [run(): pl.pallas_call(placed, out_shape=[jax.ShapeDtypeStruct(s, d) for s, d in...]
  transfers between devices with their start and end apart: 10 -> 9, of which waited for: 5 -> 2; matrix products, arithmetic and copies ran while one was open for 0% -> 0% of each run, Pallas kernels for 6% -> 6%
where the time goes in v3:
time: 146 us
  blocking collectives  97.1 us (67%)
  Pallas kernels  19.5 us (13%)
  starting transfers between devices  16.4 us (11%)
  waiting for transfers between devices  11.3 us (8%)
    all_to_all x5, blocking collectives, exchange(): return lax.all_to_all(value, ('y', 'rl'), 0, 0)  73.6 us
    pallas_call x17, Pallas kernels, run(): pl.pallas_call(placed, out_shape=[jax.ShapeDtypeStruct(s, d) for s, d in...  19.5 us
    all_to_all x1, blocking collectives, on_device(): part = lax.all_to_all(part, ('rl', 'y', 'c'), 0, 0)  13.2 us
    all_to_all x1, blocking collectives, on_device(): whole = lax.all_to_all(part, ('rl', 'y', 'c'), 0, 0)  10.3 us
    ppermute x2, waiting for transfers between devices, on_device(): lax.ppermute(f, ('zh', 'y'), [(2 * zh + y, 2 * (y ^ j) + zh) for zh in ra...  7.59 us
    all_to_all x1, starting transfers between devices, on_device(): ids = lax.all_to_all(ids, ('y', 'c', 'zh', 'rl'), 0, 0)  7.3 us
    ppermute x2, starting transfers between devices, on_device(): lax.ppermute(f, ('zh', 'y'), [(2 * zh + y, 2 * (y ^ j) + zh) for zh in ra...  4.57 us
    ppermute x1, waiting for transfers between devices, on_device(): other = lax.ppermute(own, 'zh', [(0, 1), (1, 0)])  3.72 us
  transfers between devices with their start and end apart: 9, of which 2 were waited for; matrix products, arithmetic and copies ran while one was open for 0% of the time, Pallas kernels for 6%

profile of v3, /device:TPU:0, one launch (start us, length us, event | category | flops | bytes accessed | tf_op | source)
XLA Modules:
  0.0 145.5 jit_solution(8998751470208417356)
XLA Ops:
  0.7 2.2 %prep.1 = (s32[32,16,128]{2,1,0:T(8,128)}, f32[32,1024]{1,0:T(8,128)}, f32[32,1024]{1,0:T(8,128)}, f32[248,256]{1,0:T(8,128)}) custom-call(s32[5,2,512]{2,1,0:T(2,128)} %bitcast.28, s32[2,512]{1,0:T(2,128)} %refs_1_.1, s32[10,2,256]{2,1,0:T(2,128)} %bitcast.29, s32[2,256]{1,0:T(2,128)} %refs_3_.2, s32[15,2,128]{2,1,0:T(2,128)} %bitcast.30, ...), custom_call_target="tpu_custom_call" | custom-call | bytes 7200000 | tf_op jit(solution)/shard_map/prep/pallas_call | solution.py:65
  2.9 7.3 %all-to-all-start = ((s32[32,16,128]{2,1,0:T(8,128)}), s32[32,16,128]{2,1,0:T(8,128)S(1)}, u32[]{:S(2)}, u32[]{:S(2)}) async-start(s32[32,16,128]{2,1,0:T(8,128)} %get-tuple-element.66), calls=%async_computation | async-start | bytes 524288 | tf_op jit(solution)/shard_map/all_to_all | solution.py:600
  10.2 1.8 %collective-permute-start.2 = (f32[248,256]{1,0:T(8,128)}, f32[248,256]{1,0:T(8,128)S(1)}, u32[]{:S(2)}, u32[]{:S(2)}) collective-permute-start(f32[248,256]{1,0:T(8,128)} %get-tuple-element.71.refs_0_), channel_id=1, source_target_pairs={{0,2},{2,0},{1,3},{3,1},{4,6},{6,4},{5,7},{7,5},{8,10},{10,8},{9,1... | collective-permute-start | bytes 761864 | tf_op jit(solution)/shard_map/ppermute | solution.py:608
  12.0 1.6 %collective-permute-start = (f32[32,1024]{1,0:T(8,128)}, f32[32,1024]{1,0:T(8,128)S(1)}, u32[]{:S(2)}, u32[]{:S(2)}) collective-permute-start(f32[32,1024]{1,0:T(8,128)} %get-tuple-element.67), channel_id=1, source_target_pairs={{0,0},{2,16},{16,2},{18,18},{1,1},{3,17},{17,3},{19,19},{4,4},{6,2... | collective-permute-start | bytes 393224 | tf_op jit(solution)/shard_map/ppermute | solution.py:597
  13.6 3.0 %collective-permute-start.1 = (f32[32,1024]{1,0:T(8,128)}, f32[32,1024]{1,0:T(8,128)S(1)}, u32[]{:S(2)}, u32[]{:S(2)}) collective-permute-start(f32[32,1024]{1,0:T(8,128)} %get-tuple-element.68), channel_id=1, source_target_pairs={{0,16},{2,0},{16,18},{18,2},{1,17},{3,1},{17,19},{19,3},{4,20},{6,... | collective-permute-start | bytes 393224 | tf_op jit(solution)/shard_map/ppermute | solution.py:597
  16.6 7.6 %collective-permute-done.1.refs_2_.refs_3_ = f32[32,1024]{1,0:T(8,128)S(1)} collective-permute-done((f32[32,1024]{1,0:T(8,128)}, f32[32,1024]{1,0:T(8,128)S(1)}, u32[]{:S(2)}, u32[]{:S(2)}) %collective-permute-start.1) | collective-permute-done | bytes 131104 | tf_op jit(solution)/shard_map/ppermute | solution.py:597
  24.2 4.6 %adjacency_first.1 = (bf16[1024,4096]{1,0:T(8,128)(2,1)S(1)}, f32[120,128]{1,0:T(8,128)S(1)}) custom-call(s32[32,16,128]{2,1,0:T(8,128)S(1)} %all-to-all-done.refs_0_, f32[32,1024]{1,0:T(8,128)S(1)} %collective-permute-done.refs_1_.refs_2_, f32[32,1024]{1,0:T(8,128)S(1)} %collective-permute-done.1.refs_2_.refs_3_), custom_call_target="tpu_custom_call" | custom-call | bytes 21600000 | tf_op jit(solution)/shard_map/adjacency_first/pallas_call | solution.py:65
  28.8 1.3 first.1
  30.1 19.6 %all_to_all.40.refs_1_ = f32[8,64,512]{2,1,0:T(8,128)S(1)} all-to-all(f32[8,64,512]{2,1,0:T(8,128)S(1)} %first.1), channel_id=1, replica_groups=mesh['zh'=2,'rl'=4,'y'=2,'c'=2] {'y','rl'}, dimensions={0} | all-to-all | bytes 2097152 | tf_op jit(solution)/shard_map/all_to_all | solution.py:582
  49.7 0.1 sum_first.1.refs_5_.refs_1_.refs_0_
  49.8 0.1 collective-permute-start.3
  49.9 0.5 collective-permute-start.5
  50.4 0.1 collective-permute-start.4
  50.5 2.5 %adjacency_mid.1.refs_5_.refs_1_ = bf16[512,2048]{1,0:T(8,128)(2,1)S(1)} custom-call(s32[32,16,128]{2,1,0:T(8,128)S(1)} %all-to-all-done.refs_0_, f32[128,512]{1,0:T(8,128)S(1)} %sum_first.1.refs_5_.refs_1_.refs_0_), custom_call_target="tpu_custom_call" | custom-call | bytes 10800000 | tf_op jit(solution)/shard_map/adjacency_mid/pallas_call | solution.py:65
  53.1 0.5 weights.1
  53.6 1.3 hidden_one.1
  54.8 18.7 %all_to_all.41.refs_1_ = f32[8,128,256]{2,1,0:T(8,128)S(1)} all-to-all(f32[8,128,256]{2,1,0:T(8,128)S(1)} %get-tuple-element.75), channel_id=1, replica_groups=mesh['zh'=2,'rl'=4,'y'=2,'c'=2] {'y','rl'}, dimensions={0} | all-to-all | bytes 2097152 | tf_op jit(solution)/shard_map/all_to_all | solution.py:582
  73.8 0.1 collective-permute-start.6
  73.9 1.4 adjacency_last.1.refs_7_.refs_3_
  75.3 1.2 hidden_two.1
  76.5 9.6 %all_to_all.42.refs_1_ = f32[8,48,128]{2,1,0:T(8,128)S(1)} all-to-all(f32[8,48,128]{2,1,0:T(8,128)S(1)} %get-tuple-element.80), channel_id=1, replica_groups=mesh['zh'=2,'rl'=4,'y'=2,'c'=2] {'y','rl'}, dimensions={0} | all-to-all | bytes 393216 | tf_op jit(solution)/shard_map/all_to_all | solution.py:582
  86.1 0.2 logits.1
  86.3 9.0 %all_to_all.43.refs_1_ = f32[8,48,128]{2,1,0:T(8,128)S(1)} all-to-all(f32[8,48,128]{2,1,0:T(8,128)S(1)} %get-tuple-element.82), channel_id=1, replica_groups=mesh['zh'=2,'rl'=4,'y'=2,'c'=2] {'y','rl'}, dimensions={0} | all-to-all | bytes 393216 | tf_op jit(solution)/shard_map/all_to_all | solution.py:582
  95.3 1.2 back_last.1
  96.5 16.7 %all_to_all.44.refs_0_ = f32[8,128,256]{2,1,0:T(8,128)S(1)} all-to-all(f32[8,128,256]{2,1,0:T(8,128)S(1)} %get-tuple-element.89), channel_id=1, replica_groups=mesh['zh'=2,'rl'=4,'y'=2,'c'=2] {'y','rl'}, dimensions={0} | all-to-all | bytes 2097152 | tf_op jit(solution)/shard_map/all_to_all | solution.py:582
  113.1 1.6 %grads.1 = f32[16,64,128]{2,1,0:T(8,128)S(1)} custom-call(f32[8,128,256]{2,1,0:T(8,128)S(1)} %all_to_all.44.refs_0_, bf16[512,2048]{1,0:T(8,128)(2,1)S(1)} %adjacency_mid.1.refs_5_.refs_1_, f32[256,256]{1,0:T(8,128)S(1)} %get-tuple-element.90.refs_2_, bf16[2,256,256]{2,1,0:T(8,128)(2,1)S(1)} %get-tuple-element.87.refs_7_.refs_3_, ...), custom_call_target="tpu_custom_call" | custom-call | bytes 3600000 | tf_op jit(solution)/shard_map/grads/pallas_call | solution.py:65
  114.7 13.2 %all_to_all.45.refs_0_ = f32[16,64,128]{2,1,0:T(8,128)S(1)} all-to-all(f32[16,64,128]{2,1,0:T(8,128)S(1)} %grads.1), channel_id=1, replica_groups=mesh['zh'=2,'rl'=4,'y'=2,'c'=2] {'rl','y','c'}, dimensions={0} | all-to-all | bytes 1048576 | tf_op jit(solution)/shard_map/all_to_all | solution.py:673
  127.9 2.0 %collective-permute-start.7 = (f32[112,128]{1,0:T(8,128)S(1)}, f32[112,128]{1,0:T(8,128)S(1)}, u32[]{:S(2)}, u32[]{:S(2)}) collective-permute-start(f32[112,128]{1,0:T(8,128)S(1)} %sum_grads.1.refs_0_), channel_id=1, source_target_pairs={{0,16},{16,0},{1,17},{17,1},{2,18},{18,2},{3,19},{19,3},{4,20},{20... | collective-permute-start | bytes 172040 | tf_op jit(solution)/shard_map/ppermute | solution.py:675
  129.9 3.7 %collective-permute-done.7.refs_1_ = f32[112,128]{1,0:T(8,128)S(1)} collective-permute-done((f32[112,128]{1,0:T(8,128)S(1)}, f32[112,128]{1,0:T(8,128)S(1)}, u32[]{:S(2)}, u32[]{:S(2)}) %collective-permute-start.7) | collective-permute-done | bytes 57376 | tf_op jit(solution)/shard_map/ppermute | solution.py:675
  133.6 0.1 share.1
  133.7 10.3 %all_to_all.46.refs_0_ = f32[16,32,128]{2,1,0:T(8,128)S(1)} all-to-all(f32[16,32,128]{2,1,0:T(8,128)S(1)} %share.1), channel_id=1, replica_groups=mesh['zh'=2,'rl'=4,'y'=2,'c'=2] {'rl','y','c'}, dimensions={0} | all-to-all | bytes 524288 | tf_op jit(solution)/shard_map/all_to_all | solution.py:677
  144.2 1.4 update.1
  (42 shorter events, 0.2 us)
Async XLA Ops:
  2.9 47.0 %copy-start.2 = (f32[248,256]{1,0:T(8,128)S(1)}, f32[248,256]{1,0:T(8,128)}, u32[]{:S(2)}) copy-start(f32[248,256]{1,0:T(8,128)} %get-tuple-element.71.refs_0_) | copy-start | bytes 761860
  2.9 21.3 %all-to-all-start = ((s32[32,16,128]{2,1,0:T(8,128)}), s32[32,16,128]{2,1,0:T(8,128)S(1)}, u32[]{:S(2)}, u32[]{:S(2)}) async-start(s32[32,16,128]{2,1,0:T(8,128)} %get-tuple-element.66), calls=%async_computation | async-start | bytes 524288 | tf_op jit(solution)/shard_map/all_to_all | solution.py:600
  10.2 18.6 %collective-permute-start.2 = (f32[248,256]{1,0:T(8,128)}, f32[248,256]{1,0:T(8,128)S(1)}, u32[]{:S(2)}, u32[]{:S(2)}) collective-permute-start(f32[248,256]{1,0:T(8,128)} %get-tuple-element.71.refs_0_), channel_id=1, source_target_pairs={{0,2},{2,0},{1,3},{3,1},{4,6},{6,4},{5,7},{7,5},{8,10},{10,8},{9,1... | collective-permute-start | bytes 761864 | tf_op jit(solution)/shard_map/ppermute | solution.py:608
  12.0 4.6 %collective-permute-start = (f32[32,1024]{1,0:T(8,128)}, f32[32,1024]{1,0:T(8,128)S(1)}, u32[]{:S(2)}, u32[]{:S(2)}) collective-permute-start(f32[32,1024]{1,0:T(8,128)} %get-tuple-element.67), channel_id=1, source_target_pairs={{0,0},{2,16},{16,2},{18,18},{1,1},{3,17},{17,3},{19,19},{4,4},{6,2... | collective-permute-start | bytes 393224 | tf_op jit(solution)/shard_map/ppermute | solution.py:597
  13.6 10.6 %collective-permute-start.1 = (f32[32,1024]{1,0:T(8,128)}, f32[32,1024]{1,0:T(8,128)S(1)}, u32[]{:S(2)}, u32[]{:S(2)}) collective-permute-start(f32[32,1024]{1,0:T(8,128)} %get-tuple-element.68), channel_id=1, source_target_pairs={{0,16},{2,0},{16,18},{18,2},{1,17},{3,1},{17,19},{19,3},{4,20},{6,... | collective-permute-start | bytes 393224 | tf_op jit(solution)/shard_map/ppermute | solution.py:597
  28.8 24.3 %copy-start.11 = (f32[47]{0:T(128)S(1)}, f32[47]{0:T(128)}, u32[]{:S(2)}) copy-start(f32[47]{0:T(128)} %param.35) | copy-start | bytes 568
  49.8 3.8 %collective-permute-start.3 = (f32[128,512]{1,0:T(8,128)S(1)}, f32[128,512]{1,0:T(8,128)S(1)}, u32[]{:S(2)}, u32[]{:S(2)}) collective-permute-start(f32[128,512]{1,0:T(8,128)S(1)} %sum_first.1.refs_5_.refs_1_.refs_0_), channel_id=1, source_target_pairs={{0,1},{1,0},{2,3},{3,2},{4,5},{5,4},{6,7},{7,6},{8,9},{9,8},{10,11... | collective-permute-start | bytes 786440 | tf_op jit(solution)/shard_map/ppermute | solution.py:579
  49.9 3.1 %collective-permute-start.5 = (f32[248,256]{1,0:T(8,128)S(1)}, f32[248,256]{1,0:T(8,128)S(1)}, u32[]{:S(2)}, u32[]{:S(2)}) collective-permute-start(f32[248,256]{1,0:T(8,128)S(1)} %copy-done.2), channel_id=1, source_target_pairs={{0,1},{1,0},{2,3},{3,2},{4,5},{5,4},{6,7},{7,6},{8,9},{9,8},{10,11... | collective-permute-start | bytes 761864 | tf_op jit(solution)/shard_map/ppermute | solution.py:579
  50.4 2.6 %collective-permute-start.4 = (f32[248,256]{1,0:T(8,128)S(1)}, f32[248,256]{1,0:T(8,128)S(1)}, u32[]{:S(2)}, u32[]{:S(2)}) collective-permute-start(f32[248,256]{1,0:T(8,128)S(1)} %held.1.refs_3_.refs_1_), channel_id=1, source_target_pairs={{0,1},{1,0},{2,3},{3,2},{4,5},{5,4},{6,7},{7,6},{8,9},{9,8},{10,11... | collective-permute-start | bytes 761864 | tf_op jit(solution)/shard_map/ppermute | solution.py:579
  73.6 70.5 %copy-start = (f32[2,64,256]{2,1,0:T(8,128)S(1)}, f32[2,64,256]{2,1,0:T(8,128)}, u32[]{:S(2)}) copy-start(f32[2,64,256]{2,1,0:T(8,128)} %refs_3_.3) | copy-start | bytes 393220
  73.6 70.5 %copy-start.1 = (f32[2,32,256]{2,1,0:T(8,128)S(1)}, f32[2,32,256]{2,1,0:T(8,128)}, u32[]{:S(2)}) copy-start(f32[2,32,256]{2,1,0:T(8,128)} %refs_2_.1) | copy-start | bytes 196612
  73.6 70.4 %copy-start.3 = (f32[2,64,47]{1,0,2:T(2,128)S(1)}, f32[2,64,47]{1,0,2:T(2,128)}, u32[]{:S(2)}) copy-start(f32[2,64,47]{1,0,2:T(2,128)} %param.33) | copy-start | bytes 72196
  73.6 70.4 %copy-start.4 = (f32[2,64,256]{2,1,0:T(8,128)S(1)}, f32[2,64,256]{2,1,0:T(8,128)}, u32[]{:S(2)}) copy-start(f32[2,64,256]{2,1,0:T(8,128)} %refs_8_.3) | copy-start | bytes 393220
  73.7 70.4 %copy-start.5 = (f32[2,64,256]{2,1,0:T(8,128)S(1)}, f32[2,64,256]{2,1,0:T(8,128)}, u32[]{:S(2)}) copy-start(f32[2,64,256]{2,1,0:T(8,128)} %refs_13_.1) | copy-start | bytes 393220
  73.7 70.4 %copy-start.6 = (f32[2,32,256]{2,1,0:T(8,128)S(1)}, f32[2,32,256]{2,1,0:T(8,128)}, u32[]{:S(2)}) copy-start(f32[2,32,256]{2,1,0:T(8,128)} %refs_7_.1) | copy-start | bytes 196612
  73.7 70.4 %copy-start.7 = (f32[2,32,256]{2,1,0:T(8,128)S(1)}, f32[2,32,256]{2,1,0:T(8,128)}, u32[]{:S(2)}) copy-start(f32[2,32,256]{2,1,0:T(8,128)} %refs_12_.1) | copy-start | bytes 196612
  73.7 70.4 %copy-start.8 = (f32[2,64,47]{1,0,2:T(2,128)S(1)}, f32[2,64,47]{1,0,2:T(2,128)}, u32[]{:S(2)}) copy-start(f32[2,64,47]{1,0,2:T(2,128)} %param.38) | copy-start | bytes 72196
  73.7 70.4 %copy-start.9 = (f32[2,64,47]{1,0,2:T(2,128)S(1)}, f32[2,64,47]{1,0,2:T(2,128)}, u32[]{:S(2)}) copy-start(f32[2,64,47]{1,0,2:T(2,128)} %param.43) | copy-start | bytes 72196
  73.7 70.4 %copy-start.10 = (f32[2,64]{1,0:T(2,128)S(1)}, f32[2,64]{1,0:T(2,128)}, u32[]{:S(2)}) copy-start(f32[2,64]{1,0:T(2,128)} %refs_5_.3) | copy-start | bytes 1540
  73.7 70.4 %copy-start.12 = (f32[2,64]{1,0:T(2,128)S(1)}, f32[2,64]{1,0:T(2,128)}, u32[]{:S(2)}) copy-start(f32[2,64]{1,0:T(2,128)} %refs_10_.1) | copy-start | bytes 1540
  73.7 70.4 %copy-start.13 = (f32[2,64]{1,0:T(2,128)S(1)}, f32[2,64]{1,0:T(2,128)}, u32[]{:S(2)}) copy-start(f32[2,64]{1,0:T(2,128)} %refs_15_.1) | copy-start | bytes 1540
  73.7 70.4 %copy-start.14 = (f32[47]{0:T(128)S(1)}, f32[47]{0:T(128)}, u32[]{:S(2)}) copy-start(f32[47]{0:T(128)} %param.40) | copy-start | bytes 568
  73.8 70.4 %copy-start.15 = (f32[47]{0:T(128)S(1)}, f32[47]{0:T(128)}, u32[]{:S(2)}) copy-start(f32[47]{0:T(128)} %param.45) | copy-start | bytes 568
  73.8 1.5 %collective-permute-start.6 = (f32[128,256]{1,0:T(8,128)S(1)}, f32[128,256]{1,0:T(8,128)S(1)}, u32[]{:S(2)}, u32[]{:S(2)}) collective-permute-start(f32[128,256]{1,0:T(8,128)S(1)} %sum_mid.1.refs_1_.refs_0_), channel_id=1, source_target_pairs={{0,1},{1,0},{2,3},{3,2},{4,5},{5,4},{6,7},{7,6},{8,9},{9,8},{10,11... | collective-permute-start | bytes 393224 | tf_op jit(solution)/shard_map/ppermute | solution.py:579
  127.9 5.7 %collective-permute-start.7 = (f32[112,128]{1,0:T(8,128)S(1)}, f32[112,128]{1,0:T(8,128)S(1)}, u32[]{:S(2)}, u32[]{:S(2)}) collective-permute-start(f32[112,128]{1,0:T(8,128)S(1)} %sum_grads.1.refs_0_), channel_id=1, source_target_pairs={{0,16},{16,0},{1,17},{17,1},{2,18},{18,2},{3,19},{19,3},{4,20},{20... | collective-permute-start | bytes 172040 | tf_op jit(solution)/shard_map/ppermute | solution.py:675

commit v4 on v3

--- a/solution.py
+++ b/solution.py
@@ -16,7 +16,7 @@
 CLASS_ROWS = 48
 LAST_ROWS = 64
 ROW_HIDDEN = 48
-ROW_LAST = 49
+ROW_LAST = 50
 LANE_LOSS = 47
 MIB = 1 << 20
 
@@ -107,12 +107,10 @@
         self.id_rows = -(-(self.at_c3 + l3) // 32) * 32
         self.id_part = self.id_rows // 4
         self.blocks = 2 * self.rl
-        self.pieces = 4 * self.rl
-        self.nf, self.nm, self.nl = 64 // self.pieces, 128 // self.pieces, LAST_ROWS // self.pieces
-        self.half_rows = 4 * (self.nf + self.nm)
-        self.sum_rows = 2 * self.half_rows + 4 * self.nl
-        self.ag_rows = -(-(2 * (self.nf + self.nm) + self.nl + 1) // 8) * 8
-        self.keep_first = self.blocks * self.t1 * self.s1 * 2 <= 8 * MIB
+        self.nf, self.nm, self.nl = 64 // self.blocks, 128 // self.blocks, LAST_ROWS // self.blocks
+        self.pair = self.nl // 2
+        self.at_m, self.at_l, self.piece_rows = 4 * self.nf, 4 * (self.nf + self.nm), 4 * (self.nf + self.nm + self.pair)
+        self.share_rows = -(-(self.nf + self.nm + self.pair + 1) // 8) * 8
 
 
 def prep_body(z, pos, *refs):
@@ -158,10 +156,6 @@
         wmsg[240:241, 64 * j : 64 * j + 64] = bh[j : j + 1, :]
 
 
-def held_body(pos, value, after, out):
-    out[...] = value[...]
-
-
 def weights_body(pos, own, acr, dia, cor, blast, after, w1h, w1l, w2h, w2l, wmh, wml, wlt, wlc, bias, wall, f32a, f32b):
     s = 2 * pos[2] + pos[3]
     for at, part in ((s, own), (s ^ 2, acr), (s ^ 3, dia), (s ^ 1, cor)):
@@ -249,7 +243,7 @@
         lax.fori_loop(0, z.rl, block, 0)
 
 
-def adjacency_first_body(z, pos, ids, after0, after1, a1, small, local, times):
+def adjacency_first_body(z, pos, ids, adj, small, local, times):
     me = pos[2] * z.rl + pos[1]
     for q in range(4):
         small[q * z.id_part : (q + 1) * z.id_part] = ids[2 * q * z.rl + me].astype(F32)
@@ -257,8 +251,7 @@
     n = z.id_rows
     small[n : n + CLASS_ROWS] = jnp.broadcast_to(weight, (CLASS_ROWS, LANES))
     small[n + CLASS_ROWS :] = jnp.broadcast_to(total, (8, LANES))
-    if z.keep_first:
-        adjacency_all(z, ids, z.at_first, z.f1, z.l1, z.s1, me * z.s1, local, times, a1)
+    adjacency_all(z, ids, z.at_first, z.f1, z.l1, z.s1, me * z.s1, local, times, adj)
 
 
 def adjacency_mid_body(z, pos, ids, after, a2, local, times):
@@ -296,31 +289,11 @@
     table[:width], table[width:] = halves(rows)
 
 
-def first_kept_body(z, pos, a1, got0, got1, after, out, table):
+def first_body(z, pos, adj, got0, got1, after, out, table):
     first_table(z, pos, got0, got1, table)
     for r in range(z.blocks):
-        both = dot(table[...], a1[:, r * z.t1 : (r + 1) * z.t1], NN)
+        both = dot(table[...], adj[:, r * z.t1 : (r + 1) * z.t1], NN)
         out[r] = both[: both.shape[0] // 2] + both[both.shape[0] // 2 :]
-
-
-def first_body(z, pos, ids, got0, got1, after, out, table, adj, local, times):
-    me = pos[2] * z.rl + pos[1]
-    first_table(z, pos, got0, got1, table)
-    width = 2 * got0.shape[0]
-    at = numbers()
-    distinct(z, ids, z.at_first, z.f1, z.l1, z.s1, me * z.s1, local, times)
-    for zs in range(2):
-
-        def block(lead, carry):
-            def column(j):
-                return slice(j * LANES, (j + 1) * LANES)
-
-            adjacency_block(z, zs, lead, z.f1, z.l1, z.s1, local, times, at, adj, column)
-            both = dot(table[...], adj[...], NN)
-            out[zs * z.rl + lead] = both[:width] + both[width:]
-            return carry
-
-        lax.fori_loop(0, z.rl, block, 0)
 
 
 def inverse(z, mine, at, lanes):
@@ -457,58 +430,56 @@
     last[...] = jnp.zeros_like(last)
     core0 = jnp.where(c == 0, 1.0, 0.0)
     for s in range(4):
-        last[s, :CLASS_ROWS, :64] = dwl[0][:, 64 * s : 64 * s + 64] * core0
-        last[s, :CLASS_ROWS, 64:] = dwl[1][:, 64 * s : 64 * s + 64] * (1.0 - core0)
+        last[s, :CLASS_ROWS, :64] = dwl[c, :, 64 * s : 64 * s + 64]
         here = jnp.where(c == s // 2, 1.0, 0.0)
         at = 64 * (s % 2)
         last[s, ROW_HIDDEN : ROW_HIDDEN + 1, :64] = b1[0:1, at : at + 64] * here
-        last[s, ROW_HIDDEN : ROW_HIDDEN + 1, 64:] = b2[0:1, at : at + 64] * here
+        last[s, ROW_HIDDEN + 1 : ROW_HIDDEN + 2, :64] = b2[0:1, at : at + 64] * here
         last[s, ROW_LAST : ROW_LAST + 1, :LANE_LOSS] = b3[0:1, :LANE_LOSS] * core0
         last[s, ROW_LAST : ROW_LAST + 1, LANE_LOSS : LANE_LOSS + 1] = loss[0:1, 0:1] * core0
-    n = 4 * (z.nf + z.nm)
-    for p in range(z.pieces):
+    for p in range(z.blocks):
         for s in range(4):
             e = z.nf * p
             at = 128 * (e // 32) + 32 * s + e % 32
             out[p, s * z.nf : (s + 1) * z.nf] = first[at : at + z.nf]
             e = z.nm * p
             at = 256 * (e // 64) + 64 * s + e % 64
-            out[p, 4 * z.nf + s * z.nm : 4 * z.nf + (s + 1) * z.nm] = mid[at : at + z.nm]
-            out[p, n + s * z.nl : n + (s + 1) * z.nl] = last[s, z.nl * p : z.nl * (p + 1)]
+            out[p, z.at_m + s * z.nm : z.at_m + (s + 1) * z.nm] = mid[at : at + z.nm]
+            e = z.nl * p
+            two = [last[s, e + h * z.pair : e + (h + 1) * z.pair, :64] for h in range(2)]
+            out[p, z.at_l + s * z.pair : z.at_l + (s + 1) * z.pair] = jnp.concatenate(two, axis=1)
 
 
 def sum_grads_body(z, pos, part, out):
-    n = z.half_rows
-    even, odd = part[0], part[1]
-    for d in range(2, z.pieces, 2):
-        even = even + part[d]
-        odd = odd + part[d + 1]
-    out[:n] = even[:n]
-    out[n : 2 * n] = odd[:n]
-    out[2 * n :] = even[n:] + odd[n:]
+    total = part[0]
+    for r in range(1, z.blocks):
+        total = total + part[r]
+    out[...] = total
 
 
 def share_body(z, pos, own, other, out):
-    n, nf, nm, nl = z.half_rows, z.nf, z.nm, z.nl
+    nf, nm, pair = z.nf, z.nm, z.pair
     total = own[...] + other[...]
-    piece = 4 * pos[1] + 2 * pos[2] + pos[3]
+    piece = pos[2] * z.rl + pos[1]
     lane = lax.broadcasted_iota(I32, (1, LANES), 1)
-    squares = jnp.sum(total[: 2 * n] * total[: 2 * n], axis=0, keepdims=True)
+    squares = jnp.sum(total[: z.at_l] * total[: z.at_l], axis=0, keepdims=True)
     for s in range(4):
-        for i in range(nl):
-            row = total[2 * n + s * nl + i : 2 * n + s * nl + i + 1]
-            at = piece * nl + i
-            squares = squares + jnp.where(at <= ROW_HIDDEN, 1.0, 0.0) * row * row
+        for i in range(pair):
+            row = total[z.at_l + s * pair + i : z.at_l + s * pair + i + 1]
+            at = piece * z.nl + i + jnp.where(lane < 64, 0, pair)
+            keep = at < ROW_LAST
             if s == 0:
-                squares = squares + jnp.where(at == ROW_LAST, 1.0, 0.0) * jnp.where(lane < 47, row * row, 0.0)
+                keep = jnp.logical_or(keep, jnp.logical_and(at == ROW_LAST, lane % 64 < 47))
+            squares = squares + jnp.where(keep, row * row, 0.0)
     squares = jnp.broadcast_to(jnp.sum(squares, axis=1, keepdims=True), (1, LANES))
-    pad = z.ag_rows - 2 * (nf + nm) - nl - 1
+    pad = z.share_rows - nf - nm - pair - 1
     for s in range(4):
-        rows = []
-        for h in range(2):
-            rows.append(total[h * n + s * nf : h * n + (s + 1) * nf])
-            rows.append(total[h * n + 4 * nf + s * nm : h * n + 4 * nf + (s + 1) * nm])
-        rows += [total[2 * n + s * nl : 2 * n + (s + 1) * nl], squares]
+        rows = [
+            total[s * nf : (s + 1) * nf],
+            total[z.at_m + s * nm : z.at_m + (s + 1) * nm],
+            total[z.at_l + s * pair : z.at_l + (s + 1) * pair],
+            squares,
+        ]
         if pad:
             rows.append(jnp.zeros((pad, LANES), F32))
         rows = jnp.concatenate(rows, axis=0)
@@ -520,11 +491,11 @@
     w, m, v = refs[0:5], refs[5:10], refs[10:15]
     new, moment, square = refs[15:20], refs[20:25], refs[25:30]
     loss, weight_sum, norm = refs[30:33]
-    nf, nm, nl = z.nf, z.nm, z.nl
-    at = 2 * (nf + nm) + nl
-    total = whole[0, at : at + 1, 0:1]
-    for p in range(1, z.pieces):
-        total = total + whole[p, at : at + 1, 0:1]
+    nf, nm, nl, pair = z.nf, z.nm, z.nl, z.pair
+    h = nf + nm
+    total = whole[0, h + pair : h + pair + 1, 0:1]
+    for p in range(1, 4 * z.rl):
+        total = total + whole[p, h + pair : h + pair + 1, 0:1]
     root = jnp.sqrt(total)
     scale = jnp.minimum(1.0, 0.01 / root)
     norm[...] = root
@@ -542,27 +513,35 @@
         outs = adamw(w[i][at], grad, m[i][at], v[i][at])
         new[i][at], moment[i][at], square[i][at] = outs
 
-    h = nf + nm
-    for p in range(z.pieces):
+    def source(p, c):
+        return 4 * (p % z.rl) + 2 * (p // z.rl) + c
+
+    def class_row(row, c):
+        p, i = row // nl, row % nl
+        at, lane = h + i % pair, 64 * (i // pair)
+        return whole[source(p, c), at : at + 1, lane : lane + 64]
+
+    for p in range(z.blocks):
+        a, b = source(p, 0), source(p, 1)
         e = nf * p
-        g = jnp.concatenate([whole[p, :nf], whole[p, h : h + nf]], axis=1)
+        g = jnp.concatenate([whole[a, :nf], whole[b, :nf]], axis=1)
         put(0, (e // 32, slice(e % 32, e % 32 + nf), slice(None)), g)
         e = nm * p
-        g = jnp.concatenate([whole[p, nf:h], whole[p, h + nf : 2 * h]], axis=1)
+        g = jnp.concatenate([whole[a, nf:h], whole[b, nf:h]], axis=1)
         put(1, (e // 64, slice(e % 64, e % 64 + nm), slice(None)), g)
-        a = nl * p
-        b = min(a + nl, 47)
-        if a < b:
-            for j in range(2):
-                put(2, (slice(a, b), j, slice(None)), whole[p, 2 * h : 2 * h + b - a, 64 * j : 64 * j + 64])
-        for i in range(nl):
-            row = whole[p, 2 * h + i : 2 * h + i + 1]
-            if a + i == ROW_HIDDEN:
-                for j in range(2):
-                    put(3, (slice(j, j + 1), slice(None)), row[:, 64 * j : 64 * j + 64])
-            elif a + i == ROW_LAST:
-                put(4, (slice(None), slice(None)), row[:, :47])
-                loss[...] = row[:, LANE_LOSS : LANE_LOSS + 1]
+        for j, src in enumerate((a, b)):
+            for half in range(2):
+                at = nl * p + half * pair
+                end = min(at + pair, 47)
+                if at < end:
+                    g = whole[src, h : h + end - at, 64 * half : 64 * half + 64]
+                    put(2, (slice(at, end), j, slice(None)), g)
+    for j in range(2):
+        g = jnp.where(pos[2] == 0, class_row(ROW_HIDDEN + j, 0), class_row(ROW_HIDDEN + j, 1))
+        put(3, (slice(j, j + 1), slice(None)), g)
+    row = class_row(ROW_LAST, 0)
+    put(4, (slice(None), slice(None)), row[:, :47])
+    loss[...] = row[:, LANE_LOSS : LANE_LOSS + 1]
 
 
 def on_device(
@@ -598,22 +577,15 @@
         for j, f in enumerate((f0, f1))
     )
     ids = lax.all_to_all(ids, ("y", "c", "zh", "rl"), 0, 0)
-    table = pltpu.VMEM((128, z.s1), BF16)
-    sums = [((blocks, 64, z.t1), F32)]
-    small = ((z.id_rows + CLASS_ROWS + 8, LANES), F32)
+    w_across = lax.ppermute(wmsg, "y", [(0, 1), (1, 0)])
     a1, mine = call(
-        bind(adjacency_first_body, z), [((z.s1, blocks * z.t1) if z.keep_first else (8, LANES), BF16), small],
-        "adjacency_first", 4, us=6.0, scratch=tables(z, z.f1, z.l1, z.s1),
-    )(ids, got0, got1)
-    w_across = lax.ppermute(wmsg, "y", [(0, 1), (1, 0)])
-    w_across = call(held_body, [((248, 256), F32)], "held", 4)(w_across, mine)[0]
-    if z.keep_first:
-        part = call(bind(first_kept_body, z), sums, "first", 4, us=3.0, scratch=[table])(a1, got0, got1, w_across)[0]
-    else:
-        part = call(
-            bind(first_body, z), sums, "first", 16, us=8.0,
-            scratch=[table, pltpu.VMEM((z.s1, z.t1), BF16), *tables(z, z.f1, z.l1, z.s1)],
-        )(ids, got0, got1, w_across)[0]
+        bind(adjacency_first_body, z),
+        [((z.s1, blocks * z.t1), BF16), ((z.id_rows + CLASS_ROWS + 8, LANES), F32)], "adjacency_first", 4 + blocks,
+        us=6.0, scratch=tables(z, z.f1, z.l1, z.s1),
+    )(ids)
+    part = call(
+        bind(first_body, z), [((blocks, 64, z.t1), F32)], "first", 4 + blocks, scratch=[pltpu.VMEM((128, z.s1), BF16)],
+    )(a1, got0, got1, w_across)[0]
     part = exchange(part)
     half = call(bind(sum_first_body, z), [((128, z.t1), F32)], "sum_first", 8)(mine, part, got0, got1)[0]
     other = flip(half)
@@ -664,16 +636,16 @@
     )
     part = exchange(part)
     part = call(
-        bind(grads_body, z), [((z.pieces, 4 * (z.nf + z.nm + z.nl), LANES), F32)], "grads", 12,
+        bind(grads_body, z), [((blocks, z.piece_rows, LANES), F32)], "grads", 12,
         scratch=[
             pltpu.VMEM((256, 128), F32), pltpu.VMEM((512, 128), F32),
             pltpu.VMEM((4, LAST_ROWS, LANES), F32),
         ],
     )(part, a2, dpre2, wmh, wml, slope1, x1, y2, dwl, grad, loss)[0]
-    part = lax.all_to_all(part, ("rl", "y", "c"), 0, 0)
-    own = call(bind(sum_grads_body, z), [((z.sum_rows, LANES), F32)], "sum_grads", 8)(part)[0]
+    part = exchange(part)
+    own = call(bind(sum_grads_body, z), [((z.piece_rows, LANES), F32)], "sum_grads", 8)(part)[0]
     other = lax.ppermute(own, "zh", [(0, 1), (1, 0)])
-    part = call(bind(share_body, z), [((z.pieces, z.ag_rows, LANES), F32)], "share", 8)(own, other)[0]
+    part = call(bind(share_body, z), [((4 * z.rl, z.share_rows, LANES), F32)], "share", 8)(own, other)[0]
     whole = lax.all_to_all(part, ("rl", "y", "c"), 0, 0)
 
     params = (w_first, w_mid, swapped(w_last), b_hidden, b_last[None])

time: 146 us -> 142 us (0.973)
  blocking collectives: 97.1 us -> 95.2 us
    all_to_all x1 -> x0, blocking collectives: 13.2 us -> none  [on_device(): part = lax.all_to_all(part, ('rl', 'y', 'c'), 0, 0)]
    all_to_all x5 -> x6, blocking collectives: 73.6 us -> 84.9 us  [exchange(): return lax.all_to_all(value, ('y', 'rl'), 0, 0)]
    ppermute x2, waiting for transfers between devices: 7.59 us -> 0.01 us  [on_device(): lax.ppermute(f, ('zh', 'y'), [(2 * zh + y, 2 * (y ^ j) + zh) for zh in ra...]
    all_to_all x1, waiting for transfers between devices: 0.01 us -> 5.37 us  [on_device(): ids = lax.all_to_all(ids, ('y', 'c', 'zh', 'rl'), 0, 0)]
    pallas_call x17 -> x16, Pallas kernels: 19.5 us -> 19.5 us  [run(): pl.pallas_call(placed, out_shape=[jax.ShapeDtypeStruct(s, d) for s, d in...]
where the time goes in v4:
time: 142 us; the launch traced here: 141 us
  blocking collectives  95.2 us (67%)
  Pallas kernels  19.5 us (14%)
  starting transfers between devices  15 us (11%)
  waiting for transfers between devices  10.3 us (7%)
    all_to_all x6, blocking collectives, exchange(): return lax.all_to_all(value, ('y', 'rl'), 0, 0)  84.9 us
    pallas_call x16, Pallas kernels, run(): pl.pallas_call(placed, out_shape=[jax.ShapeDtypeStruct(s, d) for s, d in...  19.5 us
    all_to_all x1, blocking collectives, on_device(): whole = lax.all_to_all(part, ('rl', 'y', 'c'), 0, 0)  10.3 us
    all_to_all x1, starting transfers between devices, on_device(): ids = lax.all_to_all(ids, ('y', 'c', 'zh', 'rl'), 0, 0)  7.3 us
    all_to_all x1, waiting for transfers between devices, on_device(): ids = lax.all_to_all(ids, ('y', 'c', 'zh', 'rl'), 0, 0)  5.37 us
    ppermute x1, waiting for transfers between devices, on_device(): other = lax.ppermute(own, 'zh', [(0, 1), (1, 0)])  4.94 us
    ppermute x2, starting transfers between devices, on_device(): lax.ppermute(f, ('zh', 'y'), [(2 * zh + y, 2 * (y ^ j) + zh) for zh in ra...  4.57 us
  transfers between devices with their start and end apart: 9, of which 2 were waited for; matrix products, arithmetic and copies ran while one was open for 0% of the time, Pallas kernels for 6%

profile of v4, /device:TPU:0, one launch (start us, length us, event | category | flops | bytes accessed | tf_op | source)
XLA Modules:
  0.0 141.2 jit_solution(7397910580764888717)
XLA Ops:
  0.7 2.2 %prep.1 = (s32[32,16,128]{2,1,0:T(8,128)}, f32[32,1024]{1,0:T(8,128)}, f32[32,1024]{1,0:T(8,128)}, f32[248,256]{1,0:T(8,128)}) custom-call(s32[5,2,512]{2,1,0:T(2,128)} %bitcast.28, s32[2,512]{1,0:T(2,128)} %refs_1_.1, s32[10,2,256]{2,1,0:T(2,128)} %bitcast.29, s32[2,256]{1,0:T(2,128)} %refs_3_.2, s32[15,2,128]{2,1,0:T(2,128)} %bitcast.30, ...), custom_call_target="tpu_custom_call" | custom-call | bytes 7200000 | tf_op jit(solution)/shard_map/prep/pallas_call | solution.py:65
  2.9 7.3 %all-to-all-start = ((s32[32,16,128]{2,1,0:T(8,128)}), s32[32,16,128]{2,1,0:T(8,128)S(1)}, u32[]{:S(2)}, u32[]{:S(2)}) async-start(s32[32,16,128]{2,1,0:T(8,128)} %get-tuple-element.66), calls=%async_computation | async-start | bytes 524288 | tf_op jit(solution)/shard_map/all_to_all | solution.py:579
  10.2 1.8 %collective-permute-start.2 = (f32[248,256]{1,0:T(8,128)}, f32[248,256]{1,0:T(8,128)S(1)}, u32[]{:S(2)}, u32[]{:S(2)}) collective-permute-start(f32[248,256]{1,0:T(8,128)} %get-tuple-element.71.refs_0_), channel_id=1, source_target_pairs={{0,2},{2,0},{1,3},{3,1},{4,6},{6,4},{5,7},{7,5},{8,10},{10,8},{9,1... | collective-permute-start | bytes 761864 | tf_op jit(solution)/shard_map/ppermute | solution.py:580
  12.0 1.6 %collective-permute-start = (f32[32,1024]{1,0:T(8,128)}, f32[32,1024]{1,0:T(8,128)S(1)}, u32[]{:S(2)}, u32[]{:S(2)}) collective-permute-start(f32[32,1024]{1,0:T(8,128)} %get-tuple-element.69), channel_id=1, source_target_pairs={{0,0},{2,16},{16,2},{18,18},{1,1},{3,17},{17,3},{19,19},{4,4},{6,2... | collective-permute-start | bytes 393224 | tf_op jit(solution)/shard_map/ppermute | solution.py:576
  13.6 3.0 %collective-permute-start.1 = (f32[32,1024]{1,0:T(8,128)}, f32[32,1024]{1,0:T(8,128)S(1)}, u32[]{:S(2)}, u32[]{:S(2)}) collective-permute-start(f32[32,1024]{1,0:T(8,128)} %get-tuple-element.70), channel_id=1, source_target_pairs={{0,16},{2,0},{16,18},{18,2},{1,17},{3,1},{17,19},{19,3},{4,20},{6,... | collective-permute-start | bytes 393224 | tf_op jit(solution)/shard_map/ppermute | solution.py:576
  16.6 5.4 %all-to-all-done.refs_0_ = s32[32,16,128]{2,1,0:T(8,128)S(1)} async-done(((s32[32,16,128]{2,1,0:T(8,128)}), s32[32,16,128]{2,1,0:T(8,128)S(1)}, u32[]{:S(2)}, u32[]{:S(2)}) %all-to-all-start) | async-done | bytes 262176 | tf_op jit(solution)/shard_map/all_to_all | solution.py:579
  22.0 4.6 %adjacency_first.1 = (bf16[1024,4096]{1,0:T(8,128)(2,1)S(1)}, f32[120,128]{1,0:T(8,128)S(1)}) custom-call(s32[32,16,128]{2,1,0:T(8,128)S(1)} %all-to-all-done.refs_0_), custom_call_target="tpu_custom_call" | custom-call | bytes 21600000 | tf_op jit(solution)/shard_map/adjacency_first/pallas_call | solution.py:65
  26.6 1.3 first.1
  27.9 19.9 %all_to_all.40.refs_1_ = f32[8,64,512]{2,1,0:T(8,128)S(1)} all-to-all(f32[8,64,512]{2,1,0:T(8,128)S(1)} %first.1), channel_id=1, replica_groups=mesh['zh'=2,'rl'=4,'y'=2,'c'=2] {'y','rl'}, dimensions={0} | all-to-all | bytes 2097152 | tf_op jit(solution)/shard_map/all_to_all | solution.py:561
  47.7 0.1 sum_first.1.refs_5_.refs_1_.refs_0_
  47.8 0.1 collective-permute-start.3
  47.9 0.5 collective-permute-start.5
  48.4 0.1 collective-permute-start.4
  48.5 2.5 %adjacency_mid.1.refs_5_.refs_1_ = bf16[512,2048]{1,0:T(8,128)(2,1)S(1)} custom-call(s32[32,16,128]{2,1,0:T(8,128)S(1)} %all-to-all-done.refs_0_, f32[128,512]{1,0:T(8,128)S(1)} %sum_first.1.refs_5_.refs_1_.refs_0_), custom_call_target="tpu_custom_call" | custom-call | bytes 10800000 | tf_op jit(solution)/shard_map/adjacency_mid/pallas_call | solution.py:65
  51.0 0.5 weights.1
  51.6 1.3 hidden_one.1
  52.8 18.7 %all_to_all.41.refs_1_ = f32[8,128,256]{2,1,0:T(8,128)S(1)} all-to-all(f32[8,128,256]{2,1,0:T(8,128)S(1)} %get-tuple-element.75), channel_id=1, replica_groups=mesh['zh'=2,'rl'=4,'y'=2,'c'=2] {'y','rl'}, dimensions={0} | all-to-all | bytes 2097152 | tf_op jit(solution)/shard_map/all_to_all | solution.py:561
  71.7 0.1 collective-permute-start.6
  71.8 1.4 adjacency_last.1.refs_7_.refs_3_
  73.2 1.2 hidden_two.1
  74.4 9.6 %all_to_all.42.refs_1_ = f32[8,48,128]{2,1,0:T(8,128)S(1)} all-to-all(f32[8,48,128]{2,1,0:T(8,128)S(1)} %get-tuple-element.80), channel_id=1, replica_groups=mesh['zh'=2,'rl'=4,'y'=2,'c'=2] {'y','rl'}, dimensions={0} | all-to-all | bytes 393216 | tf_op jit(solution)/shard_map/all_to_all | solution.py:561
  84.0 0.2 logits.1
  84.2 9.0 %all_to_all.43.refs_1_ = f32[8,48,128]{2,1,0:T(8,128)S(1)} all-to-all(f32[8,48,128]{2,1,0:T(8,128)S(1)} %get-tuple-element.82), channel_id=1, replica_groups=mesh['zh'=2,'rl'=4,'y'=2,'c'=2] {'y','rl'}, dimensions={0} | all-to-all | bytes 393216 | tf_op jit(solution)/shard_map/all_to_all | solution.py:561
  93.2 1.2 back_last.1
  94.4 16.7 %all_to_all.44.refs_0_ = f32[8,128,256]{2,1,0:T(8,128)S(1)} all-to-all(f32[8,128,256]{2,1,0:T(8,128)S(1)} %get-tuple-element.89), channel_id=1, replica_groups=mesh['zh'=2,'rl'=4,'y'=2,'c'=2] {'y','rl'}, dimensions={0} | all-to-all | bytes 2097152 | tf_op jit(solution)/shard_map/all_to_all | solution.py:561
  111.1 1.6 %grads.1 = f32[8,112,128]{2,1,0:T(8,128)S(1)} custom-call(f32[8,128,256]{2,1,0:T(8,128)S(1)} %all_to_all.44.refs_0_, bf16[512,2048]{1,0:T(8,128)(2,1)S(1)} %adjacency_mid.1.refs_5_.refs_1_, f32[256,256]{1,0:T(8,128)S(1)} %get-tuple-element.90.refs_2_, bf16[2,256,256]{2,1,0:T(8,128)(2,1)S(1)} %get-tuple-element.87.refs_7_.refs_3_, ...), custom_call_target="tpu_custom_call" | custom-call | bytes 3600000 | tf_op jit(solution)/shard_map/grads/pallas_call | solution.py:65
  112.7 11.0 %all_to_all.45.refs_0_ = f32[8,112,128]{2,1,0:T(8,128)S(1)} all-to-all(f32[8,112,128]{2,1,0:T(8,128)S(1)} %grads.1), channel_id=1, replica_groups=mesh['zh'=2,'rl'=4,'y'=2,'c'=2] {'y','rl'}, dimensions={0} | all-to-all | bytes 917504 | tf_op jit(solution)/shard_map/all_to_all | solution.py:561
  123.7 0.5 collective-permute-start.7
  124.3 4.9 %collective-permute-done.7.refs_1_ = f32[112,128]{1,0:T(8,128)S(1)} collective-permute-done((f32[112,128]{1,0:T(8,128)S(1)}, f32[112,128]{1,0:T(8,128)S(1)}, u32[]{:S(2)}, u32[]{:S(2)}) %collective-permute-start.7) | collective-permute-done | bytes 57376 | tf_op jit(solution)/shard_map/ppermute | solution.py:647
  129.2 0.1 share.1
  129.3 10.3 %all_to_all.46.refs_0_ = f32[16,32,128]{2,1,0:T(8,128)S(1)} all-to-all(f32[16,32,128]{2,1,0:T(8,128)S(1)} %share.1), channel_id=1, replica_groups=mesh['zh'=2,'rl'=4,'y'=2,'c'=2] {'rl','y','c'}, dimensions={0} | all-to-all | bytes 524288 | tf_op jit(solution)/shard_map/all_to_all | solution.py:649
  139.8 1.4 update.1
  (41 shorter events, 0.2 us)
Async XLA Ops:
  2.9 45.0 %copy-start.2 = (f32[248,256]{1,0:T(8,128)S(1)}, f32[248,256]{1,0:T(8,128)}, u32[]{:S(2)}) copy-start(f32[248,256]{1,0:T(8,128)} %get-tuple-element.71.refs_0_) | copy-start | bytes 761860
  2.9 19.1 %all-to-all-start = ((s32[32,16,128]{2,1,0:T(8,128)}), s32[32,16,128]{2,1,0:T(8,128)S(1)}, u32[]{:S(2)}, u32[]{:S(2)}) async-start(s32[32,16,128]{2,1,0:T(8,128)} %get-tuple-element.66), calls=%async_computation | async-start | bytes 524288 | tf_op jit(solution)/shard_map/all_to_all | solution.py:579
  10.2 40.8 %copy-start.11 = (f32[47]{0:T(128)S(1)}, f32[47]{0:T(128)}, u32[]{:S(2)}) copy-start(f32[47]{0:T(128)} %param.35) | copy-start | bytes 568
  10.2 16.4 %collective-permute-start.2 = (f32[248,256]{1,0:T(8,128)}, f32[248,256]{1,0:T(8,128)S(1)}, u32[]{:S(2)}, u32[]{:S(2)}) collective-permute-start(f32[248,256]{1,0:T(8,128)} %get-tuple-element.71.refs_0_), channel_id=1, source_target_pairs={{0,2},{2,0},{1,3},{3,1},{4,6},{6,4},{5,7},{7,5},{8,10},{10,8},{9,1... | collective-permute-start | bytes 761864 | tf_op jit(solution)/shard_map/ppermute | solution.py:580
  12.0 14.5 %collective-permute-start = (f32[32,1024]{1,0:T(8,128)}, f32[32,1024]{1,0:T(8,128)S(1)}, u32[]{:S(2)}, u32[]{:S(2)}) collective-permute-start(f32[32,1024]{1,0:T(8,128)} %get-tuple-element.69), channel_id=1, source_target_pairs={{0,0},{2,16},{16,2},{18,18},{1,1},{3,17},{17,3},{19,19},{4,4},{6,2... | collective-permute-start | bytes 393224 | tf_op jit(solution)/shard_map/ppermute | solution.py:576
  13.6 13.0 %collective-permute-start.1 = (f32[32,1024]{1,0:T(8,128)}, f32[32,1024]{1,0:T(8,128)S(1)}, u32[]{:S(2)}, u32[]{:S(2)}) collective-permute-start(f32[32,1024]{1,0:T(8,128)} %get-tuple-element.70), channel_id=1, source_target_pairs={{0,16},{2,0},{16,18},{18,2},{1,17},{3,1},{17,19},{19,3},{4,20},{6,... | collective-permute-start | bytes 393224 | tf_op jit(solution)/shard_map/ppermute | solution.py:576
  47.8 3.8 %collective-permute-start.3 = (f32[128,512]{1,0:T(8,128)S(1)}, f32[128,512]{1,0:T(8,128)S(1)}, u32[]{:S(2)}, u32[]{:S(2)}) collective-permute-start(f32[128,512]{1,0:T(8,128)S(1)} %sum_first.1.refs_5_.refs_1_.refs_0_), channel_id=1, source_target_pairs={{0,1},{1,0},{2,3},{3,2},{4,5},{5,4},{6,7},{7,6},{8,9},{9,8},{10,11... | collective-permute-start | bytes 786440 | tf_op jit(solution)/shard_map/ppermute | solution.py:558
  47.9 3.1 %collective-permute-start.5 = (f32[248,256]{1,0:T(8,128)S(1)}, f32[248,256]{1,0:T(8,128)S(1)}, u32[]{:S(2)}, u32[]{:S(2)}) collective-permute-start(f32[248,256]{1,0:T(8,128)S(1)} %copy-done.2), channel_id=1, source_target_pairs={{0,1},{1,0},{2,3},{3,2},{4,5},{5,4},{6,7},{7,6},{8,9},{9,8},{10,11... | collective-permute-start | bytes 761864 | tf_op jit(solution)/shard_map/ppermute | solution.py:558
  48.4 2.6 %collective-permute-start.4 = (f32[248,256]{1,0:T(8,128)S(1)}, f32[248,256]{1,0:T(8,128)S(1)}, u32[]{:S(2)}, u32[]{:S(2)}) collective-permute-start(f32[248,256]{1,0:T(8,128)S(1)} %collective-permute-done.2.refs_3_.refs_1_), channel_id=1, source_target_pairs={{0,1},{1,0},{2,3},{3,2},{4,5},{5,4},{6,7},{7,6},{8,9},{9,8},{10,11... | collective-permute-start | bytes 761864 | tf_op jit(solution)/shard_map/ppermute | solution.py:558
  71.6 68.1 %copy-start = (f32[2,64,256]{2,1,0:T(8,128)S(1)}, f32[2,64,256]{2,1,0:T(8,128)}, u32[]{:S(2)}) copy-start(f32[2,64,256]{2,1,0:T(8,128)} %refs_3_.3) | copy-start | bytes 393220
  71.6 68.1 %copy-start.1 = (f32[2,32,256]{2,1,0:T(8,128)S(1)}, f32[2,32,256]{2,1,0:T(8,128)}, u32[]{:S(2)}) copy-start(f32[2,32,256]{2,1,0:T(8,128)} %refs_2_.1) | copy-start | bytes 196612
  71.6 68.1 %copy-start.3 = (f32[2,64,47]{1,0,2:T(2,128)S(1)}, f32[2,64,47]{1,0,2:T(2,128)}, u32[]{:S(2)}) copy-start(f32[2,64,47]{1,0,2:T(2,128)} %param.33) | copy-start | bytes 72196
  71.6 68.1 %copy-start.4 = (f32[2,64,256]{2,1,0:T(8,128)S(1)}, f32[2,64,256]{2,1,0:T(8,128)}, u32[]{:S(2)}) copy-start(f32[2,64,256]{2,1,0:T(8,128)} %refs_8_.3) | copy-start | bytes 393220
  71.6 68.1 %copy-start.5 = (f32[2,64,256]{2,1,0:T(8,128)S(1)}, f32[2,64,256]{2,1,0:T(8,128)}, u32[]{:S(2)}) copy-start(f32[2,64,256]{2,1,0:T(8,128)} %refs_13_.1) | copy-start | bytes 393220
  71.6 68.1 %copy-start.6 = (f32[2,32,256]{2,1,0:T(8,128)S(1)}, f32[2,32,256]{2,1,0:T(8,128)}, u32[]{:S(2)}) copy-start(f32[2,32,256]{2,1,0:T(8,128)} %refs_7_.1) | copy-start | bytes 196612
  71.7 68.1 %copy-start.7 = (f32[2,32,256]{2,1,0:T(8,128)S(1)}, f32[2,32,256]{2,1,0:T(8,128)}, u32[]{:S(2)}) copy-start(f32[2,32,256]{2,1,0:T(8,128)} %refs_12_.1) | copy-start | bytes 196612
  71.7 68.1 %copy-start.8 = (f32[2,64,47]{1,0,2:T(2,128)S(1)}, f32[2,64,47]{1,0,2:T(2,128)}, u32[]{:S(2)}) copy-start(f32[2,64,47]{1,0,2:T(2,128)} %param.38) | copy-start | bytes 72196
  71.7 68.1 %copy-start.9 = (f32[2,64,47]{1,0,2:T(2,128)S(1)}, f32[2,64,47]{1,0,2:T(2,128)}, u32[]{:S(2)}) copy-start(f32[2,64,47]{1,0,2:T(2,128)} %param.43) | copy-start | bytes 72196
  71.7 68.1 %copy-start.10 = (f32[2,64]{1,0:T(2,128)S(1)}, f32[2,64]{1,0:T(2,128)}, u32[]{:S(2)}) copy-start(f32[2,64]{1,0:T(2,128)} %refs_5_.3) | copy-start | bytes 1540
  71.7 68.1 %copy-start.12 = (f32[2,64]{1,0:T(2,128)S(1)}, f32[2,64]{1,0:T(2,128)}, u32[]{:S(2)}) copy-start(f32[2,64]{1,0:T(2,128)} %refs_10_.1) | copy-start | bytes 1540
  71.7 68.1 %copy-start.13 = (f32[2,64]{1,0:T(2,128)S(1)}, f32[2,64]{1,0:T(2,128)}, u32[]{:S(2)}) copy-start(f32[2,64]{1,0:T(2,128)} %refs_15_.1) | copy-start | bytes 1540
  71.7 68.1 %copy-start.14 = (f32[47]{0:T(128)S(1)}, f32[47]{0:T(128)}, u32[]{:S(2)}) copy-start(f32[47]{0:T(128)} %param.40) | copy-start | bytes 568
  71.7 68.1 %copy-start.15 = (f32[47]{0:T(128)S(1)}, f32[47]{0:T(128)}, u32[]{:S(2)}) copy-start(f32[47]{0:T(128)} %param.45) | copy-start | bytes 568
  71.7 1.5 %collective-permute-start.6 = (f32[128,256]{1,0:T(8,128)S(1)}, f32[128,256]{1,0:T(8,128)S(1)}, u32[]{:S(2)}, u32[]{:S(2)}) collective-permute-start(f32[128,256]{1,0:T(8,128)S(1)} %sum_mid.1.refs_1_.refs_0_), channel_id=1, source_target_pairs={{0,1},{1,0},{2,3},{3,2},{4,5},{5,4},{6,7},{7,6},{8,9},{9,8},{10,11... | collective-permute-start | bytes 393224 | tf_op jit(solution)/shard_map/ppermute | solution.py:558
  123.7 5.5 %collective-permute-start.7 = (f32[112,128]{1,0:T(8,128)S(1)}, f32[112,128]{1,0:T(8,128)S(1)}, u32[]{:S(2)}, u32[]{:S(2)}) collective-permute-start(f32[112,128]{1,0:T(8,128)S(1)} %sum_grads.1.refs_0_), channel_id=1, source_target_pairs={{0,16},{16,0},{1,17},{17,1},{2,18},{18,2},{3,19},{19,3},{4,20},{20... | collective-permute-start | bytes 172040 | tf_op jit(solution)/shard_map/ppermute | solution.py:647

commit v5 on v4

--- a/solution.py
+++ b/solution.py
@@ -113,10 +113,10 @@
         self.share_rows = -(-(self.nf + self.nm + self.pair + 1) // 8) * 8
 
 
-def prep_body(z, pos, *refs):
-    ids, f0, f1, wmsg, rows = refs[12:17]
-    nf, cf, nm, cm, nl, cl, labels, feats, wf, wm, wl, bh = refs[17:29]
-    fetch(refs[:12], refs[17:29], refs[29])
+def ids_body(z, pos, *refs):
+    ids, rows = refs[7:9]
+    nf, cf, nm, cm, nl, cl, labels = refs[9:16]
+    fetch(refs[:7], refs[9:16], refs[16])
 
     def put(mb, at, value):
         for j in range(value.shape[1] // LANES):
@@ -144,6 +144,12 @@
         for s in range(4):
             for lead in range(z.rl):
                 ids[(2 * s + mb) * z.rl + lead] = mine
+
+
+def prep_body(z, pos, *refs):
+    f0, f1, wmsg = refs[5:8]
+    feats, wf, wm, wl, bh = refs[8:13]
+    fetch(refs[:5], refs[8:13], refs[13])
     y = pos[2]
     f0[...] = feats[y]
     f1[...] = feats[1 - y]
@@ -565,12 +571,15 @@
 
     raw = (
         swapped(neigh_first), count_first, swapped(neigh_mid), count_mid, swapped(neigh_last), count_last, labels,
-        jnp.transpose(features, (0, 2, 1)), w_first, w_mid, swapped(w_last), b_hidden,
     )
-    ids, f0, f1, wmsg = call(
-        bind(prep_body, z),
-        [((4 * z.ranks, z.id_part, LANES), I32), ((32, z.s1), F32), ((32, z.s1), F32), ((248, 256), F32)],
-        "prep", 58, scratch=[pltpu.VMEM((2, z.id_rows, LANES), I32), *like(*raw)], where=HBM, us=2.0,
+    ids = call(
+        bind(ids_body, z), [((4 * z.ranks, z.id_part, LANES), I32)], "ids", 58,
+        scratch=[pltpu.VMEM((2, z.id_rows, LANES), I32), *like(*raw)], where=HBM,
+    )(*raw)[0]
+    raw = (jnp.transpose(features, (0, 2, 1)), w_first, w_mid, swapped(w_last), b_hidden)
+    f0, f1, wmsg = call(
+        bind(prep_body, z), [((32, z.s1), F32), ((32, z.s1), F32), ((248, 256), F32)], "prep", 58, scratch=like(*raw),
+        where=HBM,
     )(*raw)
     got0, got1 = (
         lax.ppermute(f, ("zh", "y"), [(2 * zh + y, 2 * (y ^ j) + zh) for zh in range(2) for y in range(2)])
@@ -580,8 +589,10 @@
     w_across = lax.ppermute(wmsg, "y", [(0, 1), (1, 0)])
     a1, mine = call(
         bind(adjacency_first_body, z),
-        [((z.s1, blocks * z.t1), BF16), ((z.id_rows + CLASS_ROWS + 8, LANES), F32)], "adjacency_first", 4 + blocks,
-        us=6.0, scratch=tables(z, z.f1, z.l1, z.s1),
+        [
+            ((z.s1, blocks * z.t1), BF16), ((z.id_rows + CLASS_ROWS + 8, LANES), F32),
+        ],
+        "adjacency_first", 4 + blocks, us=6.0, scratch=tables(z, z.f1, z.l1, z.s1),
     )(ids)
     part = call(
         bind(first_body, z), [((blocks, 64, z.t1), F32)], "first", 4 + blocks, scratch=[pltpu.VMEM((128, z.s1), BF16)],

time: 142 us -> 140 us (0.986)
  waiting for transfers between devices: 10.3 us -> 5.2 us
  starting transfers between devices: 15 us -> 16.7 us
    all_to_all x1, waiting for transfers between devices: 5.37 us -> 2.32 us  [on_device(): ids = lax.all_to_all(ids, ('y', 'c', 'zh', 'rl'), 0, 0)]
    ppermute x1, waiting for transfers between devices: 4.94 us -> 2.86 us  [on_device(): other = lax.ppermute(own, 'zh', [(0, 1), (1, 0)])]
    ppermute x1, starting transfers between devices: 0.55 us -> 2.29 us  [on_device(): other = lax.ppermute(own, 'zh', [(0, 1), (1, 0)])]
    pallas_call x16 -> x17, Pallas kernels: 19.5 us -> 20.8 us  [run(): pl.pallas_call(placed, out_shape=[jax.ShapeDtypeStruct(s, d) for s, d in...]
  transfers between devices with their start and end apart: 9 -> 9, of which waited for: 2 -> 2; matrix products, arithmetic and copies ran while one was open for 0% -> 0% of each run, Pallas kernels for 6% -> 8%
where the time goes in v5:
time: 140 us; the launch traced here: 139 us
  blocking collectives  95.1 us (68%)
  Pallas kernels  20.8 us (15%)
  starting transfers between devices  16.7 us (12%)
  waiting for transfers between devices  5.2 us (4%)
    all_to_all x6, blocking collectives, exchange(): return lax.all_to_all(value, ('y', 'rl'), 0, 0)  84.8 us
    pallas_call x17, Pallas kernels, run(): pl.pallas_call(placed, out_shape=[jax.ShapeDtypeStruct(s, d) for s, d in...  20.8 us
    all_to_all x1, blocking collectives, on_device(): whole = lax.all_to_all(part, ('rl', 'y', 'c'), 0, 0)  10.3 us
    all_to_all x1, starting transfers between devices, on_device(): ids = lax.all_to_all(ids, ('y', 'c', 'zh', 'rl'), 0, 0)  7.3 us
    ppermute x2, starting transfers between devices, on_device(): lax.ppermute(f, ('zh', 'y'), [(2 * zh + y, 2 * (y ^ j) + zh) for zh in ra...  4.57 us
    ppermute x1, waiting for transfers between devices, on_device(): other = lax.ppermute(own, 'zh', [(0, 1), (1, 0)])  2.86 us
  transfers between devices with their start and end apart: 9, of which 2 were waited for; matrix products, arithmetic and copies ran while one was open for 0% of the time, Pallas kernels for 8%

profile of v5, /device:TPU:0, one launch (start us, length us, event | category | flops | bytes accessed | tf_op | source)
XLA Modules:
  0.0 139.0 jit_solution(12569012180568471146)
XLA Ops:
  0.7 1.6 %ids.1 = s32[32,16,128]{2,1,0:T(8,128)} custom-call(s32[5,2,512]{2,1,0:T(2,128)} %bitcast.28, s32[2,512]{1,0:T(2,128)} %refs_1_.2, s32[10,2,256]{2,1,0:T(2,128)} %bitcast.29, s32[2,256]{1,0:T(2,128)} %refs_3_.2, s32[15,2,128]{2,1,0:T(2,128)} %bitcast.30, s32[2,128]{1,0:T(2,128)} %refs_5_.2, s32[2,128]{1,0:T(2,128)} %refs_6_.1), custom_call_target="tpu_custom_call" | custom-call | bytes 3600000 | tf_op jit(solution)/shard_map/ids/pallas_call | solution.py:65
  2.3 7.3 %all-to-all-start = ((s32[32,16,128]{2,1,0:T(8,128)}), s32[32,16,128]{2,1,0:T(8,128)S(1)}, u32[]{:S(2)}, u32[]{:S(2)}) async-start(s32[32,16,128]{2,1,0:T(8,128)} %ids.1), calls=%async_computation | async-start | bytes 524288 | tf_op jit(solution)/shard_map/all_to_all | solution.py:588
  9.6 1.9 %prep.1 = (f32[32,1024]{1,0:T(8,128)}, f32[32,1024]{1,0:T(8,128)}, f32[248,256]{1,0:T(8,128)}) custom-call(f32[2,32,1024]{2,1,0:T(8,128)} %bitcast.27, f32[2,32,256]{2,1,0:T(8,128)} %refs_2_.3, f32[2,64,256]{2,1,0:T(8,128)} %refs_3_.3, f32[47,2,64]{2,1,0:T(2,128)} %bitcast.19, f32[2,64]{1,0:T(2,128)} %refs_5_.3), custom_call_target="tpu_custom_call" | custom-call | bytes 3600000 | tf_op jit(solution)/shard_map/prep/pallas_call | solution.py:65
  11.5 1.8 %collective-permute-start.2 = (f32[248,256]{1,0:T(8,128)}, f32[248,256]{1,0:T(8,128)S(1)}, u32[]{:S(2)}, u32[]{:S(2)}) collective-permute-start(f32[248,256]{1,0:T(8,128)} %get-tuple-element.69.refs_0_), channel_id=1, source_target_pairs={{0,2},{2,0},{1,3},{3,1},{4,6},{6,4},{5,7},{7,5},{8,10},{10,8},{9,1... | collective-permute-start | bytes 761864 | tf_op jit(solution)/shard_map/ppermute | solution.py:589
  13.3 1.6 %collective-permute-start = (f32[32,1024]{1,0:T(8,128)}, f32[32,1024]{1,0:T(8,128)S(1)}, u32[]{:S(2)}, u32[]{:S(2)}) collective-permute-start(f32[32,1024]{1,0:T(8,128)} %get-tuple-element.67), channel_id=1, source_target_pairs={{0,0},{2,16},{16,2},{18,18},{1,1},{3,17},{17,3},{19,19},{4,4},{6,2... | collective-permute-start | bytes 393224 | tf_op jit(solution)/shard_map/ppermute | solution.py:585
  14.9 3.0 %collective-permute-start.1 = (f32[32,1024]{1,0:T(8,128)}, f32[32,1024]{1,0:T(8,128)S(1)}, u32[]{:S(2)}, u32[]{:S(2)}) collective-permute-start(f32[32,1024]{1,0:T(8,128)} %get-tuple-element.68), channel_id=1, source_target_pairs={{0,16},{2,0},{16,18},{18,2},{1,17},{3,1},{17,19},{19,3},{4,20},{6,... | collective-permute-start | bytes 393224 | tf_op jit(solution)/shard_map/ppermute | solution.py:585
  17.9 2.3 %all-to-all-done.refs_0_ = s32[32,16,128]{2,1,0:T(8,128)S(1)} async-done(((s32[32,16,128]{2,1,0:T(8,128)}), s32[32,16,128]{2,1,0:T(8,128)S(1)}, u32[]{:S(2)}, u32[]{:S(2)}) %all-to-all-start) | async-done | bytes 262176 | tf_op jit(solution)/shard_map/all_to_all | solution.py:588
  20.2 4.6 %adjacency_first.1 = (bf16[1024,4096]{1,0:T(8,128)(2,1)S(1)}, f32[120,128]{1,0:T(8,128)S(1)}) custom-call(s32[32,16,128]{2,1,0:T(8,128)S(1)} %all-to-all-done.refs_0_), custom_call_target="tpu_custom_call" | custom-call | bytes 21600000 | tf_op jit(solution)/shard_map/adjacency_first/pallas_call | solution.py:65
  24.9 1.3 first.1
  26.1 19.7 %all_to_all.40.refs_1_ = f32[8,64,512]{2,1,0:T(8,128)S(1)} all-to-all(f32[8,64,512]{2,1,0:T(8,128)S(1)} %first.1), channel_id=1, replica_groups=mesh['zh'=2,'rl'=4,'y'=2,'c'=2] {'y','rl'}, dimensions={0} | all-to-all | bytes 2097152 | tf_op jit(solution)/shard_map/all_to_all | solution.py:567
  45.9 0.1 collective-permute-start.3
  46.0 0.5 collective-permute-start.5
  46.5 0.1 collective-permute-start.4
  46.6 2.5 %adjacency_mid.1.refs_5_.refs_1_ = bf16[512,2048]{1,0:T(8,128)(2,1)S(1)} custom-call(s32[32,16,128]{2,1,0:T(8,128)S(1)} %all-to-all-done.refs_0_, f32[128,512]{1,0:T(8,128)S(1)} %sum_first.1.refs_5_.refs_1_.refs_0_), custom_call_target="tpu_custom_call" | custom-call | bytes 10800000 | tf_op jit(solution)/shard_map/adjacency_mid/pallas_call | solution.py:65
  49.2 0.5 weights.1
  49.7 1.3 hidden_one.1
  51.0 18.7 %all_to_all.41.refs_1_ = f32[8,128,256]{2,1,0:T(8,128)S(1)} all-to-all(f32[8,128,256]{2,1,0:T(8,128)S(1)} %get-tuple-element.73), channel_id=1, replica_groups=mesh['zh'=2,'rl'=4,'y'=2,'c'=2] {'y','rl'}, dimensions={0} | all-to-all | bytes 2097152 | tf_op jit(solution)/shard_map/all_to_all | solution.py:567
  69.9 0.1 collective-permute-start.6
  70.0 1.4 adjacency_last.1.refs_7_.refs_3_
  71.4 1.2 hidden_two.1
  72.6 9.6 %all_to_all.42.refs_1_ = f32[8,48,128]{2,1,0:T(8,128)S(1)} all-to-all(f32[8,48,128]{2,1,0:T(8,128)S(1)} %get-tuple-element.78), channel_id=1, replica_groups=mesh['zh'=2,'rl'=4,'y'=2,'c'=2] {'y','rl'}, dimensions={0} | all-to-all | bytes 393216 | tf_op jit(solution)/shard_map/all_to_all | solution.py:567
  82.2 0.2 logits.1
  82.4 9.0 %all_to_all.43.refs_1_ = f32[8,48,128]{2,1,0:T(8,128)S(1)} all-to-all(f32[8,48,128]{2,1,0:T(8,128)S(1)} %get-tuple-element.80), channel_id=1, replica_groups=mesh['zh'=2,'rl'=4,'y'=2,'c'=2] {'y','rl'}, dimensions={0} | all-to-all | bytes 393216 | tf_op jit(solution)/shard_map/all_to_all | solution.py:567
  91.4 1.2 back_last.1
  92.6 16.7 %all_to_all.44.refs_0_ = f32[8,128,256]{2,1,0:T(8,128)S(1)} all-to-all(f32[8,128,256]{2,1,0:T(8,128)S(1)} %get-tuple-element.87), channel_id=1, replica_groups=mesh['zh'=2,'rl'=4,'y'=2,'c'=2] {'y','rl'}, dimensions={0} | all-to-all | bytes 2097152 | tf_op jit(solution)/shard_map/all_to_all | solution.py:567
  109.2 1.6 %grads.1 = f32[8,112,128]{2,1,0:T(8,128)S(1)} custom-call(f32[8,128,256]{2,1,0:T(8,128)S(1)} %all_to_all.44.refs_0_, bf16[512,2048]{1,0:T(8,128)(2,1)S(1)} %adjacency_mid.1.refs_5_.refs_1_, f32[256,256]{1,0:T(8,128)S(1)} %get-tuple-element.88.refs_2_, bf16[2,256,256]{2,1,0:T(8,128)(2,1)S(1)} %get-tuple-element.85.refs_7_.refs_3_, ...), custom_call_target="tpu_custom_call" | custom-call | bytes 3600000 | tf_op jit(solution)/shard_map/grads/pallas_call | solution.py:65
  110.8 11.0 %all_to_all.45.refs_0_ = f32[8,112,128]{2,1,0:T(8,128)S(1)} all-to-all(f32[8,112,128]{2,1,0:T(8,128)S(1)} %grads.1), channel_id=1, replica_groups=mesh['zh'=2,'rl'=4,'y'=2,'c'=2] {'y','rl'}, dimensions={0} | all-to-all | bytes 917504 | tf_op jit(solution)/shard_map/all_to_all | solution.py:567
  121.9 2.3 %collective-permute-start.7 = (f32[112,128]{1,0:T(8,128)S(1)}, f32[112,128]{1,0:T(8,128)S(1)}, u32[]{:S(2)}, u32[]{:S(2)}) collective-permute-start(f32[112,128]{1,0:T(8,128)S(1)} %sum_grads.1.refs_0_), channel_id=1, source_target_pairs={{0,16},{16,0},{1,17},{17,1},{2,18},{18,2},{3,19},{19,3},{4,20},{20... | collective-permute-start | bytes 172040 | tf_op jit(solution)/shard_map/ppermute | solution.py:658
  124.2 2.9 %collective-permute-done.7.refs_1_ = f32[112,128]{1,0:T(8,128)S(1)} collective-permute-done((f32[112,128]{1,0:T(8,128)S(1)}, f32[112,128]{1,0:T(8,128)S(1)}, u32[]{:S(2)}, u32[]{:S(2)}) %collective-permute-start.7) | collective-permute-done | bytes 57376 | tf_op jit(solution)/shard_map/ppermute | solution.py:658
  127.0 0.1 share.1
  127.2 10.3 %all_to_all.46.refs_0_ = f32[16,32,128]{2,1,0:T(8,128)S(1)} all-to-all(f32[16,32,128]{2,1,0:T(8,128)S(1)} %share.1), channel_id=1, replica_groups=mesh['zh'=2,'rl'=4,'y'=2,'c'=2] {'rl','y','c'}, dimensions={0} | all-to-all | bytes 524288 | tf_op jit(solution)/shard_map/all_to_all | solution.py:660
  137.6 1.4 update.1
  (42 shorter events, 0.3 us)
Async XLA Ops:
  2.3 18.0 %all-to-all-start = ((s32[32,16,128]{2,1,0:T(8,128)}), s32[32,16,128]{2,1,0:T(8,128)S(1)}, u32[]{:S(2)}, u32[]{:S(2)}) async-start(s32[32,16,128]{2,1,0:T(8,128)} %ids.1), calls=%async_computation | async-start | bytes 524288 | tf_op jit(solution)/shard_map/all_to_all | solution.py:588
  11.5 34.5 %copy-start.2 = (f32[248,256]{1,0:T(8,128)S(1)}, f32[248,256]{1,0:T(8,128)}, u32[]{:S(2)}) copy-start(f32[248,256]{1,0:T(8,128)} %get-tuple-element.69.refs_0_) | copy-start | bytes 761860
  11.5 37.7 %copy-start.11 = (f32[47]{0:T(128)S(1)}, f32[47]{0:T(128)}, u32[]{:S(2)}) copy-start(f32[47]{0:T(128)} %param.35) | copy-start | bytes 568
  11.5 13.3 %collective-permute-start.2 = (f32[248,256]{1,0:T(8,128)}, f32[248,256]{1,0:T(8,128)S(1)}, u32[]{:S(2)}, u32[]{:S(2)}) collective-permute-start(f32[248,256]{1,0:T(8,128)} %get-tuple-element.69.refs_0_), channel_id=1, source_target_pairs={{0,2},{2,0},{1,3},{3,1},{4,6},{6,4},{5,7},{7,5},{8,10},{10,8},{9,1... | collective-permute-start | bytes 761864 | tf_op jit(solution)/shard_map/ppermute | solution.py:589
  13.3 11.5 %collective-permute-start = (f32[32,1024]{1,0:T(8,128)}, f32[32,1024]{1,0:T(8,128)S(1)}, u32[]{:S(2)}, u32[]{:S(2)}) collective-permute-start(f32[32,1024]{1,0:T(8,128)} %get-tuple-element.67), channel_id=1, source_target_pairs={{0,0},{2,16},{16,2},{18,18},{1,1},{3,17},{17,3},{19,19},{4,4},{6,2... | collective-permute-start | bytes 393224 | tf_op jit(solution)/shard_map/ppermute | solution.py:585
  14.9 9.9 %collective-permute-start.1 = (f32[32,1024]{1,0:T(8,128)}, f32[32,1024]{1,0:T(8,128)S(1)}, u32[]{:S(2)}, u32[]{:S(2)}) collective-permute-start(f32[32,1024]{1,0:T(8,128)} %get-tuple-element.68), channel_id=1, source_target_pairs={{0,16},{2,0},{16,18},{18,2},{1,17},{3,1},{17,19},{19,3},{4,20},{6,... | collective-permute-start | bytes 393224 | tf_op jit(solution)/shard_map/ppermute | solution.py:585
  45.9 3.8 %collective-permute-start.3 = (f32[128,512]{1,0:T(8,128)S(1)}, f32[128,512]{1,0:T(8,128)S(1)}, u32[]{:S(2)}, u32[]{:S(2)}) collective-permute-start(f32[128,512]{1,0:T(8,128)S(1)} %sum_first.1.refs_5_.refs_1_.refs_0_), channel_id=1, source_target_pairs={{0,1},{1,0},{2,3},{3,2},{4,5},{5,4},{6,7},{7,6},{8,9},{9,8},{10,11... | collective-permute-start | bytes 786440 | tf_op jit(solution)/shard_map/ppermute | solution.py:564
  46.0 3.1 %collective-permute-start.5 = (f32[248,256]{1,0:T(8,128)S(1)}, f32[248,256]{1,0:T(8,128)S(1)}, u32[]{:S(2)}, u32[]{:S(2)}) collective-permute-start(f32[248,256]{1,0:T(8,128)S(1)} %copy-done.2), channel_id=1, source_target_pairs={{0,1},{1,0},{2,3},{3,2},{4,5},{5,4},{6,7},{7,6},{8,9},{9,8},{10,11... | collective-permute-start | bytes 761864 | tf_op jit(solution)/shard_map/ppermute | solution.py:564
  46.5 2.6 %collective-permute-start.4 = (f32[248,256]{1,0:T(8,128)S(1)}, f32[248,256]{1,0:T(8,128)S(1)}, u32[]{:S(2)}, u32[]{:S(2)}) collective-permute-start(f32[248,256]{1,0:T(8,128)S(1)} %collective-permute-done.2.refs_3_.refs_1_), channel_id=1, source_target_pairs={{0,1},{1,0},{2,3},{3,2},{4,5},{5,4},{6,7},{7,6},{8,9},{9,8},{10,11... | collective-permute-start | bytes 761864 | tf_op jit(solution)/shard_map/ppermute | solution.py:564
  69.7 67.8 %copy-start = (f32[2,64,256]{2,1,0:T(8,128)S(1)}, f32[2,64,256]{2,1,0:T(8,128)}, u32[]{:S(2)}) copy-start(f32[2,64,256]{2,1,0:T(8,128)} %refs_3_.3) | copy-start | bytes 393220
  69.7 67.7 %copy-start.1 = (f32[2,32,256]{2,1,0:T(8,128)S(1)}, f32[2,32,256]{2,1,0:T(8,128)}, u32[]{:S(2)}) copy-start(f32[2,32,256]{2,1,0:T(8,128)} %refs_2_.3) | copy-start | bytes 196612
  69.7 67.7 %copy-start.3 = (f32[2,64,47]{1,0,2:T(2,128)S(1)}, f32[2,64,47]{1,0,2:T(2,128)}, u32[]{:S(2)}) copy-start(f32[2,64,47]{1,0,2:T(2,128)} %param.33) | copy-start | bytes 72196
  69.8 67.7 %copy-start.4 = (f32[2,64,256]{2,1,0:T(8,128)S(1)}, f32[2,64,256]{2,1,0:T(8,128)}, u32[]{:S(2)}) copy-start(f32[2,64,256]{2,1,0:T(8,128)} %refs_8_.1) | copy-start | bytes 393220
  69.8 67.7 %copy-start.5 = (f32[2,64,256]{2,1,0:T(8,128)S(1)}, f32[2,64,256]{2,1,0:T(8,128)}, u32[]{:S(2)}) copy-start(f32[2,64,256]{2,1,0:T(8,128)} %refs_13_.1) | copy-start | bytes 393220
  69.8 67.7 %copy-start.6 = (f32[2,32,256]{2,1,0:T(8,128)S(1)}, f32[2,32,256]{2,1,0:T(8,128)}, u32[]{:S(2)}) copy-start(f32[2,32,256]{2,1,0:T(8,128)} %refs_7_.1) | copy-start | bytes 196612
  69.8 67.7 %copy-start.7 = (f32[2,32,256]{2,1,0:T(8,128)S(1)}, f32[2,32,256]{2,1,0:T(8,128)}, u32[]{:S(2)}) copy-start(f32[2,32,256]{2,1,0:T(8,128)} %refs_12_.1) | copy-start | bytes 196612
  69.8 67.7 %copy-start.8 = (f32[2,64,47]{1,0,2:T(2,128)S(1)}, f32[2,64,47]{1,0,2:T(2,128)}, u32[]{:S(2)}) copy-start(f32[2,64,47]{1,0,2:T(2,128)} %param.38) | copy-start | bytes 72196
  69.8 67.7 %copy-start.9 = (f32[2,64,47]{1,0,2:T(2,128)S(1)}, f32[2,64,47]{1,0,2:T(2,128)}, u32[]{:S(2)}) copy-start(f32[2,64,47]{1,0,2:T(2,128)} %param.43) | copy-start | bytes 72196
  69.8 67.7 %copy-start.10 = (f32[2,64]{1,0:T(2,128)S(1)}, f32[2,64]{1,0:T(2,128)}, u32[]{:S(2)}) copy-start(f32[2,64]{1,0:T(2,128)} %refs_5_.3) | copy-start | bytes 1540
  69.8 67.7 %copy-start.12 = (f32[2,64]{1,0:T(2,128)S(1)}, f32[2,64]{1,0:T(2,128)}, u32[]{:S(2)}) copy-start(f32[2,64]{1,0:T(2,128)} %refs_10_.1) | copy-start | bytes 1540
  69.9 67.7 %copy-start.13 = (f32[2,64]{1,0:T(2,128)S(1)}, f32[2,64]{1,0:T(2,128)}, u32[]{:S(2)}) copy-start(f32[2,64]{1,0:T(2,128)} %refs_15_.1) | copy-start | bytes 1540
  69.9 67.7 %copy-start.14 = (f32[47]{0:T(128)S(1)}, f32[47]{0:T(128)}, u32[]{:S(2)}) copy-start(f32[47]{0:T(128)} %param.40) | copy-start | bytes 568
  69.9 67.7 %copy-start.15 = (f32[47]{0:T(128)S(1)}, f32[47]{0:T(128)}, u32[]{:S(2)}) copy-start(f32[47]{0:T(128)} %param.45) | copy-start | bytes 568
  69.9 1.5 %collective-permute-start.6 = (f32[128,256]{1,0:T(8,128)S(1)}, f32[128,256]{1,0:T(8,128)S(1)}, u32[]{:S(2)}, u32[]{:S(2)}) collective-permute-start(f32[128,256]{1,0:T(8,128)S(1)} %sum_mid.1.refs_1_.refs_0_), channel_id=1, source_target_pairs={{0,1},{1,0},{2,3},{3,2},{4,5},{5,4},{6,7},{7,6},{8,9},{9,8},{10,11... | collective-permute-start | bytes 393224 | tf_op jit(solution)/shard_map/ppermute | solution.py:564
  121.9 5.1 %collective-permute-start.7 = (f32[112,128]{1,0:T(8,128)S(1)}, f32[112,128]{1,0:T(8,128)S(1)}, u32[]{:S(2)}, u32[]{:S(2)}) collective-permute-start(f32[112,128]{1,0:T(8,128)S(1)} %sum_grads.1.refs_0_), channel_id=1, source_target_pairs={{0,16},{16,0},{1,17},{17,1},{2,18},{18,2},{3,19},{19,3},{4,20},{20... | collective-permute-start | bytes 172040 | tf_op jit(solution)/shard_map/ppermute | solution.py:658

commit v6 on v5

--- a/solution.py
+++ b/solution.py
@@ -328,11 +328,22 @@
 def hidden_one_body(z, pos, own, other, w1h, w1l, bias, a2, out, x1, h1, slope):
     c = pos[3]
     put_columns(pos, own, other, x1)
-    pre = dot_split((w1h[...], w1l[...]), halves(x1[...]), NN) + bias[:, 0:1]
-    sigma = sigmoid(pre)
-    h1[...] = pre * sigma
+    high, low = halves(x1[...])
+
+    def layer(rows, lanes):
+        pre = dot_split((w1h[rows, :], w1l[rows, :]), (high[:, :lanes], low[:, :lanes]), NN) + bias[rows, 0:1]
+        sigma = sigmoid(pre)
+        return pre, sigma
+
+    mine = pl.ds(pl.multiple_of(c * 128, 128), 128)
+    rest = pl.ds(pl.multiple_of((1 - c) * 128, 128), 128)
+    pre, sigma = layer(mine, z.t1)
+    hidden = pre * sigma
     slope[...] = sigma * (1.0 + pre * (1.0 - sigma))
-    table = jnp.concatenate(halves(h1[pl.ds(pl.multiple_of(c * 128, 128), 128)]), axis=0)
+    h1[mine] = hidden[:, : z.t2]
+    table = jnp.concatenate(halves(hidden), axis=0)
+    pre, sigma = layer(rest, z.t2)
+    h1[rest] = pre * sigma
     for r in range(2 * z.rl):
         both = dot(table, a2[:, r * z.t2 : (r + 1) * z.t2], NN)
         out[r] = both[:128] + both[128:]
@@ -347,7 +358,7 @@
 
 def hidden_two_body(z, pos, own, other, h1, w2h, w2l, bias, wlt, a3, out, y2, h2, slope, local):
     c = pos[3]
-    y2[:256] = h1[:, : z.t2]
+    y2[:256] = h1[...]
     y2[pl.ds(pl.multiple_of(256 + c * 128, 128), 128)] = own[...]
     y2[pl.ds(pl.multiple_of(256 + (1 - c) * 128, 128), 128)] = other[...]
     pre = dot_split((w2h[...], w2l[...]), halves(y2[...]), NN) + bias[:, 1:2]
@@ -428,7 +439,7 @@
     dh = both[:128] + both[128:]
     at_own = dot_split((wmh[0, mine, :], wml[0, mine, :]), halves(dpre2[...]), NN)
     dh = dh + jnp.concatenate([at_own, jnp.zeros((128, z.t1 - z.t2), F32)], axis=1)
-    dpre1 = dh * slope[mine]
+    dpre1 = dh * slope[...]
     half2 = dpre2[mine]
     first[...] = dot_full(x1[...], dpre1, NT)
     mid[...] = dot_full(y2[...], half2, NT)
@@ -617,7 +628,7 @@
     )(ids, half)[0]
     part, x1, h1, slope1 = call(
         bind(hidden_one_body, z),
-        [((blocks, 128, z.t2), F32), ((256, z.t1), F32), ((256, z.t1), F32), ((256, z.t1), F32)],
+        [((blocks, 128, z.t2), F32), ((256, z.t1), F32), ((256, z.t2), F32), ((128, z.t1), F32)],
         "hidden_one", 16,
     )(half, other, w1h, w1l, bias, a2)
     part = exchange(part)

time: 140 us -> 139 us (level)
  no operation moved by 1% of the time
where the time goes in v6:
time: 139 us
  blocking collectives  95.1 us (68%)
  Pallas kernels  20.7 us (15%)
  starting transfers between devices  16.7 us (12%)
  waiting for transfers between devices  5.21 us (4%)
    all_to_all x6, blocking collectives, exchange(): return lax.all_to_all(value, ('y', 'rl'), 0, 0)  84.8 us
    pallas_call x17, Pallas kernels, run(): pl.pallas_call(placed, out_shape=[jax.ShapeDtypeStruct(s, d) for s, d in...  20.7 us
    all_to_all x1, blocking collectives, on_device(): whole = lax.all_to_all(part, ('rl', 'y', 'c'), 0, 0)  10.3 us
    all_to_all x1, starting transfers between devices, on_device(): ids = lax.all_to_all(ids, ('y', 'c', 'zh', 'rl'), 0, 0)  7.3 us
    ppermute x2, starting transfers between devices, on_device(): lax.ppermute(f, ('zh', 'y'), [(2 * zh + y, 2 * (y ^ j) + zh) for zh in ra...  4.57 us
    ppermute x1, waiting for transfers between devices, on_device(): other = lax.ppermute(own, 'zh', [(0, 1), (1, 0)])  2.87 us
  transfers between devices with their start and end apart: 9, of which 2 were waited for; matrix products, arithmetic and copies ran while one was open for 0% of the time, Pallas kernels for 8%

profile of v6, /device:TPU:0, one launch (start us, length us, event | category | flops | bytes accessed | tf_op | source)
XLA Modules:
  0.0 138.9 jit_solution(17364046495454765250)
XLA Ops:
  0.7 1.6 %ids.1 = s32[32,16,128]{2,1,0:T(8,128)} custom-call(s32[5,2,512]{2,1,0:T(2,128)} %bitcast.28, s32[2,512]{1,0:T(2,128)} %refs_1_.2, s32[10,2,256]{2,1,0:T(2,128)} %bitcast.29, s32[2,256]{1,0:T(2,128)} %refs_3_.2, s32[15,2,128]{2,1,0:T(2,128)} %bitcast.30, s32[2,128]{1,0:T(2,128)} %refs_5_.2, s32[2,128]{1,0:T(2,128)} %refs_6_.1), custom_call_target="tpu_custom_call" | custom-call | bytes 3600000 | tf_op jit(solution)/shard_map/ids/pallas_call | solution.py:65
  2.3 7.3 %all-to-all-start = ((s32[32,16,128]{2,1,0:T(8,128)}), s32[32,16,128]{2,1,0:T(8,128)S(1)}, u32[]{:S(2)}, u32[]{:S(2)}) async-start(s32[32,16,128]{2,1,0:T(8,128)} %ids.1), calls=%async_computation | async-start | bytes 524288 | tf_op jit(solution)/shard_map/all_to_all | solution.py:599
  9.6 1.9 %prep.1 = (f32[32,1024]{1,0:T(8,128)}, f32[32,1024]{1,0:T(8,128)}, f32[248,256]{1,0:T(8,128)}) custom-call(f32[2,32,1024]{2,1,0:T(8,128)} %bitcast.27, f32[2,32,256]{2,1,0:T(8,128)} %refs_2_.3, f32[2,64,256]{2,1,0:T(8,128)} %refs_3_.3, f32[47,2,64]{2,1,0:T(2,128)} %bitcast.19, f32[2,64]{1,0:T(2,128)} %refs_5_.3), custom_call_target="tpu_custom_call" | custom-call | bytes 3600000 | tf_op jit(solution)/shard_map/prep/pallas_call | solution.py:65
  11.5 1.8 %collective-permute-start.2 = (f32[248,256]{1,0:T(8,128)}, f32[248,256]{1,0:T(8,128)S(1)}, u32[]{:S(2)}, u32[]{:S(2)}) collective-permute-start(f32[248,256]{1,0:T(8,128)} %get-tuple-element.69.refs_0_), channel_id=1, source_target_pairs={{0,2},{2,0},{1,3},{3,1},{4,6},{6,4},{5,7},{7,5},{8,10},{10,8},{9,1... | collective-permute-start | bytes 761864 | tf_op jit(solution)/shard_map/ppermute | solution.py:600
  13.3 1.6 %collective-permute-start = (f32[32,1024]{1,0:T(8,128)}, f32[32,1024]{1,0:T(8,128)S(1)}, u32[]{:S(2)}, u32[]{:S(2)}) collective-permute-start(f32[32,1024]{1,0:T(8,128)} %get-tuple-element.67), channel_id=1, source_target_pairs={{0,0},{2,16},{16,2},{18,18},{1,1},{3,17},{17,3},{19,19},{4,4},{6,2... | collective-permute-start | bytes 393224 | tf_op jit(solution)/shard_map/ppermute | solution.py:596
  14.9 3.0 %collective-permute-start.1 = (f32[32,1024]{1,0:T(8,128)}, f32[32,1024]{1,0:T(8,128)S(1)}, u32[]{:S(2)}, u32[]{:S(2)}) collective-permute-start(f32[32,1024]{1,0:T(8,128)} %get-tuple-element.68), channel_id=1, source_target_pairs={{0,16},{2,0},{16,18},{18,2},{1,17},{3,1},{17,19},{19,3},{4,20},{6,... | collective-permute-start | bytes 393224 | tf_op jit(solution)/shard_map/ppermute | solution.py:596
  17.9 2.3 %all-to-all-done.refs_0_ = s32[32,16,128]{2,1,0:T(8,128)S(1)} async-done(((s32[32,16,128]{2,1,0:T(8,128)}), s32[32,16,128]{2,1,0:T(8,128)S(1)}, u32[]{:S(2)}, u32[]{:S(2)}) %all-to-all-start) | async-done | bytes 262176 | tf_op jit(solution)/shard_map/all_to_all | solution.py:599
  20.2 4.6 %adjacency_first.1 = (bf16[1024,4096]{1,0:T(8,128)(2,1)S(1)}, f32[120,128]{1,0:T(8,128)S(1)}) custom-call(s32[32,16,128]{2,1,0:T(8,128)S(1)} %all-to-all-done.refs_0_), custom_call_target="tpu_custom_call" | custom-call | bytes 21600000 | tf_op jit(solution)/shard_map/adjacency_first/pallas_call | solution.py:65
  24.9 1.3 first.1
  26.1 19.7 %all_to_all.40.refs_1_ = f32[8,64,512]{2,1,0:T(8,128)S(1)} all-to-all(f32[8,64,512]{2,1,0:T(8,128)S(1)} %first.1), channel_id=1, replica_groups=mesh['zh'=2,'rl'=4,'y'=2,'c'=2] {'y','rl'}, dimensions={0} | all-to-all | bytes 2097152 | tf_op jit(solution)/shard_map/all_to_all | solution.py:578
  45.9 0.1 collective-permute-start.3
  46.0 0.5 collective-permute-start.5
  46.5 0.1 collective-permute-start.4
  46.6 2.5 %adjacency_mid.1.refs_5_.refs_1_ = bf16[512,2048]{1,0:T(8,128)(2,1)S(1)} custom-call(s32[32,16,128]{2,1,0:T(8,128)S(1)} %all-to-all-done.refs_0_, f32[128,512]{1,0:T(8,128)S(1)} %sum_first.1.refs_5_.refs_1_.refs_0_), custom_call_target="tpu_custom_call" | custom-call | bytes 10800000 | tf_op jit(solution)/shard_map/adjacency_mid/pallas_call | solution.py:65
  49.2 0.5 weights.1
  49.7 1.2 hidden_one.1
  50.9 18.7 %all_to_all.41.refs_1_ = f32[8,128,256]{2,1,0:T(8,128)S(1)} all-to-all(f32[8,128,256]{2,1,0:T(8,128)S(1)} %get-tuple-element.73), channel_id=1, replica_groups=mesh['zh'=2,'rl'=4,'y'=2,'c'=2] {'y','rl'}, dimensions={0} | all-to-all | bytes 2097152 | tf_op jit(solution)/shard_map/all_to_all | solution.py:578
  69.8 0.1 collective-permute-start.6
  69.9 1.4 adjacency_last.1.refs_7_.refs_3_
  71.3 1.2 hidden_two.1
  72.5 9.6 %all_to_all.42.refs_1_ = f32[8,48,128]{2,1,0:T(8,128)S(1)} all-to-all(f32[8,48,128]{2,1,0:T(8,128)S(1)} %get-tuple-element.78), channel_id=1, replica_groups=mesh['zh'=2,'rl'=4,'y'=2,'c'=2] {'y','rl'}, dimensions={0} | all-to-all | bytes 393216 | tf_op jit(solution)/shard_map/all_to_all | solution.py:578
  82.1 0.2 logits.1
  82.3 9.0 %all_to_all.43.refs_1_ = f32[8,48,128]{2,1,0:T(8,128)S(1)} all-to-all(f32[8,48,128]{2,1,0:T(8,128)S(1)} %get-tuple-element.80), channel_id=1, replica_groups=mesh['zh'=2,'rl'=4,'y'=2,'c'=2] {'y','rl'}, dimensions={0} | all-to-all | bytes 393216 | tf_op jit(solution)/shard_map/all_to_all | solution.py:578
  91.3 1.2 back_last.1
  92.5 16.7 %all_to_all.44.refs_0_ = f32[8,128,256]{2,1,0:T(8,128)S(1)} all-to-all(f32[8,128,256]{2,1,0:T(8,128)S(1)} %get-tuple-element.87), channel_id=1, replica_groups=mesh['zh'=2,'rl'=4,'y'=2,'c'=2] {'y','rl'}, dimensions={0} | all-to-all | bytes 2097152 | tf_op jit(solution)/shard_map/all_to_all | solution.py:578
  109.2 1.6 %grads.1 = f32[8,112,128]{2,1,0:T(8,128)S(1)} custom-call(f32[8,128,256]{2,1,0:T(8,128)S(1)} %all_to_all.44.refs_0_, bf16[512,2048]{1,0:T(8,128)(2,1)S(1)} %adjacency_mid.1.refs_5_.refs_1_, f32[256,256]{1,0:T(8,128)S(1)} %get-tuple-element.88.refs_2_, bf16[2,256,256]{2,1,0:T(8,128)(2,1)S(1)} %get-tuple-element.85.refs_7_.refs_3_, ...), custom_call_target="tpu_custom_call" | custom-call | bytes 3600000 | tf_op jit(solution)/shard_map/grads/pallas_call | solution.py:65
  110.7 11.0 %all_to_all.45.refs_0_ = f32[8,112,128]{2,1,0:T(8,128)S(1)} all-to-all(f32[8,112,128]{2,1,0:T(8,128)S(1)} %grads.1), channel_id=1, replica_groups=mesh['zh'=2,'rl'=4,'y'=2,'c'=2] {'y','rl'}, dimensions={0} | all-to-all | bytes 917504 | tf_op jit(solution)/shard_map/all_to_all | solution.py:578
  121.8 2.3 %collective-permute-start.7 = (f32[112,128]{1,0:T(8,128)S(1)}, f32[112,128]{1,0:T(8,128)S(1)}, u32[]{:S(2)}, u32[]{:S(2)}) collective-permute-start(f32[112,128]{1,0:T(8,128)S(1)} %sum_grads.1.refs_0_), channel_id=1, source_target_pairs={{0,16},{16,0},{1,17},{17,1},{2,18},{18,2},{3,19},{19,3},{4,20},{20... | collective-permute-start | bytes 172040 | tf_op jit(solution)/shard_map/ppermute | solution.py:669
  124.1 2.9 %collective-permute-done.7.refs_1_ = f32[112,128]{1,0:T(8,128)S(1)} collective-permute-done((f32[112,128]{1,0:T(8,128)S(1)}, f32[112,128]{1,0:T(8,128)S(1)}, u32[]{:S(2)}, u32[]{:S(2)}) %collective-permute-start.7) | collective-permute-done | bytes 57376 | tf_op jit(solution)/shard_map/ppermute | solution.py:669
  127.0 0.1 share.1
  127.1 10.3 %all_to_all.46.refs_0_ = f32[16,32,128]{2,1,0:T(8,128)S(1)} all-to-all(f32[16,32,128]{2,1,0:T(8,128)S(1)} %share.1), channel_id=1, replica_groups=mesh['zh'=2,'rl'=4,'y'=2,'c'=2] {'rl','y','c'}, dimensions={0} | all-to-all | bytes 524288 | tf_op jit(solution)/shard_map/all_to_all | solution.py:671
  137.5 1.4 update.1
  (42 shorter events, 0.3 us)
Async XLA Ops:
  2.3 18.0 %all-to-all-start = ((s32[32,16,128]{2,1,0:T(8,128)}), s32[32,16,128]{2,1,0:T(8,128)S(1)}, u32[]{:S(2)}, u32[]{:S(2)}) async-start(s32[32,16,128]{2,1,0:T(8,128)} %ids.1), calls=%async_computation | async-start | bytes 524288 | tf_op jit(solution)/shard_map/all_to_all | solution.py:599
  11.5 34.5 %copy-start.2 = (f32[248,256]{1,0:T(8,128)S(1)}, f32[248,256]{1,0:T(8,128)}, u32[]{:S(2)}) copy-start(f32[248,256]{1,0:T(8,128)} %get-tuple-element.69.refs_0_) | copy-start | bytes 761860
  11.5 37.7 %copy-start.11 = (f32[47]{0:T(128)S(1)}, f32[47]{0:T(128)}, u32[]{:S(2)}) copy-start(f32[47]{0:T(128)} %param.35) | copy-start | bytes 568
  11.5 13.3 %collective-permute-start.2 = (f32[248,256]{1,0:T(8,128)}, f32[248,256]{1,0:T(8,128)S(1)}, u32[]{:S(2)}, u32[]{:S(2)}) collective-permute-start(f32[248,256]{1,0:T(8,128)} %get-tuple-element.69.refs_0_), channel_id=1, source_target_pairs={{0,2},{2,0},{1,3},{3,1},{4,6},{6,4},{5,7},{7,5},{8,10},{10,8},{9,1... | collective-permute-start | bytes 761864 | tf_op jit(solution)/shard_map/ppermute | solution.py:600
  13.3 11.5 %collective-permute-start = (f32[32,1024]{1,0:T(8,128)}, f32[32,1024]{1,0:T(8,128)S(1)}, u32[]{:S(2)}, u32[]{:S(2)}) collective-permute-start(f32[32,1024]{1,0:T(8,128)} %get-tuple-element.67), channel_id=1, source_target_pairs={{0,0},{2,16},{16,2},{18,18},{1,1},{3,17},{17,3},{19,19},{4,4},{6,2... | collective-permute-start | bytes 393224 | tf_op jit(solution)/shard_map/ppermute | solution.py:596
  14.9 9.9 %collective-permute-start.1 = (f32[32,1024]{1,0:T(8,128)}, f32[32,1024]{1,0:T(8,128)S(1)}, u32[]{:S(2)}, u32[]{:S(2)}) collective-permute-start(f32[32,1024]{1,0:T(8,128)} %get-tuple-element.68), channel_id=1, source_target_pairs={{0,16},{2,0},{16,18},{18,2},{1,17},{3,1},{17,19},{19,3},{4,20},{6,... | collective-permute-start | bytes 393224 | tf_op jit(solution)/shard_map/ppermute | solution.py:596
  45.9 3.8 %collective-permute-start.3 = (f32[128,512]{1,0:T(8,128)S(1)}, f32[128,512]{1,0:T(8,128)S(1)}, u32[]{:S(2)}, u32[]{:S(2)}) collective-permute-start(f32[128,512]{1,0:T(8,128)S(1)} %sum_first.1.refs_5_.refs_1_.refs_0_), channel_id=1, source_target_pairs={{0,1},{1,0},{2,3},{3,2},{4,5},{5,4},{6,7},{7,6},{8,9},{9,8},{10,11... | collective-permute-start | bytes 786440 | tf_op jit(solution)/shard_map/ppermute | solution.py:575
  46.0 3.1 %collective-permute-start.5 = (f32[248,256]{1,0:T(8,128)S(1)}, f32[248,256]{1,0:T(8,128)S(1)}, u32[]{:S(2)}, u32[]{:S(2)}) collective-permute-start(f32[248,256]{1,0:T(8,128)S(1)} %copy-done.2), channel_id=1, source_target_pairs={{0,1},{1,0},{2,3},{3,2},{4,5},{5,4},{6,7},{7,6},{8,9},{9,8},{10,11... | collective-permute-start | bytes 761864 | tf_op jit(solution)/shard_map/ppermute | solution.py:575
  46.5 2.6 %collective-permute-start.4 = (f32[248,256]{1,0:T(8,128)S(1)}, f32[248,256]{1,0:T(8,128)S(1)}, u32[]{:S(2)}, u32[]{:S(2)}) collective-permute-start(f32[248,256]{1,0:T(8,128)S(1)} %collective-permute-done.2.refs_3_.refs_1_), channel_id=1, source_target_pairs={{0,1},{1,0},{2,3},{3,2},{4,5},{5,4},{6,7},{7,6},{8,9},{9,8},{10,11... | collective-permute-start | bytes 761864 | tf_op jit(solution)/shard_map/ppermute | solution.py:575
  69.6 67.8 %copy-start = (f32[2,64,256]{2,1,0:T(8,128)S(1)}, f32[2,64,256]{2,1,0:T(8,128)}, u32[]{:S(2)}) copy-start(f32[2,64,256]{2,1,0:T(8,128)} %refs_3_.3) | copy-start | bytes 393220
  69.7 67.8 %copy-start.1 = (f32[2,32,256]{2,1,0:T(8,128)S(1)}, f32[2,32,256]{2,1,0:T(8,128)}, u32[]{:S(2)}) copy-start(f32[2,32,256]{2,1,0:T(8,128)} %refs_2_.3) | copy-start | bytes 196612
  69.7 67.7 %copy-start.3 = (f32[2,64,47]{1,0,2:T(2,128)S(1)}, f32[2,64,47]{1,0,2:T(2,128)}, u32[]{:S(2)}) copy-start(f32[2,64,47]{1,0,2:T(2,128)} %param.33) | copy-start | bytes 72196
  69.7 67.7 %copy-start.4 = (f32[2,64,256]{2,1,0:T(8,128)S(1)}, f32[2,64,256]{2,1,0:T(8,128)}, u32[]{:S(2)}) copy-start(f32[2,64,256]{2,1,0:T(8,128)} %refs_8_.1) | copy-start | bytes 393220
  69.7 67.7 %copy-start.5 = (f32[2,64,256]{2,1,0:T(8,128)S(1)}, f32[2,64,256]{2,1,0:T(8,128)}, u32[]{:S(2)}) copy-start(f32[2,64,256]{2,1,0:T(8,128)} %refs_13_.1) | copy-start | bytes 393220
  69.7 67.7 %copy-start.6 = (f32[2,32,256]{2,1,0:T(8,128)S(1)}, f32[2,32,256]{2,1,0:T(8,128)}, u32[]{:S(2)}) copy-start(f32[2,32,256]{2,1,0:T(8,128)} %refs_7_.1) | copy-start | bytes 196612
  69.7 67.7 %copy-start.7 = (f32[2,32,256]{2,1,0:T(8,128)S(1)}, f32[2,32,256]{2,1,0:T(8,128)}, u32[]{:S(2)}) copy-start(f32[2,32,256]{2,1,0:T(8,128)} %refs_12_.1) | copy-start | bytes 196612
  69.7 67.7 %copy-start.8 = (f32[2,64,47]{1,0,2:T(2,128)S(1)}, f32[2,64,47]{1,0,2:T(2,128)}, u32[]{:S(2)}) copy-start(f32[2,64,47]{1,0,2:T(2,128)} %param.38) | copy-start | bytes 72196
  69.7 67.7 %copy-start.9 = (f32[2,64,47]{1,0,2:T(2,128)S(1)}, f32[2,64,47]{1,0,2:T(2,128)}, u32[]{:S(2)}) copy-start(f32[2,64,47]{1,0,2:T(2,128)} %param.43) | copy-start | bytes 72196
  69.8 67.7 %copy-start.10 = (f32[2,64]{1,0:T(2,128)S(1)}, f32[2,64]{1,0:T(2,128)}, u32[]{:S(2)}) copy-start(f32[2,64]{1,0:T(2,128)} %refs_5_.3) | copy-start | bytes 1540
  69.8 67.7 %copy-start.12 = (f32[2,64]{1,0:T(2,128)S(1)}, f32[2,64]{1,0:T(2,128)}, u32[]{:S(2)}) copy-start(f32[2,64]{1,0:T(2,128)} %refs_10_.1) | copy-start | bytes 1540
  69.8 67.7 %copy-start.13 = (f32[2,64]{1,0:T(2,128)S(1)}, f32[2,64]{1,0:T(2,128)}, u32[]{:S(2)}) copy-start(f32[2,64]{1,0:T(2,128)} %refs_15_.1) | copy-start | bytes 1540
  69.8 67.7 %copy-start.14 = (f32[47]{0:T(128)S(1)}, f32[47]{0:T(128)}, u32[]{:S(2)}) copy-start(f32[47]{0:T(128)} %param.40) | copy-start | bytes 568
  69.8 67.7 %copy-start.15 = (f32[47]{0:T(128)S(1)}, f32[47]{0:T(128)}, u32[]{:S(2)}) copy-start(f32[47]{0:T(128)} %param.45) | copy-start | bytes 568
  69.8 1.5 %collective-permute-start.6 = (f32[128,256]{1,0:T(8,128)S(1)}, f32[128,256]{1,0:T(8,128)S(1)}, u32[]{:S(2)}, u32[]{:S(2)}) collective-permute-start(f32[128,256]{1,0:T(8,128)S(1)} %sum_mid.1.refs_1_.refs_0_), channel_id=1, source_target_pairs={{0,1},{1,0},{2,3},{3,2},{4,5},{5,4},{6,7},{7,6},{8,9},{9,8},{10,11... | collective-permute-start | bytes 393224 | tf_op jit(solution)/shard_map/ppermute | solution.py:575
  121.8 5.1 %collective-permute-start.7 = (f32[112,128]{1,0:T(8,128)S(1)}, f32[112,128]{1,0:T(8,128)S(1)}, u32[]{:S(2)}, u32[]{:S(2)}) collective-permute-start(f32[112,128]{1,0:T(8,128)S(1)} %sum_grads.1.refs_0_), channel_id=1, source_target_pairs={{0,16},{16,0},{1,17},{17,1},{2,18},{18,2},{3,19},{19,3},{4,20},{20... | collective-permute-start | bytes 172040 | tf_op jit(solution)/shard_map/ppermute | solution.py:669
